TPU v7x, 32 devices: a whole 2x2x4 slice. The times are simulated.
32 devices in a mesh: row: 4 (over y, x), col: 8 (over z, core).
Axes of the slice: x: 2, y: 2, z: 4, core: 2. Of those that a mesh axis runs over, the one named last changes fastest.
Arguments:
- queries: bfloat16 [16384, 768], P(('col', 'row')), may hold values from -11 to 11
- key_vectors: bfloat16 [16384, 768], P(('col', 'row')), may hold values from -11 to 11
- value_vectors: bfloat16 [16384, 768], P(('col', 'row')), may hold values from -6 to 6
- out_grad: bfloat16 [16384, 768], P(('col', 'row')), may hold values from -6 to 6
- near_offsets: int32 [12], replicated, may hold values from 0 to 15, as said below
- far_offsets: int32 [12], replicated, may hold values from 0 to 255, as said below
Outputs:
- attended: bfloat16 [16384, 768], P(('col', 'row'))
- query_grad: bfloat16 [16384, 768], P(('col', 'row'))
- key_grad: bfloat16 [16384, 768], P(('col', 'row'))
- value_grad: bfloat16 [16384, 768], P(('col', 'row'))
Inputs may be any that keep to these rules, and one draw needn't show every extreme that they name: `near_offsets`: some head has offset 0 and some head offset 16 - 1. `far_offsets`: some head has offset 0 and some head offset 256 - 1.
All inputs are finite; a program needn't handle non-finite values.
Results may differ from a plain program's by a relative error of at most 0.022.
Values may be sent and summed in bfloat16 or wider, within the bound.
No kernel may reach another device: no remote copies, remote signals or barrier semaphores. Data moves between devices by JAX's collectives and lax.ppermute only.
A program may use at most 128 MiB of HBM per device.

v0:
```python
import jax
import jax.numpy as jnp
from jax import lax
from jax.sharding import PartitionSpec as P

H = 12
HD = 64
R2 = 16
R3 = 256
S1 = 512
SEG2 = 2048


NEG = -1e30


def attend(queries, keys_block, values_block, allowed):
    scale = queries.shape[-1] ** (-0.5)
    scores = (
        jnp.einsum("...qd,...kd->...qk", queries, keys_block, preferred_element_type=jnp.float32)
        * scale
    )
    scores = jnp.where(allowed, scores, NEG)
    highest = jnp.max(scores, axis=-1)
    weights = jnp.exp(scores - highest[..., None])
    total = jnp.sum(weights, axis=-1)
    mixed = jnp.einsum(
        "...qk,...kd->...qd",
        weights.astype(jnp.bfloat16),
        values_block,
        preferred_element_type=jnp.float32,
    )
    return (highest, total, mixed)


def backward_block(queries, keys_block, values_block, grad_out, log_total, row_dot, allowed):
    scale = queries.shape[-1] ** (-0.5)
    scores = (
        jnp.einsum("...qd,...kd->...qk", queries, keys_block, preferred_element_type=jnp.float32)
        * scale
    )
    scores = jnp.where(allowed, scores, NEG)
    probs = jnp.exp(scores - log_total[..., None])
    grad_prob = jnp.einsum(
        "...qd,...kd->...qk", grad_out, values_block, preferred_element_type=jnp.float32
    )
    grad_score = probs * (grad_prob - row_dot[..., None])
    score_half = grad_score.astype(jnp.bfloat16)
    prob_half = probs.astype(jnp.bfloat16)
    grad_query = scale * jnp.einsum(
        "...qk,...kd->...qd", score_half, keys_block, preferred_element_type=jnp.float32
    )
    grad_key = scale * jnp.einsum(
        "...qk,...qd->...kd", score_half, queries, preferred_element_type=jnp.float32
    )
    grad_value = jnp.einsum(
        "...qk,...qd->...kd", prob_half, grad_out, preferred_element_type=jnp.float32
    )
    return (grad_query, grad_key, grad_value)


def pick(source, offsets, dilation):
    head_count, length = (source.shape[0], source.shape[1])
    trailing = source.shape[2:]
    shaped = source.reshape((head_count, length // dilation, dilation) + trailing)
    lanes = lax.broadcasted_iota(jnp.int32, (1, 1, dilation) + (1,) * len(trailing), 2)
    chosen = lanes == offsets.reshape((head_count, 1, 1) + (1,) * len(trailing))
    zeros = jnp.zeros((), source.dtype)
    return jnp.sum(jnp.where(chosen, shaped, zeros), axis=2, dtype=source.dtype)


def spread(values, offsets, dilation, filler):
    head_count, rows = (values.shape[0], values.shape[1])
    trailing = values.shape[2:]
    lanes = lax.broadcasted_iota(jnp.int32, (1, 1, dilation) + (1,) * len(trailing), 2)
    chosen = lanes == offsets.reshape((head_count, 1, 1) + (1,) * len(trailing))
    placed = jnp.where(chosen, values[:, :, None], filler)
    return placed.reshape((head_count, rows * dilation) + trailing)


def far_order(count, block, row_count, col_count):
    slots = lax.iota(jnp.int32, count)
    group = slots // block
    return (group % col_count * row_count + group // col_count) * block + slots % block


def near_mask(query_places, key_places):
    seg_near = SEG2 // R2
    return (key_places <= query_places) & (key_places // seg_near == query_places // seg_near)


def shards(queries, key_vectors, value_vectors, out_grad, near_offsets, far_offsets):
    length = queries.shape[0]
    row_count = lax.axis_size("row")
    col_count = lax.axis_size("col")
    row_here = lax.axis_index("row")
    seq_here = lax.axis_index("col") * row_count + row_here

    def heads_first(source):
        return jnp.moveaxis(source.reshape(length, H, HD), 1, 0)

    def tokens_first(source):
        return jnp.moveaxis(source, 0, 1).reshape(length, H * HD)

    query_h = heads_first(queries)
    key_h = heads_first(key_vectors)
    value_h = heads_first(value_vectors)
    grad_h = heads_first(out_grad)
    seg_count = length // S1

    def segments(source):
        return source.reshape((H, seg_count, S1) + source.shape[2:])

    def joined(source):
        return source.reshape((H, length) + source.shape[3:])

    causal_one = lax.broadcasted_iota(jnp.int32, (S1, S1), 1) <= lax.broadcasted_iota(
        jnp.int32, (S1, S1), 0
    )
    near_query = pick(query_h, near_offsets, R2)
    near_key = pick(key_h, near_offsets, R2)
    near_value = pick(value_h, near_offsets, R2)
    far_query = pick(query_h, far_offsets, R3)
    far_key = pick(key_h, far_offsets, R3)
    far_value = pick(value_h, far_offsets, R3)
    near_rows = near_query.shape[1]
    far_rows = far_query.shape[1]
    near_keys_all, near_values_all = (
        lax.all_gather(near_key, "row", axis=1, tiled=True),
        lax.all_gather(near_value, "row", axis=1, tiled=True),
    )
    far_keys_all, far_values_all = (
        lax.all_gather(far_key, ("row", "col"), axis=1, tiled=True),
        lax.all_gather(far_value, ("row", "col"), axis=1, tiled=True),
    )
    first = lax.map(
        lambda parts: attend(parts[0], parts[1], parts[2], causal_one),
        (segments(query_h), segments(key_h), segments(value_h)),
    )
    near_width = near_keys_all.shape[1]
    own_near = row_here * near_rows + lax.iota(jnp.int32, near_rows)
    near_allowed = near_mask(own_near[:, None], lax.iota(jnp.int32, near_width)[None, :])
    second = attend(near_query, near_keys_all, near_values_all, near_allowed)
    far_width = far_keys_all.shape[1]
    far_allowed = (
        far_order(far_width, far_rows, row_count, col_count)[None, :]
        <= (seq_here * far_rows + lax.iota(jnp.int32, far_rows))[:, None]
    )
    third = attend(far_query, far_keys_all, far_values_all, far_allowed)
    high_one, total_one, mixed_one = (joined(first[0]), joined(first[1]), joined(first[2]))
    high_two = spread(second[0], near_offsets, R2, NEG)
    total_two = spread(second[1], near_offsets, R2, 0.0)
    mixed_two = spread(second[2], near_offsets, R2, 0.0)
    high_three = spread(third[0], far_offsets, R3, NEG)
    total_three = spread(third[1], far_offsets, R3, 0.0)
    mixed_three = spread(third[2], far_offsets, R3, 0.0)
    top = jnp.maximum(jnp.maximum(high_one, high_two), high_three)
    weight_one = jnp.exp(high_one - top)
    weight_two = jnp.exp(high_two - top)
    weight_three = jnp.exp(high_three - top)
    total = weight_one * total_one + weight_two * total_two + weight_three * total_three
    mixed = (
        weight_one[..., None] * mixed_one
        + weight_two[..., None] * mixed_two
        + weight_three[..., None] * mixed_three
    )
    attended_h = (mixed / total[..., None]).astype(jnp.bfloat16)
    log_total = top + jnp.log(total)
    row_dot = jnp.sum(grad_h.astype(jnp.float32) * attended_h.astype(jnp.float32), axis=-1)
    first_grads = lax.map(
        lambda parts: backward_block(
            parts[0], parts[1], parts[2], parts[3], parts[4], parts[5], causal_one
        ),
        (
            segments(query_h),
            segments(key_h),
            segments(value_h),
            segments(grad_h),
            segments(log_total),
            segments(row_dot),
        ),
    )
    near_grad_out = pick(grad_h, near_offsets, R2)
    near_logs = pick(log_total, near_offsets, R2)
    near_dots = pick(row_dot, near_offsets, R2)
    far_grad_out = pick(grad_h, far_offsets, R3)
    far_logs = pick(log_total, far_offsets, R3)
    far_dots = pick(row_dot, far_offsets, R3)
    near_qgrad, near_kpart, near_vpart = backward_block(
        near_query,
        near_keys_all,
        near_values_all,
        near_grad_out,
        near_logs,
        near_dots,
        near_allowed,
    )
    far_qgrad, far_kpart, far_vpart = backward_block(
        far_query, far_keys_all, far_values_all, far_grad_out, far_logs, far_dots, far_allowed
    )
    near_kgrad, near_vgrad = (
        lax.psum_scatter(
            near_kpart.astype(jnp.bfloat16), "row", scatter_dimension=1, tiled=True
        ).astype(jnp.float32),
        lax.psum_scatter(
            near_vpart.astype(jnp.bfloat16), "row", scatter_dimension=1, tiled=True
        ).astype(jnp.float32),
    )
    far_kgrad, far_vgrad = (
        lax.psum_scatter(far_kpart, ("row", "col"), scatter_dimension=1, tiled=True),
        lax.psum_scatter(far_vpart, ("row", "col"), scatter_dimension=1, tiled=True),
    )
    query_sum = (
        joined(first_grads[0])
        + spread(near_qgrad, near_offsets, R2, 0.0)
        + spread(far_qgrad, far_offsets, R3, 0.0)
    )
    key_sum = (
        joined(first_grads[1])
        + spread(near_kgrad, near_offsets, R2, 0.0)
        + spread(far_kgrad, far_offsets, R3, 0.0)
    )
    value_sum = (
        joined(first_grads[2])
        + spread(near_vgrad, near_offsets, R2, 0.0)
        + spread(far_vgrad, far_offsets, R3, 0.0)
    )
    return (
        tokens_first(attended_h),
        tokens_first(query_sum.astype(jnp.bfloat16)),
        tokens_first(key_sum.astype(jnp.bfloat16)),
        tokens_first(value_sum.astype(jnp.bfloat16)),
    )


def solution(mesh):
    placed = (
        P(("col", "row"), None),
        P(("col", "row"), None),
        P(("col", "row"), None),
        P(("col", "row"), None),
        P(),
        P(),
    )
    return jax.shard_map(
        shards,
        mesh=mesh,
        in_specs=placed,
        out_specs=(
            P(("col", "row"), None),
            P(("col", "row"), None),
            P(("col", "row"), None),
            P(("col", "row"), None),
        ),
        check_vma=False,
    )
```

profile of v0, /device:TPU:0, one launch (start us, length us, event | category | flops | bytes accessed | tf_op | source)
XLA Modules:
  0.0 383.0 jit_solution(12207137426741572875)
XLA Ops:
  24.0 32.7 %while.30 = (s32[]{:T(128)}, f32[12,1,512]{2,1,0:T(1,128)S(1)}, f32[12,1,512]{2,1,0:T(1,128)S(1)}, f32[12,1,512,64]{2,3,1,0:T(8,128)S(1)}, bf16[12,1,512,64]{3,2...) while((s32[]{:T(128)}, f32[12,1,512]{2,1,0:T(1,128)S(1)}, ...), condition=%wide.region_3.4_spmd.clone, body=%wide.region_0.3_spmd.clone.sunk | while | flops 69204992 | bytes 3688545 | solution.py:136
  65.7 1.9 copy.119
  67.6 5.4 %fusion.73 = (bf16[12,2,64]{1,2,0:T(8,128)(2,1)}, bf16[12,2,64]{1,2,0:T(8,128)(2,1)}, bf16[12,2,64]{1,2,0:T(8,128)(2,1)S(1)}, bf16[12,2,64]{1,2,0:T(8,128)(2,1)S(1)}) fusion(bf16[12,2,256,64]{2,1,3,0:T(2,128)(2,1)} %copy.119, pred[12,256]{1,0:T(8,128)(4,1)S(1)} %iota_compare_fusion.2, bf16[12,2,256,64]{2,1,3,0:T(2,128)(2,1)S(1)} %copy-done.8, ...), kind=kLoop, calls=%fused_computation.111 | loop fusion | flops 3139584 | bytes 3161088 | tf_op jit(solution)/shard_map/reduce_sum | solution.py:69
  74.4 44.3 %all_gather.15 = bf16[12,64,64]{2,0,1:T(8,128)(2,1)S(1)} all-gather(bf16[12,2,64]{2,0,1:T(8,128)(2,1)S(1)} %copy.105), channel_id=1, replica_groups=mesh['row'=4,'col'=8] {'row','col'}, dimensions={1}, use_global_device_ids=true | all-gather | bytes 101376 | tf_op jit(solution)/shard_map/all_gather | solution.py:134
  118.7 37.9 %all_gather.13 = bf16[12,64,64]{2,0,1:T(8,128)(2,1)S(1)} all-gather(bf16[12,2,64]{2,0,1:T(8,128)(2,1)S(1)} %copy.100), channel_id=1, replica_groups=mesh['row'=4,'col'=8] {'row','col'}, dimensions={1}, use_global_device_ids=true | all-gather | bytes 101376 | tf_op jit(solution)/shard_map/all_gather | solution.py:133
  160.1 5.7 %select_reduce_fusion = (bf16[12,32,64]{2,1,0:T(8,128)(2,1)}, bf16[12,32,64]{2,1,0:T(8,128)(2,1)S(1)}, bf16[12,32,64]{2,1,0:T(8,128)(2,1)}, bf16[12,32,64]{2,1,0:T(8,128)(2,1)S(1)}) fusion(pred[12,16]{1,0:T(8,128)(4,1)} %copy-done.32, bf16[512,12,64]{2,0,1:T(8,128)(2,1)S(1)} %copy.112, bf16[12,512,64]{2,1,0:T(8,128)(2,1)} %copy.99, ...), kind=kLoop, calls=%fused_computation.84 | loop fusion | flops 3047424 | bytes 3342528 | tf_op jit(solution)/shard_map/reduce_sum | solution.py:69
  165.8 8.5 %all_gather.12 = bf16[12,128,64]{2,1,0:T(8,128)(2,1)S(1)} all-gather(bf16[12,32,64]{2,1,0:T(8,128)(2,1)S(1)} %get-tuple-element.233), channel_id=1, replica_groups=mesh['row'=4,'col'=8] {'row'}, dimensions={1}, use_global_device_ids=true | all-gather | bytes 245760 | tf_op jit(solution)/shard_map/all_gather | solution.py:129
  181.2 10.0 %all_gather.14 = bf16[12,128,64]{2,1,0:T(8,128)(2,1)S(1)} all-gather(bf16[12,32,64]{2,1,0:T(8,128)(2,1)} %get-tuple-element.234), channel_id=1, replica_groups=mesh['row'=4,'col'=8] {'row'}, dimensions={1}, use_global_device_ids=true | all-gather | bytes 245760 | tf_op jit(solution)/shard_map/all_gather | solution.py:130
  192.9 2.3 copy.103
  196.2 10.7 %multiply_reduce_fusion = (f32[12,512]{1,0:T(8,128)}, bf16[12,512,64]{2,1,0:T(8,128)(2,1)S(1)}) fusion(bf16[512,12,64]{2,0,1:T(8,128)(2,1)S(1)} %copy.112, f32[12,512]{1,0:T(8,128)S(1)} %get-tuple-element.274, f32[12,2,64]{2,1,0:T(2,128)} %fusion.85, pred[12,512]{1,0:T(8,128)(4,1)} %bitcast.293, f32[12,512]{1,0:T(8,128)S(1)} %get-tuple-element.276, ...), kind=kLoop, calls=%fused_computation.82 | loop fusion | flops 5105664 | bytes 3385344 | tf_op jit(solution)/shard_map/reduce_sum | solution.py:169
  214.6 2.8 fusion.80
  222.3 2.1 fusion.114
  227.4 2.2 convolution_convert_fusion
  231.9 2.0 fusion.63
  235.4 2.0 convolution_multiply_fusion.6
  239.6 2.3 copy.130
  245.1 85.3 %while.31 = (s32[]{:T(128)}, f32[12,1,512,64]{2,3,1,0:T(8,128)}, f32[12,1,512,64]{2,3,1,0:T(8,128)}, f32[12,1,512,64]{2,3,1,0:T(8,128)S(1)}, bf16[12,1,512,64]{3...) while((s32[]{:T(128)}, f32[12,1,512,64]{2,3,1,0:T(8,128)}, ...), condition=%wide.region_16.17_spmd.clone, body=%wide.region_15.16_spmd.clone.sunk | while | flops 169934848 | bytes 6046845 | solution.py:170
  250.4 1.9 fusion.182
  331.6 2.1 copy.127
  333.7 3.3 copy.118
  337.0 3.3 copy.124
  340.4 14.8 %all-reduce.5.cloned.1.call-done = (f32[12,64,64]{2,1,0:T(8,128)}, f32[12,64,64]{2,1,0:T(8,128)}) async-done(((f32[12,64,64]{2,1,0:T(8,128)}, f32[12,64,64]{2,1,0:T(8,128)}), (f32[12,64,64]{2,1,0:T(8,128)}, f32[12,64,64]{2,1,0:T(8,128)})) %all-reduce.5.cloned.1.call-update) | async-done | bytes 393232
  358.8 8.3 %fusion.49 = (bf16[12,512,64]{2,1,0:T(8,128)(2,1)}, bf16[12,512,64]{2,1,0:T(8,128)(2,1)}, bf16[12,512,64]{2,1,0:T(8,128)(2,1)}) fusion(f32[12,1,512,64]{3,2,0,1:T(8,128)S(1)} %copy.127, f32[12,2,64]{2,1,0:T(2,128)S(1)} %constant_dynamic-slice_fusion.2, f32[12,32,64]{2,1,0:T(8,128)S(1)} %convert_element_type.73, pred[12,512]{1,0:T(8,128)(4,1)S(1)} %bitcast.294, ...), kind=kLoop, calls=%fused_computation.61 | loop fusion | flops 5898240 | bytes 7403520 | tf_op jit(solution)/shard_map/convert_element_type | solution.py:232
  371.4 2.3 copy.132
  (307 shorter events, 190.5 us)
Async XLA Ops:
  8.0 347.3 %all-reduce.5.cloned.1.call-start = ((), (), s32[]{:S(2)}) async-start(), calls=%async_computation.4 | async-start | bytes 1572864
  24.0 37.0 %copy-start.35 = (s32[12]{0:T(128)S(1)}, s32[12]{0:T(128)}, u32[]{:S(2)}) copy-start(s32[12]{0:T(128)} %param.14) | copy-start | bytes 148
  24.0 37.1 %copy-start.36 = (s32[12]{0:T(128)S(1)}, s32[12]{0:T(128)}, u32[]{:S(2)}) copy-start(s32[12]{0:T(128)} %param.15) | copy-start | bytes 148
  56.8 8.0 %copy-start.4 = (f32[12,1,512,64]{2,3,1,0:T(8,128)}, f32[12,1,512,64]{2,3,1,0:T(8,128)S(1)}, u32[]{:S(2)}) copy-start(f32[12,1,512,64]{2,3,1,0:T(8,128)S(1)} %get-tuple-element.108) | copy-start | bytes 4718596
  56.8 8.8 %copy-start.17 = (f32[12,1,512]{2,1,0:T(1,128)}, f32[12,1,512]{2,1,0:T(1,128)S(1)}, u32[]{:S(2)}) copy-start(f32[12,1,512]{2,1,0:T(1,128)S(1)} %get-tuple-element.109) | copy-start | bytes 73732
  56.8 8.8 %copy-start.19 = (f32[12,1,512]{2,1,0:T(1,128)}, f32[12,1,512]{2,1,0:T(1,128)S(1)}, u32[]{:S(2)}) copy-start(f32[12,1,512]{2,1,0:T(1,128)S(1)} %get-tuple-element.107) | copy-start | bytes 73732
  61.1 4.5 %copy-start.32 = (pred[12,16]{1,0:T(8,128)(4,1)}, pred[12,16]{1,0:T(8,128)(4,1)S(1)}, u32[]{:S(2)}) copy-start(pred[12,16]{1,0:T(8,128)(4,1)S(1)} %iota_compare_fusion.4) | copy-start | bytes 580
  61.2 6.4 %copy-start.30 = (pred[12,256]{1,0:T(8,128)(4,1)}, pred[12,256]{1,0:T(8,128)(4,1)S(1)}, u32[]{:S(2)}) copy-start(pred[12,256]{1,0:T(8,128)(4,1)S(1)} %iota_compare_fusion.2) | copy-start | bytes 9220
  73.0 87.1 %copy-start.2 = (bf16[12,512,64]{2,1,0:T(8,128)(2,1)S(1)}, bf16[12,512,64]{2,1,0:T(8,128)(2,1)}, u32[]{:S(2)}) copy-start(bf16[12,512,64]{2,1,0:T(8,128)(2,1)} %copy.104) | copy-start | bytes 2359300
  118.7 40.8 %copy-start.16 = (bf16[12,64,64]{2,0,1:T(8,128)(2,1)}, bf16[12,64,64]{2,0,1:T(8,128)(2,1)S(1)}, u32[]{:S(2)}) copy-start(bf16[12,64,64]{2,0,1:T(8,128)(2,1)S(1)} %all_gather.15) | copy-start | bytes 294916
  157.8 8.0 %copy-start.23 = (f32[12,2]{1,0:T(8,128)}, f32[12,2]{1,0:T(8,128)S(1)}, u32[]{:S(2)}) copy-start(f32[12,2]{1,0:T(8,128)S(1)} %fusion.111) | copy-start | bytes 292
  160.1 14.2 %copy-start.37 = (s32[128]{0:T(128)S(1)}, s32[128]{0:T(128)}, u32[]{:S(2)}) copy-start(s32[128]{0:T(128)} %and_select_fusion.5) | copy-start | bytes 1540
  160.1 14.2 %copy-start.38 = (s32[32]{0:T(128)S(1)}, s32[32]{0:T(128)}, u32[]{:S(2)}) copy-start(s32[32]{0:T(128)} %get-tuple-element.293) | copy-start | bytes 388
  160.1 14.3 %copy-start.39 = (s32[32]{0:T(128)S(1)}, s32[32]{0:T(128)}, u32[]{:S(2)}) copy-start(s32[32]{0:T(128)} %get-tuple-element.294) | copy-start | bytes 388
  165.8 9.7 %copy-start.12 = (bf16[12,32,64]{2,1,0:T(8,128)(2,1)}, bf16[12,32,64]{2,1,0:T(8,128)(2,1)S(1)}, u32[]{:S(2)}) copy-start(bf16[12,32,64]{2,1,0:T(8,128)(2,1)S(1)} %get-tuple-element.235) | copy-start | bytes 147460
  174.3 18.6 %copy-start.5 = (f32[12,1,512,64]{2,3,1,0:T(8,128)S(1)}, f32[12,1,512,64]{2,3,1,0:T(8,128)}, u32[]{:S(2)}) copy-start(f32[12,1,512,64]{2,3,1,0:T(8,128)} %copy-done.4) | copy-start | bytes 4718596
  217.4 10.0 %copy-start.28 = (f32[12,32]{1,0:T(8,128)S(1)}, f32[12,32]{1,0:T(8,128)}, u32[]{:S(2)}) copy-start(f32[12,32]{1,0:T(8,128)} %get-tuple-element.230) | copy-start | bytes 4612
  224.4 5.5 %copy-start.31 = (f32[12,32]{1,0:T(8,128)S(1)}, f32[12,32]{1,0:T(8,128)}, u32[]{:S(2)}) copy-start(f32[12,32]{1,0:T(8,128)} %get-tuple-element.231) | copy-start | bytes 4612
  227.4 129.6 %reduce-scatter.7.cloned.1.call-start = ((), (), s32[]{:S(2)}) async-start(), calls=%async_computation.3 | async-start | bytes 491520 | tf_op jit(solution)/shard_map/reduce_scatter | solution.py:205
  229.6 8.5 %copy-start.9 = (f32[12,32,16]{2,1,0:T(8,128)S(1)}, f32[12,32,16]{2,1,0:T(8,128)}, u32[]{:S(2)}) copy-start(f32[12,32,16]{2,1,0:T(8,128)} %get-tuple-element.288) | copy-start | bytes 73732
  229.6 128.2 %reduce-scatter.5.cloned.1.call-start = ((), (), s32[]{:S(2)}) async-start(), calls=%async_computation.2 | async-start | bytes 491520 | tf_op jit(solution)/shard_map/reduce_scatter | solution.py:202
  231.9 5.4 %copy-start.10 = (f32[12,32,16]{2,1,0:T(8,128)S(1)}, f32[12,32,16]{2,1,0:T(8,128)}, u32[]{:S(2)}) copy-start(f32[12,32,16]{2,1,0:T(8,128)} %get-tuple-element.287) | copy-start | bytes 73732
  337.0 21.8 %copy-start.21 = (pred[2,8,2,256]{3,1,2,0:T(8,128)(4,1)S(1)}, pred[2,8,2,256]{3,1,2,0:T(8,128)(4,1)}, u32[]{:S(2)}) copy-start(pred[2,8,2,256]{3,1,2,0:T(8,128)(4,1)} %copy.145) | copy-start | bytes 24580
  337.0 21.8 %copy-start.22 = (pred[12,512]{1,0:T(8,128)(4,1)S(1)}, pred[12,512]{1,0:T(8,128)(4,1)}, u32[]{:S(2)}) copy-start(pred[12,512]{1,0:T(8,128)(4,1)} %broadcast_in_dim.348) | copy-start | bytes 18436
  (19 other events, 44.2 us)
Sparse Core Ops, SparseCore 0:
  227.5 127.7 all-reduce.4
Sparse Core Ops, SparseCore 1:
  230.8 22.7 reduce-scatter.6
  256.5 24.4 reduce-scatter.4
where the time goes:
time: 386 us; the launch traced here: 383 us
  matrix products  122 us (32%)
  blocking collectives  101 us (26%)
  local copies, waits for them, and re-layouts  85.7 us (22%)
  other arithmetic  43.3 us (11%)
  between operations  16 us (4%)
  waiting for transfers between devices  14.9 us (4%)
    all_gather x1, blocking collectives, shards(): lax.all_gather(far_value, ('row', 'col'), axis=1, tiled=True)  44.3 us
    all_gather x1, blocking collectives, shards(): lax.all_gather(far_key, ('row', 'col'), axis=1, tiled=True)  37.9 us
    dot_general x14, matrix products, backward_block(): jnp.einsum('...qk,...qd->...kd', score_half, queries, preferred_element_t...  24.8 us
    dot_general x14, matrix products, backward_block(): jnp.einsum('...qk,...kd->...qd', score_half, keys_block, preferred_elemen...  24.2 us
    unnamed x99, local copies, waits for them, and re-layouts  24 us
    dot_general x14, matrix products, backward_block(): jnp.einsum('...qd,...kd->...qk', grad_out, values_block, preferred_elemen...  17.3 us
    dot_general x14, matrix products, attend(): jnp.einsum('...qd,...kd->...qk', queries, keys_block, preferred_element_t...  16.4 us
    dot_general x14, matrix products, attend(): jnp.einsum('...qk,...kd->...qd', weights.astype(jnp.bfloat16), values_blo...  16.2 us
  transfers between devices with their start and end apart: 3, of which 1 were waited for; matrix products, arithmetic and copies ran while one was open for 29% of the time, Pallas kernels for 0%

commit v1 on v0

v1 whole, which is shorter than its diff:
```python
import functools

import jax
import jax.numpy as jnp
from jax import lax
from jax.experimental import pallas as pl
from jax.experimental.pallas import tpu as pltpu
from jax.sharding import PartitionSpec as P

H = 12
HD = 64
R2 = 16
R3 = 256
S1 = 512
SEG2 = 2048

NEG = -1e30
SCALE = HD**-0.5
GH = 4
GW = GH * HD
PW = 2 * HD
FM = 16
F32 = jnp.float32
BF = jnp.bfloat16
VMEM_LIMIT = 48 * 1024 * 1024


def iota(shape, axis):
    return lax.broadcasted_iota(jnp.int32, shape, axis)


def nn(a, b):
    return lax.dot_general(a, b, (((1,), (0,)), ((), ())), preferred_element_type=F32)


def nt(a, b):
    return lax.dot_general(a, b, (((1,), (1,)), ((), ())), preferred_element_type=F32)


def tn(a, b):
    return lax.dot_general(a, b, (((0,), (0,)), ((), ())), preferred_element_type=F32)


def onehot(cond):
    return jnp.where(cond, 1.0, 0.0).astype(BF)


def lane_offsets(ref, group):
    head = iota((1, GW), 1) // HD
    out = jnp.zeros((1, GW), jnp.int32)
    for h in range(GH):
        out = jnp.where(head == h, ref[group * GH + h], out)
    return out


def expand(x):
    head = iota((1, GW), 1) // HD
    return jnp.concatenate([x * onehot(head == h) for h in range(GH)], axis=0)


def collapse(x):
    n = x.shape[0] // GH
    head = iota((1, GW), 1) // HD
    out = x[:n]
    for h in range(1, GH):
        out = jnp.where(head == h, x[h * n : (h + 1) * n], out)
    return out


def split3(x):
    hi = x.astype(BF)
    rest = x - hi.astype(F32)
    mid = rest.astype(BF)
    low = (rest - mid.astype(F32)).astype(BF)
    return hi.astype(F32), mid.astype(F32), low.astype(F32)


def pack_aux(log_total, row_dot):
    lane = iota((1, log_total.shape[1]), 1) % HD
    out = jnp.zeros(log_total.shape, F32)
    for at, piece in enumerate(split3(log_total) + split3(row_dot)):
        out = jnp.where(lane == at, piece, out)
    return out


def piece_rows(rows, width, which):
    head = iota((rows, width), 1) // HD
    lane = iota((rows, width), 1) % HD // 3
    return head, lane == which


def spread_sum(x, width):
    block = onehot(iota((width, width), 0) // HD == iota((width, width), 1) // HD)
    hi = x.astype(BF)
    low = (x - hi.astype(F32)).astype(BF)
    return nn(hi, block) + nn(low, block)


def piece_spread(aux, which):
    a = iota((GW, GW), 0)
    sel = onehot((a // HD == iota((GW, GW), 1) // HD) & (a % HD // 3 == which))
    return nn(aux, sel)


def piece_column(aux_expanded, which):
    a = iota((GW, 128), 0)
    return nn(aux_expanded, onehot(a % HD // 3 == which))[:, :1]


def near_select(n, length):
    return onehot(iota((n, length), 1) // R2 == iota((n, length), 0))


def near_place(n, length):
    return onehot(iota((length, n), 0) // R2 == iota((length, n), 1))


def far_select(rows, length, first):
    return onehot(iota((rows, length), 1) // R3 == iota((rows, length), 0) - first)


def far_place(length):
    return onehot(iota((length, FM), 0) // R3 == iota((length, FM), 1))


def token_masks(near_ref, far_ref, group, length):
    t = iota((length, GW), 0)
    near = t % R2 == lane_offsets(near_ref, group)
    far = t % R3 == lane_offsets(far_ref, group)
    return near, far


def pick_kernel(peers, near_ref, far_ref, q_ref, k_ref, v_ref, g_ref, kv_ref, qg_ref, fr_ref, *msg_refs):
    group = pl.program_id(0)
    length = q_ref.shape[0]
    n, f = length // R2, length // R3
    near, far = token_masks(near_ref, far_ref, group, length)
    near, far = onehot(near), onehot(far)
    sel = near_select(n, length)
    q, k, v, g = q_ref[...], k_ref[...], v_ref[...], g_ref[...]
    picked = [nn(sel, x * near).astype(BF) for x in (k, v, q, g)]
    kv = jnp.concatenate(picked[:2], axis=0)
    qg = jnp.concatenate(picked[2:], axis=0)
    kv_ref[...] = kv
    qg_ref[...] = qg
    fr = jnp.zeros((FM, GW), F32)
    for at, x in enumerate((q, k, v, g)):
        fr += nn(far_select(FM, length, at * f), x * far)
    fr_ref[...] = fr.astype(BF)
    own = lax.axis_index("row") % peers
    for slot in range(1, peers):
        later = (own ^ slot) > own

        @pl.when(later)
        def _(slot=slot):
            msg_refs[slot - 1][...] = kv

        @pl.when(jnp.logical_not(later))
        def _(slot=slot):
            msg_refs[slot - 1][...] = qg


def forward_kernel(strip, q_ref, k_ref, v_ref, g_ref, att_ref, aux_ref):
    length = q_ref.shape[0]
    lane = iota((1, PW), 1)
    first = lane < HD
    in_head = (onehot(first), onehot(jnp.logical_not(first)))
    k = k_ref[...]
    v = v_ref[...]
    with_ones = [v * in_head[h] + in_head[1 - h] for h in range(2)]
    diag = iota((strip, strip), 1) <= iota((strip, strip), 0)
    for r in range(length // strip):
        rows = slice(r * strip, (r + 1) * strip)
        width = (r + 1) * strip
        q = q_ref[rows, :] * jnp.asarray(SCALE, BF)
        tops, outs = [], []
        for h in range(2):
            s = nt(q * in_head[h], k[:width])
            last = jnp.where(diag, s[:, r * strip :], NEG)
            s = jnp.concatenate([s[:, : r * strip], last], axis=1) if r else last
            top = jnp.max(s, axis=1, keepdims=True)
            w = jnp.exp(s - top).astype(BF)
            tops.append(top)
            outs.append(nn(w, with_ones[h][:width]))
        total = pltpu.roll(jnp.where(first, outs[1], outs[0]), HD, 1)
        att = jnp.where(first, outs[0], outs[1]) / total
        log_total = jnp.where(first, tops[0], tops[1]) + jnp.log(total)
        row_dot = spread_sum(g_ref[rows, :].astype(F32) * att, PW)
        att_ref[rows, :] = att.astype(BF)
        aux_ref[rows, :] = pack_aux(log_total, row_dot).astype(BF)


def near_valid_queries(shape, n, own):
    row, lane = iota(shape, 0) % n, iota(shape, 1)
    slot, key = lane // n, lane % n
    return ((slot ^ own) < own) | ((slot == 0) & (key <= row))


def near_valid_keys(shape, n, own):
    row, lane = iota(shape, 0) % n, iota(shape, 1)
    slot, query = lane // n, lane % n
    return ((slot ^ own) > own) | ((slot == 0) & (row <= query))


def merge_kernel(peers, near_ref, far_ref, kv_ref, qg_ref, *rest):
    got, (aux_ref, att_ref, fr_ref, out_ref, aux_out_ref, att_out_ref) = rest[: peers - 1], rest[peers - 1 :]
    group = pl.program_id(0)
    length = aux_ref.shape[0]
    n, f = length // R2, length // R3
    own = lax.axis_index("row") % peers
    near, far = token_masks(near_ref, far_ref, group, length)
    keys = jnp.concatenate([r[:n, :] for r in (kv_ref, *got)], axis=0)
    values = jnp.concatenate([r[n:, :] for r in (kv_ref, *got)], axis=0)
    queries = expand(qg_ref[:n, :] * jnp.asarray(SCALE, BF))
    s = nt(queries, keys)
    s = jnp.where(near_valid_queries(s.shape, n, own), s, NEG)
    top = jnp.max(s, axis=1, keepdims=True)
    w = jnp.exp(s - top)
    total = jnp.sum(w, axis=1, keepdims=True)
    out2 = collapse(nn(w.astype(BF), values) / total)
    log2 = collapse(jnp.broadcast_to(top + jnp.log(total), (GH * n, GW)))

    sel = near_select(n, length)
    nearh = onehot(near)
    aux = aux_ref[...]
    att = att_ref[...]
    log1 = piece_spread(nn(sel, aux * nearh).astype(BF), 0)
    out1 = nn(sel, att * nearh)
    top = jnp.maximum(log1, log2)
    e1, e2 = jnp.exp(log1 - top), jnp.exp(log2 - top)
    both = e1 + e2
    log12 = top + jnp.log(both)
    out12 = (e1 * out1 + e2 * out2) / both
    dot12 = spread_sum(qg_ref[n:, :].astype(F32) * out12, GW)
    aux12 = pack_aux(log12, dot12).astype(BF)
    place = near_place(n, length)
    att_out_ref[...] = jnp.where(near, nn(place, out12.astype(BF)), att.astype(F32)).astype(BF)
    aux_all = jnp.where(near, nn(place, aux12), aux.astype(F32))
    far_aux = nn(far_select(FM, length, 4 * f), aux_all.astype(BF) * onehot(far))
    out_ref[:n, :] = aux12
    out_ref[n:, :] = (fr_ref[...].astype(F32) + far_aux).astype(BF)
    lane = iota((1, GW), 1) % HD
    aux_out_ref[...] = jnp.where(far, jnp.where(lane == 0, -NEG, 0.0), aux_all).astype(BF)


def backward_kernel(strip, aliased, q_ref, k_ref, v_ref, g_ref, aux_ref, *rest):
    dq_ref, dk_ref, dv_ref = rest[aliased:]
    length = q_ref.shape[0]
    first = iota((1, PW), 1) < HD
    in_head = (onehot(first), onehot(jnp.logical_not(first)))
    q = q_ref[...] * jnp.asarray(SCALE, BF)
    g = g_ref[...]
    k = k_ref[...]
    v = v_ref[...]
    row, lane = iota((8, PW), 0), iota((8, PW), 1)
    pieces = onehot((lane // HD == row % 2) & (lane % HD // 3 == row // 2) & (row < 4))
    stats = nt(pieces, aux_ref[...])
    eye = onehot(iota((PW, PW), 0) == iota((PW, PW), 1))
    k_t = (nt(eye, k) * SCALE).astype(BF)
    diag = iota((strip, strip), 0) <= iota((strip, strip), 1)
    dq_t = [[jnp.zeros((HD, strip), F32) for _ in range(length // strip)] for _ in range(2)]
    for c in range(length // strip):
        rows = slice(c * strip, (c + 1) * strip)
        dks, dvs = [], []
        for h in range(2):
            s = nt(k[rows] * in_head[h], q[c * strip :])
            p = jnp.exp(s - stats[h : h + 1, c * strip :])
            head = jnp.where(diag, p[:, :strip], 0.0)
            p = jnp.concatenate([head, p[:, strip:]], axis=1) if p.shape[1] > strip else head
            dp = nt(v[rows] * in_head[h], g[c * strip :])
            ds = (p * (dp - stats[2 + h : 3 + h, c * strip :])).astype(BF)
            dvs.append(nn(p.astype(BF), g[c * strip :]))
            dks.append(nn(ds, q[c * strip :]))
            part = nn(k_t[h * HD : (h + 1) * HD, rows], ds)
            for r in range(c, length // strip):
                at = (r - c) * strip
                dq_t[h][r] += part[:, at : at + strip]
        dk_ref[rows, :] = jnp.where(first, dks[0], dks[1]).astype(BF)
        dv_ref[rows, :] = jnp.where(first, dvs[0], dvs[1]).astype(BF)
    for r in range(length // strip):
        both = jnp.concatenate([dq_t[0][r], dq_t[1][r]], axis=0)
        dq_ref[r * strip : (r + 1) * strip, :] = both.T.astype(BF)


def far_seq(index, f, peers, masks, own):
    slot = index // f
    seq = own ^ (slot % peers)
    bits = slot // peers
    for at, mask in enumerate(masks):
        seq = seq ^ (((bits >> at) & 1) * mask)
    return seq * f + index % f


def final_kernel(peers, masks, near_ref, far_ref, kv_ref, qg_ref, *rest):
    got, rest = rest[: peers - 1], rest[peers - 1 :]
    auxs, rest = rest[:peers], rest[peers:]
    fa_ref, k_ref, v_ref, dq1_ref, dk1_ref, dv1_ref, att_ref, att_out, dq_out, dk_out, dv_out = rest
    group = pl.program_id(0)
    length = k_ref.shape[0]
    n, f = length // R2, length // R3
    blocks = fa_ref.shape[0] // FM
    F = blocks * f
    row_here = lax.axis_index("row")
    own = row_here % peers
    seq = lax.axis_index("col") * lax.axis_size("row") + row_here
    near, far = token_masks(near_ref, far_ref, group, length)
    scale = jnp.asarray(SCALE, BF)

    r, c = iota((5 * F, blocks * FM), 0), iota((5 * F, blocks * FM), 1)
    i, at = r // F, r % F
    sel = onehot(c == at // f * FM + i * f + at % f)
    fa = nn(sel, fa_ref[...]).astype(BF)
    fq, fk, fv, fg, faux = (fa[i * F : (i + 1) * F] for i in range(5))
    qx, gx, ax = expand(fq * scale), expand(fg), expand(faux)
    s = nt(qx, fk)
    dp = nt(gx, fv)
    place_q = far_seq(iota(s.shape, 0) % F, f, peers, masks, seq)
    place_k = far_seq(iota(s.shape, 1), f, peers, masks, seq)
    ok = place_k <= place_q
    s = jnp.where(ok, s, NEG)
    top = jnp.max(s, axis=1, keepdims=True)
    w = jnp.exp(s - top)
    total = jnp.sum(w, axis=1, keepdims=True)
    log3 = top + jnp.log(total)
    dot3 = jnp.sum(w * dp, axis=1, keepdims=True) / total
    log12, dot12 = piece_column(ax, 0), piece_column(ax, 1)
    top = jnp.maximum(log12, log3)
    e12, e3 = jnp.exp(log12 - top), jnp.exp(log3 - top)
    both = e12 + e3
    log_all = top + jnp.log(both)
    dot_all = (e12 * dot12 + e3 * dot3) / both
    p = jnp.exp(s - log_all)
    ds = p * (dp - dot_all)
    pb, dsb = p.astype(BF), ds.astype(BF)
    far_dv = tn(pb, gx)[:FM]
    far_dk = tn(dsb, qx)[:FM]
    far_dq = collapse(nn(dsb, fk))[:FM] * SCALE
    far_out = collapse(nn(pb, fv))[:FM]
    keep = collapse(jnp.broadcast_to(e12 / both, (GH * F, GW)))[:FM]
    att = att_ref[...]
    far_out += keep * nn(far_select(FM, length, 0), att * onehot(far))

    def own_rows(x):
        return jnp.concatenate([x[h * F : h * F + FM] for h in range(GH)], axis=0)

    qx, gx, log_own, dot_own = own_rows(qx), own_rows(gx), own_rows(log_all), own_rows(dot_all)
    k, v = k_ref[...], v_ref[...]
    r = iota((GH * FM, 1), 0)
    reach = jnp.zeros((GH * FM, 1), jnp.int32)
    for h in range(GH):
        reach = jnp.where(r // FM == h, far_ref[group * GH + h], reach)
    reach = jnp.where(r % FM < f, reach + r % FM * R3, -1)
    ok = iota((GH * FM, length), 1) <= reach
    p = jnp.where(ok, jnp.exp(nt(qx, k) - log_own), 0.0)
    ds = (p * (nt(gx, v) - dot_own)).astype(BF)
    far_dq += collapse(nn(ds, k)) * SCALE
    dk = tn(ds, qx)
    dv = tn(p.astype(BF), gx)

    rows = peers * n
    final_aux = collapse(
        pack_aux(jnp.broadcast_to(log_all, (GH * F, GW)), jnp.broadcast_to(dot_all, (GH * F, GW)))
    )[:FM].astype(BF)
    r, c = iota((rows, FM), 0), iota((rows, FM), 1)
    subst = nn(onehot(c == r // n * f + r % n * R2 // R3), final_aux)
    noff, foff = lane_offsets(near_ref, group), lane_offsets(far_ref, group)
    also_far = (iota((rows, GW), 0) % (R3 // R2) == foff // R2) & (foff % R2 == noff)
    naux = jnp.concatenate([a[:n, :] for a in auxs], axis=0)
    naux = jnp.where(also_far, subst, naux.astype(F32)).astype(BF)
    heads = [kv_ref, *got]
    keys = jnp.concatenate([x[:n, :] for x in heads], axis=0)
    values = jnp.concatenate([x[n:, :] for x in heads], axis=0)
    heads = [qg_ref, *got]
    queries = jnp.concatenate([x[:n, :] for x in heads], axis=0) * scale
    grads = jnp.concatenate([x[n:, :] for x in heads], axis=0)

    ax = expand(naux[:n])
    s = nt(expand(queries[:n]), keys)
    dp = nt(expand(grads[:n]), values)
    ok = near_valid_queries(s.shape, n, own)
    p = jnp.where(ok, jnp.exp(s - piece_column(ax, 0)), 0.0)
    ds = (p * (dp - piece_column(ax, 1))).astype(BF)
    near_dq = collapse(nn(ds, keys)) * SCALE

    s = nt(expand(keys[:n]), queries)
    dp = nt(expand(values[:n]), grads)
    ok = near_valid_keys(s.shape, n, own)
    r, c = iota((GH * n, GW), 0), iota((GH * n, GW), 1)
    mine = c // HD == r // n
    log_k = nt(onehot(mine & (c % HD // 3 == 0)), naux)
    dot_k = nt(onehot(mine & (c % HD // 3 == 1)), naux)
    p = jnp.where(ok, jnp.exp(s - log_k), 0.0)
    ds = (p * (dp - dot_k)).astype(BF)
    near_dk = collapse(nn(ds, queries))
    near_dv = collapse(nn(p.astype(BF), grads))

    place_n, place_f = near_place(n, length), far_place(length)

    def terms(near_part, far_part):
        return jnp.where(near, nn(place_n, near_part.astype(BF)), 0.0) + jnp.where(
            far, nn(place_f, far_part.astype(BF)), 0.0
        )

    att_out[...] = jnp.where(far, nn(place_f, far_out.astype(BF)), att.astype(F32)).astype(BF)
    dq_out[...] = (dq1_ref[...].astype(F32) + terms(near_dq, far_dq)).astype(BF)
    dk_out[...] = (dk1_ref[...].astype(F32) + dk + terms(near_dk, far_dk)).astype(BF)
    dv_out[...] = (dv1_ref[...].astype(F32) + dv + terms(near_dv, far_dv)).astype(BF)


def smem():
    return pl.BlockSpec(memory_space=pltpu.SMEM)


def group_block(rows):
    return pl.BlockSpec((rows, GW), lambda g: (0, g))


def params():
    return pltpu.CompilerParams(vmem_limit_bytes=VMEM_LIMIT)


def shards(queries, key_vectors, value_vectors, out_grad, near_offsets, far_offsets):
    length, width = queries.shape
    row_count = lax.axis_size("row")
    col_count = lax.axis_size("col")
    peers = SEG2 // length
    n, f = length // R2, length // R3
    groups = width // GW
    pairs = width // PW

    def like(rows):
        return jax.ShapeDtypeStruct((rows, width), BF)

    def swap(x, axis, mask):
        size = lax.axis_size(axis)
        return lax.ppermute(x, axis, [(i, i ^ mask) for i in range(size)])

    picked = pl.pallas_call(
        functools.partial(pick_kernel, peers),
        grid=(groups,),
        in_specs=[smem(), smem()] + [group_block(length)] * 4,
        out_specs=[group_block(2 * n)] * 2 + [group_block(FM)] + [group_block(2 * n)] * (peers - 1),
        out_shape=[like(2 * n)] * 2 + [like(FM)] + [like(2 * n)] * (peers - 1),
        compiler_params=params(),
        name="pick",
    )(near_offsets, far_offsets, queries, key_vectors, value_vectors, out_grad)
    kv, qg, fr, msgs = picked[0], picked[1], picked[2], picked[3:]
    got = [swap(msgs[s - 1], "row", s) for s in range(1, peers)]

    pair_block = pl.BlockSpec((length, PW), lambda p: (0, p))
    ops = 2 * H * length * length * HD
    att1, aux1 = pl.pallas_call(
        functools.partial(forward_kernel, 256),
        grid=(pairs,),
        in_specs=[pair_block] * 4,
        out_specs=[pair_block] * 2,
        out_shape=[like(length)] * 2,
        compiler_params=params(),
        cost_estimate=pl.CostEstimate(flops=2 * ops * 4, bytes_accessed=6 * length * width * 2, transcendentals=0),
        name="forward",
    )(queries, key_vectors, value_vectors, out_grad)

    mine, aux, att12 = pl.pallas_call(
        functools.partial(merge_kernel, peers),
        grid=(groups,),
        in_specs=[smem(), smem()] + [group_block(2 * n)] * (peers + 1) + [group_block(length)] * 2 + [group_block(FM)],
        out_specs=[group_block(n + FM)] + [group_block(length)] * 2,
        out_shape=[like(n + FM)] + [like(length)] * 2,
        compiler_params=params(),
        name="merge",
    )(near_offsets, far_offsets, kv, qg, *got, aux1, att1, fr)
    theirs = [swap(mine, "row", s) for s in range(1, peers)]

    pieces = 3
    per = pairs // pieces
    grads = []
    for piece in range(pieces):
        block = pl.BlockSpec((length, PW), lambda p, piece=piece: (0, piece * per + p))
        any_spec = pl.BlockSpec(memory_space=pl.ANY)
        aliased = len(grads)
        grads = pl.pallas_call(
            functools.partial(backward_kernel, 256, aliased),
            grid=(per,),
            in_specs=[block] * 5 + [any_spec] * aliased,
            out_specs=[block] * 3,
            out_shape=[like(length)] * 3,
            input_output_aliases={5 + i: i for i in range(aliased)},
            compiler_params=params(),
            cost_estimate=pl.CostEstimate(
                flops=5 * ops * 4 // pieces, bytes_accessed=8 * length * width * 2 // pieces, transcendentals=0
            ),
            name="backward",
        )(queries, key_vectors, value_vectors, out_grad, aux, *grads)

    far_all = jnp.concatenate([x[n:] for x in (mine, *theirs)], axis=0)
    masks = []
    for axis, size, least in (("row", row_count, peers), ("col", col_count, 1)):
        mask = size // 2
        while mask >= least:
            far_all = jnp.concatenate([far_all, swap(far_all, axis, mask)], axis=0)
            masks.append(mask if axis == "row" else mask * row_count)
            mask //= 2

    return pl.pallas_call(
        functools.partial(final_kernel, peers, tuple(masks)),
        grid=(groups,),
        in_specs=[smem(), smem()]
        + [group_block(2 * n)] * (peers + 1)
        + [group_block(n + FM)] * peers
        + [group_block(far_all.shape[0])]
        + [group_block(length)] * 6,
        out_specs=[group_block(length)] * 4,
        out_shape=[like(length)] * 4,
        compiler_params=params(),
        name="final",
    )(near_offsets, far_offsets, kv, qg, *got, mine, *theirs, far_all, key_vectors, value_vectors, *grads, att12)


def solution(mesh):
    placed = (
        P(("col", "row"), None),
        P(("col", "row"), None),
        P(("col", "row"), None),
        P(("col", "row"), None),
        P(),
        P(),
    )
    return jax.shard_map(
        shards,
        mesh=mesh,
        in_specs=placed,
        out_specs=(
            P(("col", "row"), None),
            P(("col", "row"), None),
            P(("col", "row"), None),
            P(("col", "row"), None),
        ),
        check_vma=False,
    )
```

time: 386 us -> 68.7 us (0.18)
  matrix products: 122 us -> 0 us
  blocking collectives: 101 us -> 0 us
  local copies, waits for them, and re-layouts: 85.7 us -> 6.84 us
  other arithmetic: 43.3 us -> 0.01 us
  Pallas kernels: 0 us -> 40.8 us
  between operations: 16 us -> 0.83 us
  starting transfers between devices: 0.35 us -> 12.6 us
  waiting for transfers between devices: 14.9 us -> 7.23 us
    dot_general x96 -> x0, matrix products: 122 us -> none  [the longest x14 24.8 us: backward_block(): jnp.einsum('...qk,...qd->...kd', score_half, queries, preferred_element_t...]
    all_gather x4 -> x0, blocking collectives: 101 us -> none  [the longest x1 44.3 us: shards(): lax.all_gather(far_value, ('row', 'col'), axis=1, tiled=True)]
    pallas_call x0 -> x7, Pallas kernels: none -> 40.8 us  [the longest x3 12 us: shards(): pl.pallas_call(functools.partial(backward_kernel, 256, aliased), grid=(pe...]
    reduce_sum x19 -> x0, other arithmetic: 29 us -> none  [the longest x4 15.5 us: pick(): return jnp.sum(jnp.where(chosen, shaped, zeros), axis=2, dtype=source.dtype)]
    unnamed x99 -> x29, local copies, waits for them, and re-layouts: 24 us -> 6.78 us
    unnamed x4 -> x0, waiting for transfers between devices: 14.9 us -> none
    ppermute x0 -> x9, starting transfers between devices: none -> 12.6 us  [swap(): return lax.ppermute(x, axis, [(i, i ^ mask) for i in range(size)])]
    reshape x12 -> x0, local copies, waits for them, and re-layouts: 12.4 us -> none  [the longest x6 7.17 us: pick(): source.reshape((head_count, length // dilation, dilation) + trailing)]
  transfers between devices with their start and end apart: 3 -> 9, of which waited for: 1 -> 2; matrix products, arithmetic and copies ran while one was open for 29% -> 0% of each run, Pallas kernels for 0% -> 35%
where the time goes in v1:
time: 68.7 us; the launch traced here: 68.2 us
  Pallas kernels  40.8 us (59%)
  starting transfers between devices  12.6 us (18%)
  waiting for transfers between devices  7.23 us (11%)
  local copies, waits for them, and re-layouts  6.84 us (10%)
  between operations  0.83 us (1%)
    ppermute x9, starting transfers between devices, swap(): return lax.ppermute(x, axis, [(i, i ^ mask) for i in range(size)])  12.6 us
    pallas_call x3, Pallas kernels, shards(): pl.pallas_call(functools.partial(backward_kernel, 256, aliased), grid=(pe...  12 us
    pallas_call x1, Pallas kernels, shards(): pl.pallas_call(functools.partial(forward_kernel, 256), grid=(pairs,), in_...  11.6 us
    pallas_call x1, Pallas kernels, shards(): pl.pallas_call(functools.partial(final_kernel, peers, tuple(masks)), grid...  10.2 us
    ppermute x9, waiting for transfers between devices, swap(): return lax.ppermute(x, axis, [(i, i ^ mask) for i in range(size)])  7.23 us
    unnamed x29, local copies, waits for them, and re-layouts  6.78 us
    pallas_call x1, Pallas kernels, shards(): pl.pallas_call(functools.partial(merge_kernel, peers), grid=(groups,), in...  4.61 us
    pallas_call x1, Pallas kernels, shards(): pl.pallas_call(functools.partial(pick_kernel, peers), grid=(groups,), in_...  2.32 us
  transfers between devices with their start and end apart: 9, of which 2 were waited for; matrix products, arithmetic and copies ran while one was open for 0% of the time, Pallas kernels for 35%

profile of v1, /device:TPU:0, one launch (start us, length us, event | category | flops | bytes accessed | tf_op | source)
XLA Modules:
  0.0 68.2 jit_solution(5627684053166176707)
XLA Ops:
  0.6 1.1 %copy-done = bf16[512,768]{1,0:T(8,128)(2,1)S(1)} copy-done((bf16[512,768]{1,0:T(8,128)(2,1)S(1)}, bf16[512,768]{1,0:T(8,128)(2,1)}, u32[]{:S(2)}) %copy-start) | copy-done | bytes 786456
  1.8 1.1 %copy-done.2 = bf16[512,768]{1,0:T(8,128)(2,1)S(1)} copy-done((bf16[512,768]{1,0:T(8,128)(2,1)S(1)}, bf16[512,768]{1,0:T(8,128)(2,1)}, u32[]{:S(2)}) %copy-start.2) | copy-done | bytes 786456
  2.9 1.1 %copy-done.4 = bf16[512,768]{1,0:T(8,128)(2,1)S(1)} copy-done((bf16[512,768]{1,0:T(8,128)(2,1)S(1)}, bf16[512,768]{1,0:T(8,128)(2,1)}, u32[]{:S(2)}) %copy-start.4) | copy-done | bytes 786456
  4.0 1.1 %copy-done.6 = bf16[512,768]{1,0:T(8,128)(2,1)S(1)} copy-done((bf16[512,768]{1,0:T(8,128)(2,1)S(1)}, bf16[512,768]{1,0:T(8,128)(2,1)}, u32[]{:S(2)}) %copy-start.6) | copy-done | bytes 786456
  5.2 0.7 copy-done.9
  5.8 0.7 copy-done.10
  6.5 2.3 %pick.1 = (bf16[64,768]{1,0:T(8,128)(2,1)S(1)}, bf16[64,768]{1,0:T(8,128)(2,1)S(1)}, bf16[16,768]{1,0:T(8,128)(2,1)S(1)}, bf16[64,768]{1,0:T(8,128)(2,1)S(1)}, b...) custom-call(s32[12]{0:T(128)S(1)} %copy-done.9, s32[12]{0:T(128)S(1)} %copy-done.10, ...), custom_call_target="tpu_custom_call" | custom-call | tf_op jit(solution)/shard_map/pick/pallas_call | solution.py:438
  8.8 3.0 %collective-permute-start = (bf16[64,768]{1,0:T(8,128)(2,1)S(1)}, bf16[64,768]{1,0:T(8,128)(2,1)S(1)}, u32[]{:S(2)}, u32[]{:S(2)}) collective-permute-start(bf16[64,768]{1,0:T(8,128)(2,1)S(1)} %get-tuple-element.26), channel_id=1, source_target_pairs={{0,8},{8,0},{16,24},{24,16},{1,9},{9,1},{17,25},{25,17},{2,10},{10... | collective-permute-start | bytes 294920 | tf_op jit(solution)/shard_map/ppermute | solution.py:436
  11.8 1.5 %collective-permute-start.1 = (bf16[64,768]{1,0:T(8,128)(2,1)S(1)}, bf16[64,768]{1,0:T(8,128)(2,1)S(1)}, u32[]{:S(2)}, u32[]{:S(2)}) collective-permute-start(bf16[64,768]{1,0:T(8,128)(2,1)S(1)} %get-tuple-element.27), channel_id=1, source_target_pairs={{0,16},{8,24},{16,0},{24,8},{1,17},{9,25},{17,1},{25,9},{2,18},{10... | collective-permute-start | bytes 294920 | tf_op jit(solution)/shard_map/ppermute | solution.py:436
  13.4 11.6 %forward.1 = (bf16[512,768]{1,0:T(8,128)(2,1)S(1)}, bf16[512,768]{1,0:T(8,128)(2,1)S(1)}) custom-call(bf16[512,768]{1,0:T(8,128)(2,1)S(1)} %copy-done.4, bf16[512,768]{1,0:T(8,128)(2,1)S(1)} %copy-done.1, bf16[512,768]{1,0:T(8,128)(2,1)S(1)} %copy-done.3, bf16[512,768]{1,0:T(8,128)(2,1)S(1)} %copy-done.7), custom_call_target="tpu_custom_call" | custom-call | flops 3221225472 | bytes 4718592 | tf_op jit(solution)/shard_map/forward/pallas_call | solution.py:452
  25.0 4.6 %merge.1 = (bf16[48,768]{1,0:T(8,128)(2,1)S(1)}, bf16[512,768]{1,0:T(8,128)(2,1)S(1)}, bf16[512,768]{1,0:T(8,128)(2,1)S(1)}) custom-call(s32[12]{0:T(128)S(1)} %copy-done.9, s32[12]{0:T(128)S(1)} %copy-done.10, bf16[64,768]{1,0:T(8,128)(2,1)S(1)} %get-tuple-element.24.kv_ref, bf16[64,768]{1,0:T(8,128)(2,1)S(1)} %get-tuple-element.25.qg_ref, ...), custom_call_target="tpu_custom_call" | custom-call | tf_op jit(solution)/shard_map/merge/pallas_call | solution.py:463
  29.7 0.9 %copy-done.11 = bf16[512,768]{1,0:T(8,128)(2,1)} copy-done((bf16[512,768]{1,0:T(8,128)(2,1)}, bf16[512,768]{1,0:T(8,128)(2,1)S(1)}, u32[]{:S(2)}) %copy-start.11) | copy-done | bytes 786456
  30.5 2.9 %collective-permute-start.5 = (bf16[48,768]{1,0:T(8,128)(2,1)S(1)}, bf16[48,768]{1,0:T(8,128)(2,1)S(1)}, u32[]{:S(2)}, u32[]{:S(2)}) collective-permute-start(bf16[48,768]{1,0:T(8,128)(2,1)S(1)} %get-tuple-element.32.rest_3_), channel_id=1, source_target_pairs={{0,24},{8,16},{16,8},{24,0},{1,25},{9,17},{17,9},{25,1},{2,26},{10... | collective-permute-start | bytes 221192 | tf_op jit(solution)/shard_map/ppermute | solution.py:436
  33.4 0.5 collective-permute-start.4
  33.9 0.1 collective-permute-start.3
  34.0 4.3 %collective-permute-done.3.rest_4_ = bf16[48,768]{1,0:T(8,128)(2,1)S(1)} collective-permute-done((bf16[48,768]{1,0:T(8,128)(2,1)S(1)}, bf16[48,768]{1,0:T(8,128)(2,1)S(1)}, u32[]{:S(2)}, u32[]{:S(2)}) %collective-permute-start.3) | collective-permute-done | bytes 73760 | tf_op jit(solution)/shard_map/ppermute | solution.py:436
  38.4 2.7 %collective-permute-start.6 = (bf16[64,768]{1,0:T(8,128)(2,1)S(1)}, bf16[64,768]{1,0:T(8,128)(2,1)S(1)}, u32[]{:S(2)}, u32[]{:S(2)}) collective-permute-start(bf16[64,768]{1,0:T(8,128)(2,1)S(1)} %pad_maximum_fusion), channel_id=1, source_target_pairs={{0,4},{1,5},{2,6},{3,7},{4,0},{5,1},{6,2},{7,3},{8,12},{9,13},{10,... | collective-permute-start | bytes 294920 | tf_op jit(solution)/shard_map/ppermute | solution.py:436
  41.0 2.9 %collective-permute-done.6 = bf16[64,768]{1,0:T(8,128)(2,1)S(1)} collective-permute-done((bf16[64,768]{1,0:T(8,128)(2,1)S(1)}, bf16[64,768]{1,0:T(8,128)(2,1)S(1)}, u32[]{:S(2)}, u32[]{:S(2)}) %collective-permute-start.6) | collective-permute-done | bytes 98336 | tf_op jit(solution)/shard_map/ppermute | solution.py:436
  44.0 1.8 %collective-permute-start.7 = (bf16[128,768]{1,0:T(8,128)(2,1)S(1)}, bf16[128,768]{1,0:T(8,128)(2,1)S(1)}, u32[]{:S(2)}, u32[]{:S(2)}) collective-permute-start(bf16[128,768]{1,0:T(8,128)(2,1)S(1)} %get-tuple-element.48), channel_id=1, source_target_pairs={{0,2},{1,3},{2,0},{3,1},{4,6},{5,7},{6,4},{7,5},{8,10},{9,11},{10,... | collective-permute-start | bytes 589832 | tf_op jit(solution)/shard_map/ppermute | solution.py:436
  45.8 4.0 %backward.3 = (bf16[512,768]{1,0:T(8,128)(2,1)S(1)}, bf16[512,768]{1,0:T(8,128)(2,1)S(1)}, bf16[512,768]{1,0:T(8,128)(2,1)S(1)}) custom-call(bf16[512,768]{1,0:T(8,128)(2,1)S(1)} %copy-done.5, bf16[512,768]{1,0:T(8,128)(2,1)S(1)} %copy-done.1, bf16[512,768]{1,0:T(8,128)(2,1)S(1)} %copy-done.3, bf16[512,768]{1,0:T(8,128)(2,1)S(1)} %copy-done.7, ...), custom_call_target="tpu_custom_call" | custom-call | flops 2684354560 | bytes 2097152 | tf_op jit(solution)/shard_map/backward/pallas_call | solution.py:481
  49.8 0.1 collective-permute-start.8
  49.9 4.0 %backward.4 = (bf16[512,768]{1,0:T(8,128)(2,1)S(1)}, bf16[512,768]{1,0:T(8,128)(2,1)S(1)}, bf16[512,768]{1,0:T(8,128)(2,1)S(1)}) custom-call(bf16[512,768]{1,0:T(8,128)(2,1)S(1)} %copy-done.5, bf16[512,768]{1,0:T(8,128)(2,1)S(1)} %copy-done.1, bf16[512,768]{1,0:T(8,128)(2,1)S(1)} %copy-done.3, ...), custom_call_target="tpu_custom_call", output_to_operand_aliasing={{0}: (5, {}), {1}: (6, {}), {2}: (7, {})} | custom-call | flops 2684354560 | bytes 2097152 | tf_op jit(solution)/shard_map/backward/pallas_call | solution.py:481
  54.0 4.0 %backward.5 = (bf16[512,768]{1,0:T(8,128)(2,1)S(1)}, bf16[512,768]{1,0:T(8,128)(2,1)S(1)}, bf16[512,768]{1,0:T(8,128)(2,1)S(1)}) custom-call(bf16[512,768]{1,0:T(8,128)(2,1)S(1)} %copy-done.5, bf16[512,768]{1,0:T(8,128)(2,1)S(1)} %copy-done.1, bf16[512,768]{1,0:T(8,128)(2,1)S(1)} %copy-done.3, ...), custom_call_target="tpu_custom_call", output_to_operand_aliasing={{0}: (5, {}), {1}: (6, {}), {2}: (7, {})} | custom-call | flops 2684354560 | bytes 2097152 | tf_op jit(solution)/shard_map/backward/pallas_call | solution.py:481
  58.0 10.2 %final.1 = (bf16[512,768]{1,0:T(8,128)(2,1)}, bf16[512,768]{1,0:T(8,128)(2,1)}, bf16[512,768]{1,0:T(8,128)(2,1)}, bf16[512,768]{1,0:T(8,128)(2,1)}) custom-call(s32[12]{0:T(128)S(1)} %copy-done.9, s32[12]{0:T(128)S(1)} %copy-done.10, bf16[64,768]{1,0:T(8,128)(2,1)S(1)} %get-tuple-element.24.kv_ref, bf16[64,768]{1,0:T(8,128)(2,1)S(1)} %get-tuple-element.25.qg_ref, ...), custom_call_target="tpu_custom_call" | custom-call | tf_op jit(solution)/shard_map/final/pallas_call | solution.py:504
  (33 shorter events, 0.2 us)
Async XLA Ops:
  0.6 1.1 %copy-start = (bf16[512,768]{1,0:T(8,128)(2,1)S(1)}, bf16[512,768]{1,0:T(8,128)(2,1)}, u32[]{:S(2)}) copy-start(bf16[512,768]{1,0:T(8,128)(2,1)} %rest_8_.1) | copy-start | bytes 2359300
  1.8 1.1 %copy-start.2 = (bf16[512,768]{1,0:T(8,128)(2,1)S(1)}, bf16[512,768]{1,0:T(8,128)(2,1)}, u32[]{:S(2)}) copy-start(bf16[512,768]{1,0:T(8,128)(2,1)} %rest_9_.1) | copy-start | bytes 2359300
  2.9 1.1 %copy-start.4 = (bf16[512,768]{1,0:T(8,128)(2,1)S(1)}, bf16[512,768]{1,0:T(8,128)(2,1)}, u32[]{:S(2)}) copy-start(bf16[512,768]{1,0:T(8,128)(2,1)} %q_ref.9) | copy-start | bytes 2359300
  4.0 1.1 %copy-start.6 = (bf16[512,768]{1,0:T(8,128)(2,1)S(1)}, bf16[512,768]{1,0:T(8,128)(2,1)}, u32[]{:S(2)}) copy-start(bf16[512,768]{1,0:T(8,128)(2,1)} %g_ref.9) | copy-start | bytes 2359300
  5.2 0.7 copy-start.9
  5.8 0.7 copy-start.10
  6.5 6.9 %copy-start.1 = (bf16[512,768]{1,0:T(8,128)(2,1)S(1)}, bf16[512,768]{1,0:T(8,128)(2,1)}, u32[]{:S(2)}) copy-start(bf16[512,768]{1,0:T(8,128)(2,1)} %rest_8_.1) | copy-start | bytes 2359300
  6.5 6.9 %copy-start.3 = (bf16[512,768]{1,0:T(8,128)(2,1)S(1)}, bf16[512,768]{1,0:T(8,128)(2,1)}, u32[]{:S(2)}) copy-start(bf16[512,768]{1,0:T(8,128)(2,1)} %rest_9_.1) | copy-start | bytes 2359300
  6.5 6.9 %copy-start.7 = (bf16[512,768]{1,0:T(8,128)(2,1)S(1)}, bf16[512,768]{1,0:T(8,128)(2,1)}, u32[]{:S(2)}) copy-start(bf16[512,768]{1,0:T(8,128)(2,1)} %g_ref.9) | copy-start | bytes 2359300
  8.8 16.2 %collective-permute-start = (bf16[64,768]{1,0:T(8,128)(2,1)S(1)}, bf16[64,768]{1,0:T(8,128)(2,1)S(1)}, u32[]{:S(2)}, u32[]{:S(2)}) collective-permute-start(bf16[64,768]{1,0:T(8,128)(2,1)S(1)} %get-tuple-element.26), channel_id=1, source_target_pairs={{0,8},{8,0},{16,24},{24,16},{1,9},{9,1},{17,25},{25,17},{2,10},{10... | collective-permute-start | bytes 294920 | tf_op jit(solution)/shard_map/ppermute | solution.py:436
  11.8 13.2 %collective-permute-start.1 = (bf16[64,768]{1,0:T(8,128)(2,1)S(1)}, bf16[64,768]{1,0:T(8,128)(2,1)S(1)}, u32[]{:S(2)}, u32[]{:S(2)}) collective-permute-start(bf16[64,768]{1,0:T(8,128)(2,1)S(1)} %get-tuple-element.27), channel_id=1, source_target_pairs={{0,16},{8,24},{16,0},{24,8},{1,17},{9,25},{17,1},{25,9},{2,18},{10... | collective-permute-start | bytes 294920 | tf_op jit(solution)/shard_map/ppermute | solution.py:436
  13.3 11.7 %collective-permute-start.2 = (bf16[64,768]{1,0:T(8,128)(2,1)S(1)}, bf16[64,768]{1,0:T(8,128)(2,1)S(1)}, u32[]{:S(2)}, u32[]{:S(2)}) collective-permute-start(bf16[64,768]{1,0:T(8,128)(2,1)S(1)} %get-tuple-element.28), channel_id=1, source_target_pairs={{0,24},{8,16},{16,8},{24,0},{1,25},{9,17},{17,9},{25,1},{2,26},{10... | collective-permute-start | bytes 294920 | tf_op jit(solution)/shard_map/ppermute | solution.py:436
  29.6 0.9 %copy-start.11 = (bf16[512,768]{1,0:T(8,128)(2,1)}, bf16[512,768]{1,0:T(8,128)(2,1)S(1)}, u32[]{:S(2)}) copy-start(bf16[512,768]{1,0:T(8,128)(2,1)S(1)} %get-tuple-element.33.aux_ref) | copy-start | bytes 2359300
  30.5 13.5 %copy-start.8 = (bf16[512,768]{1,0:T(8,128)(2,1)}, bf16[512,768]{1,0:T(8,128)(2,1)S(1)}, u32[]{:S(2)}) copy-start(bf16[512,768]{1,0:T(8,128)(2,1)S(1)} %get-tuple-element.43.rest_13_) | copy-start | bytes 2359300
  30.5 15.3 %copy-start.5 = (bf16[512,768]{1,0:T(8,128)(2,1)S(1)}, bf16[512,768]{1,0:T(8,128)(2,1)}, u32[]{:S(2)}) copy-start(bf16[512,768]{1,0:T(8,128)(2,1)} %q_ref.9) | copy-start | bytes 2359300
  30.5 7.8 %collective-permute-start.5 = (bf16[48,768]{1,0:T(8,128)(2,1)S(1)}, bf16[48,768]{1,0:T(8,128)(2,1)S(1)}, u32[]{:S(2)}, u32[]{:S(2)}) collective-permute-start(bf16[48,768]{1,0:T(8,128)(2,1)S(1)} %get-tuple-element.32.rest_3_), channel_id=1, source_target_pairs={{0,24},{8,16},{16,8},{24,0},{1,25},{9,17},{17,9},{25,1},{2,26},{10... | collective-permute-start | bytes 221192 | tf_op jit(solution)/shard_map/ppermute | solution.py:436
  33.4 4.9 %collective-permute-start.4 = (bf16[48,768]{1,0:T(8,128)(2,1)S(1)}, bf16[48,768]{1,0:T(8,128)(2,1)S(1)}, u32[]{:S(2)}, u32[]{:S(2)}) collective-permute-start(bf16[48,768]{1,0:T(8,128)(2,1)S(1)} %get-tuple-element.32.rest_3_), channel_id=1, source_target_pairs={{0,16},{8,24},{16,0},{24,8},{1,17},{9,25},{17,1},{25,9},{2,18},{10... | collective-permute-start | bytes 221192 | tf_op jit(solution)/shard_map/ppermute | solution.py:436
  33.9 4.4 %collective-permute-start.3 = (bf16[48,768]{1,0:T(8,128)(2,1)S(1)}, bf16[48,768]{1,0:T(8,128)(2,1)S(1)}, u32[]{:S(2)}, u32[]{:S(2)}) collective-permute-start(bf16[48,768]{1,0:T(8,128)(2,1)S(1)} %get-tuple-element.32.rest_3_), channel_id=1, source_target_pairs={{0,8},{8,0},{16,24},{24,16},{1,9},{9,1},{17,25},{25,17},{2,10},{10... | collective-permute-start | bytes 221192 | tf_op jit(solution)/shard_map/ppermute | solution.py:436
  38.4 5.6 %collective-permute-start.6 = (bf16[64,768]{1,0:T(8,128)(2,1)S(1)}, bf16[64,768]{1,0:T(8,128)(2,1)S(1)}, u32[]{:S(2)}, u32[]{:S(2)}) collective-permute-start(bf16[64,768]{1,0:T(8,128)(2,1)S(1)} %pad_maximum_fusion), channel_id=1, source_target_pairs={{0,4},{1,5},{2,6},{3,7},{4,0},{5,1},{6,2},{7,3},{8,12},{9,13},{10,... | collective-permute-start | bytes 294920 | tf_op jit(solution)/shard_map/ppermute | solution.py:436
  44.0 5.8 %collective-permute-start.7 = (bf16[128,768]{1,0:T(8,128)(2,1)S(1)}, bf16[128,768]{1,0:T(8,128)(2,1)S(1)}, u32[]{:S(2)}, u32[]{:S(2)}) collective-permute-start(bf16[128,768]{1,0:T(8,128)(2,1)S(1)} %get-tuple-element.48), channel_id=1, source_target_pairs={{0,2},{1,3},{2,0},{3,1},{4,6},{5,7},{6,4},{7,5},{8,10},{9,11},{10,... | collective-permute-start | bytes 589832 | tf_op jit(solution)/shard_map/ppermute | solution.py:436
  49.8 8.1 %collective-permute-start.8 = (bf16[256,768]{1,0:T(8,128)(2,1)S(1)}, bf16[256,768]{1,0:T(8,128)(2,1)S(1)}, u32[]{:S(2)}, u32[]{:S(2)}) collective-permute-start(bf16[256,768]{1,0:T(8,128)(2,1)S(1)} %get-tuple-element.44), channel_id=1, source_target_pairs={{0,1},{1,0},{2,3},{3,2},{4,5},{5,4},{6,7},{7,6},{8,9},{9,8},{10,11... | collective-permute-start | bytes 1179656 | tf_op jit(solution)/shard_map/ppermute | solution.py:436

commit v2 on v1

v2 whole, which is shorter than its diff:
```python
import functools

import jax
import jax.numpy as jnp
from jax import lax
from jax.experimental import pallas as pl
from jax.experimental.pallas import tpu as pltpu
from jax.sharding import PartitionSpec as P

H = 12
HD = 64
R2 = 16
R3 = 256
S1 = 512
SEG2 = 2048

NEG = -1e30
SCALE = HD**-0.5
GH = 4
GW = GH * HD
PW = 2 * HD
FM = 16
F32 = jnp.float32
BF = jnp.bfloat16
VMEM_LIMIT = 40
PICK_LIMIT = 62


def iota(shape, axis):
    return lax.broadcasted_iota(jnp.int32, shape, axis)


def nn(a, b):
    return lax.dot_general(a, b, (((1,), (0,)), ((), ())), preferred_element_type=F32)


def nt(a, b):
    return lax.dot_general(a, b, (((1,), (1,)), ((), ())), preferred_element_type=F32)


def tn(a, b):
    return lax.dot_general(a, b, (((0,), (0,)), ((), ())), preferred_element_type=F32)


def onehot(cond):
    return jnp.where(cond, 1.0, 0.0).astype(BF)


def lane_offsets(ref, group):
    head = iota((1, GW), 1) // HD
    out = jnp.zeros((1, GW), jnp.int32)
    for h in range(GH):
        out = jnp.where(head == h, ref[group * GH + h], out)
    return out


def expand(x):
    head = iota((1, GW), 1) // HD
    return jnp.concatenate([x * onehot(head == h) for h in range(GH)], axis=0)


def collapse(x):
    n = x.shape[0] // GH
    head = iota((1, GW), 1) // HD
    out = x[:n]
    for h in range(1, GH):
        out = jnp.where(head == h, x[h * n : (h + 1) * n], out)
    return out


def split3(x):
    hi = x.astype(BF)
    rest = x - hi.astype(F32)
    mid = rest.astype(BF)
    low = (rest - mid.astype(F32)).astype(BF)
    return hi.astype(F32), mid.astype(F32), low.astype(F32)


def pack_aux(log_total, row_dot):
    lane = iota((1, log_total.shape[1]), 1) % HD
    out = jnp.zeros(log_total.shape, F32)
    for at, piece in enumerate(split3(log_total) + split3(row_dot)):
        out = jnp.where(lane == at, piece, out)
    return out


def spread_sum(x, width):
    block = onehot(iota((width, width), 0) // HD == iota((width, width), 1) // HD)
    hi = x.astype(BF)
    low = (x - hi.astype(F32)).astype(BF)
    return nn(hi, block) + nn(low, block)


def piece_column(aux_expanded, which):
    a = iota((GW, 128), 0)
    return nn(aux_expanded, onehot(a % HD // 3 == which))[:, :1]


def near_select(n, length):
    return onehot(iota((n, length), 1) // R2 == iota((n, length), 0))


def near_place(n, length):
    return onehot(iota((length, n), 0) // R2 == iota((length, n), 1))


def far_select(rows, length, first):
    return onehot(iota((rows, length), 1) // R3 == iota((rows, length), 0) - first)


def far_place(length):
    return onehot(iota((length, FM), 0) // R3 == iota((length, FM), 1))


def token_masks(near_ref, far_ref, group, length):
    t = iota((length, GW), 0)
    near = t % R2 == lane_offsets(near_ref, group)
    far = t % R3 == lane_offsets(far_ref, group)
    return near, far


def pick_kernel(peers, near_ref, far_ref, q_ref, k_ref, v_ref, g_ref, kv_ref, qg_ref, fr_ref, *msg_refs):
    group = pl.program_id(0)
    length = q_ref.shape[0]
    n, f = length // R2, length // R3
    near, far = token_masks(near_ref, far_ref, group, length)
    near, far = onehot(near), onehot(far)
    sel = near_select(n, length)
    q, k, v, g = q_ref[...], k_ref[...], v_ref[...], g_ref[...]
    picked = [nn(sel, x * near).astype(BF) for x in (k, v, q, g)]
    kv = jnp.concatenate(picked[:2], axis=0)
    qg = jnp.concatenate(picked[2:], axis=0)
    kv_ref[...] = kv
    qg_ref[...] = qg
    fr = jnp.zeros((FM, GW), F32)
    for at, x in enumerate((q, k, v, g)):
        fr += nn(far_select(FM, length, at * f), x * far)
    fr_ref[...] = fr.astype(BF)
    own = lax.axis_index("row") % peers
    for slot in range(1, peers):
        later = (own ^ slot) > own

        @pl.when(later)
        def _(slot=slot):
            msg_refs[slot - 1][...] = kv

        @pl.when(jnp.logical_not(later))
        def _(slot=slot):
            msg_refs[slot - 1][...] = qg


def staged(units, stages, skew):
    for t in range(len(units) + (len(stages) - 1) * skew):
        for i, stage in enumerate(stages):
            if 0 <= t - i * skew < len(units):
                stage(*units[t - i * skew])


def lockstep(bodies):
    bodies = list(bodies)
    while bodies:
        for body in list(bodies):
            try:
                next(body)
            except StopIteration:
                bodies.remove(body)


def head_masks():
    first = iota((1, PW), 1) < HD
    return first, (onehot(first), onehot(jnp.logical_not(first)))


def eye_of(n):
    return onehot(iota((n, n), 0) == iota((n, n), 1))


def pair_columns(p):
    return slice(p * PW, (p + 1) * PW)


def forward_kernel(strip, skew, q_ref, k_ref, v_ref, g_ref, att_ref, st_ref):
    length, width = q_ref.shape
    _, in_head = head_masks()
    diag = iota((strip, strip), 0) <= iota((strip, strip), 1)
    eye = eye_of(PW)
    kept = {}

    def score(p, r, h):
        cols, rows = pair_columns(p), slice(r * strip, (r + 1) * strip)
        if r == 0 and h == 0:
            kept["v", p] = nt(eye, v_ref[:, cols]).astype(BF)
            kept["g", p] = nt(eye, g_ref[:, cols])
        q = q_ref[rows, cols] * jnp.asarray(SCALE, BF) * in_head[h]
        kept["s", p, r, h] = nt(k_ref[: (r + 1) * strip, cols], q)

    def soften(p, r, h):
        s = kept.pop(("s", p, r, h))
        last = jnp.where(diag, s[r * strip :], NEG)
        s = jnp.concatenate([s[: r * strip], last], axis=0) if r else last
        top = jnp.max(s, axis=0, keepdims=True)
        w = jnp.exp(s - top)
        kept["w", p, r, h] = w.astype(BF), top, jnp.sum(w, axis=0, keepdims=True)

    def mix(p, r, h):
        cols, rows = pair_columns(p), slice(r * strip, (r + 1) * strip)
        lanes = slice(h * HD, (h + 1) * HD)
        w, top, total = kept.pop(("w", p, r, h))
        out = nn(kept["v", p][lanes, : (r + 1) * strip], w) / total
        kept["o", p, r, h] = out
        st_ref[p * 8 + h : p * 8 + h + 1, rows] = top + jnp.log(total)
        st_ref[p * 8 + 2 + h : p * 8 + 3 + h, rows] = jnp.sum(
            out * kept["g", p][lanes, rows], axis=0, keepdims=True
        )
        if h == 1:
            both = jnp.concatenate([kept.pop(("o", p, r, 0)), kept.pop(("o", p, r, 1))], axis=0)
            att_ref[rows, cols] = both.T.astype(BF)

    for p in range(width // PW):
        st_ref[p * 8 + 4 : p * 8 + 8, :] = jnp.zeros((4, length), F32)
    units = [(p, r, h) for p in range(width // PW) for r in range(length // strip) for h in range(2)]
    staged(units, (score, soften, mix), skew)


def near_valid_queries(shape, n, own):
    row, lane = iota(shape, 0) % n, iota(shape, 1)
    slot, key = lane // n, lane % n
    return ((slot ^ own) < own) | ((slot == 0) & (key <= row))


def near_valid_keys(shape, n, own):
    row, lane = iota(shape, 0) % n, iota(shape, 1)
    slot, query = lane // n, lane % n
    return ((slot ^ own) > own) | ((slot == 0) & (row <= query))


SR = GH // 2 * 8


def stat_row(shape, axis):
    r = iota(shape, axis) % SR
    return r // 8 * 2 + r % 2, r % 8 // 2


def stat_offsets(ref, group):
    head, _ = stat_row((SR, 1), 0)
    out = jnp.zeros((SR, 1), jnp.int32)
    for h in range(GH):
        out = jnp.where(head == h, ref[group * GH + h], out)
    return out


def pieces3(x):
    return jnp.concatenate([piece.astype(BF) for piece in split3(x)], axis=0)


def group_columns(group):
    return slice(group * GW, (group + 1) * GW)


def fetch(sources, targets, sems):
    copies = []
    for i, (source, target) in enumerate(zip(sources, targets)):
        copy = pltpu.make_async_copy(source, target, sems.at[i])
        copy.start()
        copies.append(copy)
    return copies


def merge_group(peers, group, near_ref, far_ref, kv_ref, qg_ref, got, st_ref, att_ref, fr_ref, out_ref, st_out, near_out):
    cols = group_columns(group)
    srows = slice(group * SR, (group + 1) * SR)
    length = att_ref.shape[0]
    n, f = length // R2, length // R3
    own = lax.axis_index("row") % peers
    heads = (kv_ref, *got)
    keys = jnp.concatenate([r[:n, cols] for r in heads], axis=0)
    values = jnp.concatenate([r[n:, cols] for r in heads], axis=0)
    s = nt(expand(qg_ref[:n, cols] * jnp.asarray(SCALE, BF)), keys)
    yield
    st = st_ref[srows, :]
    t = iota((SR, length), 1)
    near_st = t % R2 == stat_offsets(near_ref, group)
    far_st = t % R3 == stat_offsets(far_ref, group)
    sel = near_select(n, length)
    log1 = nt(sel, pieces3(jnp.where(near_st, st, 0.0)))
    near = onehot(iota((length, GW), 0) % R2 == lane_offsets(near_ref, group))
    out1 = nn(sel, att_ref[:, cols] * near)
    yield
    s = jnp.where(near_valid_queries(s.shape, n, own), s, NEG)
    top = jnp.max(s, axis=1, keepdims=True)
    yield
    w = jnp.exp(s - top)
    total = jnp.sum(w, axis=1, keepdims=True)
    out2 = nn(w.astype(BF), values)
    head, what = stat_row((3 * SR, GW), 0)
    lane = iota((3 * SR, GW), 1)
    log1 = nn(log1.astype(BF), onehot((lane // HD == head) & (what == 0)))
    yield
    out2 = collapse(out2 / total)
    log2 = collapse(jnp.broadcast_to(top + jnp.log(total), (GH * n, GW)))
    top = jnp.maximum(log1, log2)
    e1, e2 = jnp.exp(log1 - top), jnp.exp(log2 - top)
    both = e1 + e2
    log12 = top + jnp.log(both)
    out12 = (e1 * out1 + e2 * out2) / both
    near_out[:, cols] = out12.astype(BF)
    dot12 = spread_sum(qg_ref[n:, cols].astype(F32) * out12, GW)
    yield
    aux12 = pack_aux(log12, dot12).astype(BF)
    out_ref[:n, cols] = aux12
    head, what = stat_row((SR, GW), 0)
    lane = iota((SR, GW), 1)
    compact = nt(onehot((lane // HD == head) & (lane % HD // 3 == what)), aux12)
    yield
    place = onehot(iota((n, length), 1) // R2 == iota((n, length), 0))
    placed = nn(pieces3(compact), place)
    yield
    placed = placed[:SR] + placed[SR : 2 * SR] + placed[2 * SR :]
    st = jnp.where(near_st, placed, st)
    st_out[srows, :] = jnp.where(far_st, -NEG, st)
    far_aux = nt(far_select(FM, length, 4 * f), pieces3(jnp.where(far_st, st, 0.0)))
    yield
    head, what = stat_row((3 * SR, GW), 0)
    lane, piece = iota((3 * SR, GW), 1), iota((3 * SR, GW), 0) // SR
    far_aux = nn(far_aux.astype(BF), onehot((lane // HD == head) & (lane % HD == what * 3 + piece)))
    out_ref[n:, cols] = (fr_ref[:, cols].astype(F32) + far_aux).astype(BF)


def merge_kernel(peers, near_ref, far_ref, kv_ref, qg_ref, *rest):
    got, rest = rest[: peers - 1], rest[peers - 1 :]
    groups = kv_ref.shape[1] // GW
    lockstep(merge_group(peers, group, near_ref, far_ref, kv_ref, qg_ref, got, *rest) for group in range(groups))


def backward_kernel(strip, skew, aliased, q_ref, k_ref, v_ref, g_ref, st_ref, *rest):
    dq_ref, dk_ref, dv_ref = rest[aliased:]
    length, width = q_ref.shape
    first, in_head = head_masks()
    diag = iota((strip, strip), 0) <= iota((strip, strip), 1)
    eye = eye_of(PW)
    strips = length // strip
    kept = {}

    def score(p, c, h):
        cols, rows = pair_columns(p), slice(c * strip, (c + 1) * strip)
        if c == 0 and h == 0:
            kept["k", p] = (nt(eye, k_ref[:, cols]) * SCALE).astype(BF)
            kept["q", p] = q_ref[:, cols] * jnp.asarray(SCALE, BF)
        s = nt(k_ref[rows, cols] * in_head[h], kept["q", p][c * strip :])
        dp = nt(v_ref[rows, cols] * in_head[h], g_ref[c * strip :, cols])
        kept["s", p, c, h] = s, dp

    def soften(p, c, h):
        s, dp = kept.pop(("s", p, c, h))
        prob = jnp.exp(s - st_ref[p * 8 + h : p * 8 + h + 1, c * strip :])
        head = jnp.where(diag, prob[:, :strip], 0.0)
        prob = jnp.concatenate([head, prob[:, strip:]], axis=1) if c + 1 < strips else head
        ds = prob * (dp - st_ref[p * 8 + 2 + h : p * 8 + 3 + h, c * strip :])
        kept["p", p, c, h] = prob.astype(BF), ds.astype(BF)

    def mix(p, c, h):
        cols, rows = pair_columns(p), slice(c * strip, (c + 1) * strip)
        prob, ds = kept.pop(("p", p, c, h))
        dv = nn(prob, g_ref[c * strip :, cols])
        dk = nn(ds, kept["q", p][c * strip :])
        part = nn(kept["k", p][h * HD : (h + 1) * HD, rows], ds)
        for r in range(c, strips):
            term = part[:, (r - c) * strip : (r - c + 1) * strip]
            kept["dq", p, r, h] = kept["dq", p, r, h] + term if c else term
        kept["dkv", p, c, h] = dk, dv
        if h == 1:
            one, two = kept.pop(("dkv", p, c, 0)), kept.pop(("dkv", p, c, 1))
            dk_ref[rows, cols] = jnp.where(first, one[0], two[0]).astype(BF)
            dv_ref[rows, cols] = jnp.where(first, one[1], two[1]).astype(BF)
            both = jnp.concatenate([kept.pop(("dq", p, c, 0)), kept.pop(("dq", p, c, 1))], axis=0)
            dq_ref[rows, cols] = both.T.astype(BF)

    units = [(p, c, h) for p in range(width // PW) for c in range(strips) for h in range(2)]
    staged(units, (score, soften, mix), skew)


def far_seq(index, f, peers, masks, own):
    slot = index // f
    seq = own ^ (slot % peers)
    bits = slot // peers
    for at, mask in enumerate(masks):
        seq = seq ^ (((bits >> at) & 1) * mask)
    return seq * f + index % f


def final_group(
    peers, masks, group, near_ref, far_ref, got, auxs, fa_ref, k_ref, v_ref, base, near_out, outs, ready, done
):
    kv_ref, qg_ref, got = got[0], got[1], got[2:]
    cols = group_columns(group)
    length = k_ref.shape[0]
    n, f = length // R2, length // R3
    blocks = fa_ref.shape[0] // FM
    F = blocks * f
    row_here = lax.axis_index("row")
    own = row_here % peers
    seq = lax.axis_index("col") * lax.axis_size("row") + row_here
    scale = jnp.asarray(SCALE, BF)

    ready("far")
    r, c = iota((5 * F, blocks * FM), 0), iota((5 * F, blocks * FM), 1)
    i, at = r // F, r % F
    sel = onehot(c == at // f * FM + i * f + at % f)
    fa = nn(sel, fa_ref[:, cols])
    yield
    fa = fa.astype(BF)
    fq, fk, fv, fg, faux = (fa[i * F : (i + 1) * F] for i in range(5))
    qx, gx, ax = expand(fq * scale), expand(fg), expand(faux)
    s = nt(qx, fk)
    dp = nt(gx, fv)
    log12, dot12 = piece_column(ax, 0), piece_column(ax, 1)
    yield
    ready("near")
    heads = [kv_ref, *got]
    keys = jnp.concatenate([x[:n, cols] for x in heads], axis=0)
    values = jnp.concatenate([x[n:, cols] for x in heads], axis=0)
    heads = [qg_ref, *got]
    queries = jnp.concatenate([x[:n, cols] for x in heads], axis=0) * scale
    grads = jnp.concatenate([x[n:, cols] for x in heads], axis=0)
    near_s = nt(expand(queries[:n]), keys)
    near_dp = nt(expand(grads[:n]), values)
    near_s2 = nt(expand(keys[:n]), queries)
    near_dp2 = nt(expand(values[:n]), grads)
    yield
    place_q = far_seq(iota((GH * F, 1), 0) % F, f, peers, masks, seq)
    place_k = far_seq(iota((1, F), 1), f, peers, masks, seq)
    s = jnp.where(place_k <= place_q, s, NEG)
    top = jnp.max(s, axis=1, keepdims=True)
    yield
    w = jnp.exp(s - top)
    total = jnp.sum(w, axis=1, keepdims=True)
    dot3 = jnp.sum(w * dp, axis=1, keepdims=True)
    yield
    log3 = top + jnp.log(total)
    dot3 = dot3 / total
    top = jnp.maximum(log12, log3)
    e12, e3 = jnp.exp(log12 - top), jnp.exp(log3 - top)
    both = e12 + e3
    log_all = top + jnp.log(both)
    dot_all = (e12 * dot12 + e3 * dot3) / both
    p = jnp.exp(s - log_all)
    ds = p * (dp - dot_all)
    pb, dsb = p.astype(BF), ds.astype(BF)
    yield
    far_dv = tn(pb, gx)[:FM]
    far_dk = tn(dsb, qx)[:FM]
    far_dq = collapse(nn(dsb, fk))[:FM] * SCALE
    far_out = collapse(nn(pb, fv))[:FM]
    keep = collapse(jnp.broadcast_to(e12 / both, (GH * F, GW)))[:FM]
    yield

    def own_rows(x):
        return jnp.concatenate([x[h * F : h * F + FM] for h in range(GH)], axis=0)

    ready("local")
    qx, gx, log_own, dot_own = own_rows(qx), own_rows(gx), own_rows(log_all), own_rows(dot_all)
    k, v = k_ref[:, cols], v_ref[:, cols]
    s = nt(qx, k)
    dp = nt(gx, v)

    rows = peers * n
    final_aux = collapse(
        pack_aux(jnp.broadcast_to(log_all, (GH * F, GW)), jnp.broadcast_to(dot_all, (GH * F, GW)))
    )[:FM].astype(BF)
    r, c = iota((rows, FM), 0), iota((rows, FM), 1)
    subst = nn(onehot(c == r // n * f + r % n * R2 // R3), final_aux)
    yield
    noff, foff = lane_offsets(near_ref, group), lane_offsets(far_ref, group)
    also_far = (iota((rows, GW), 0) % (R3 // R2) == foff // R2) & (foff % R2 == noff)
    naux = jnp.concatenate([a[:n, cols] for a in auxs], axis=0)
    naux = jnp.where(also_far, subst, naux.astype(F32)).astype(BF)
    ax = expand(naux[:n])
    log_q, dot_q = piece_column(ax, 0), piece_column(ax, 1)
    r, c = iota((GH * n, GW), 0), iota((GH * n, GW), 1)
    mine = c // HD == r // n
    log_k = nt(onehot(mine & (c % HD // 3 == 0)), naux)
    dot_k = nt(onehot(mine & (c % HD // 3 == 1)), naux)
    yield
    r = iota((GH * FM, 1), 0)
    reach = jnp.zeros((GH * FM, 1), jnp.int32)
    for h in range(GH):
        reach = jnp.where(r // FM == h, far_ref[group * GH + h], reach)
    reach = jnp.where(r % FM < f, reach + r % FM * R3, -1)
    ok = iota((GH * FM, length), 1) <= reach
    p = jnp.where(ok, jnp.exp(s - log_own), 0.0)
    ds = (p * (dp - dot_own)).astype(BF)
    pb = p.astype(BF)
    yield
    far_dq += collapse(nn(ds, k)) * SCALE
    dk = tn(ds, qx)
    dv = tn(pb, gx)
    yield
    ok = near_valid_queries(near_s.shape, n, own)
    p = jnp.where(ok, jnp.exp(near_s - log_q), 0.0)
    ds = (p * (near_dp - dot_q)).astype(BF)
    ok = near_valid_keys(near_s2.shape, n, own)
    p2 = jnp.where(ok, jnp.exp(near_s2 - log_k), 0.0)
    ds2 = (p2 * (near_dp2 - dot_k)).astype(BF)
    yield
    near_dq = collapse(nn(ds, keys)) * SCALE
    near_dk = collapse(nn(ds2, queries))
    near_dv = collapse(nn(p2.astype(BF), grads))
    yield
    ready("base")
    near, far = token_masks(near_ref, far_ref, group, length)
    place_n, place_f = near_place(n, length), far_place(length)
    att = jnp.where(near, nn(place_n, near_out[:, cols]), base[0][:, cols].astype(F32))
    far_out += keep * nn(far_select(FM, length, 0), att.astype(BF) * onehot(far))
    yield

    def terms(near_part, far_part):
        return jnp.where(near, nn(place_n, near_part.astype(BF)), 0.0) + jnp.where(
            far, nn(place_f, far_part.astype(BF)), 0.0
        )

    outs[1][:, cols] = (base[1][:, cols].astype(F32) + terms(near_dq, far_dq)).astype(BF)
    done(1, cols)
    yield
    outs[2][:, cols] = (base[2][:, cols].astype(F32) + dk + terms(near_dk, far_dk)).astype(BF)
    done(2, cols)
    yield
    outs[3][:, cols] = (base[3][:, cols].astype(F32) + dv + terms(near_dv, far_dv)).astype(BF)
    done(3, cols)
    yield
    outs[0][:, cols] = jnp.where(far, nn(place_f, far_out.astype(BF)), att).astype(BF)
    done(0, cols)


def final_kernel(peers, masks, near_ref, far_ref, *refs):
    count = 1 + (peers + 1) + peers + 2 + 5
    sources, results = refs[:count], refs[count : count + 4]
    scratch = refs[count + 4 :]
    held, outs, sems, out_sems = scratch[:count], scratch[count : count + 4], scratch[-2], scratch[-1]
    copies = fetch(sources, held, sems)
    ends = {"far": (0, 1), "near": (1, 2 + 2 * peers)}
    ends["local"] = (ends["near"][1], ends["near"][1] + 2)
    ends["base"] = (ends["local"][1], count)
    waited = set()

    def ready(what):
        if what not in waited:
            waited.add(what)
            for copy in copies[slice(*ends[what])]:
                copy.wait()

    sent = []

    def done(which, cols):
        copy = pltpu.make_async_copy(
            outs[which].at[:, cols], results[which].at[:, cols], out_sems.at[which, cols.start // GW]
        )
        copy.start()
        sent.append(copy)

    far, near, local = (held[slice(*ends[what])] for what in ("far", "near", "local"))
    base = held[slice(*ends["base"])]
    groups = results[0].shape[1] // GW
    lockstep(
        final_group(
            peers, masks, group, near_ref, far_ref, near[: peers + 1], near[peers + 1 :], far[0], *local,
            base[:4], base[4], outs, ready, done,
        )
        for group in range(groups)
    )
    for copy in sent:
        copy.wait()


def smem():
    return pl.BlockSpec(memory_space=pltpu.SMEM)


def whole_block(rows, width):
    return pl.BlockSpec((rows, width), lambda g: (0, 0))


def group_block(rows):
    return pl.BlockSpec((rows, GW), lambda g: (0, g))


def params(limit=VMEM_LIMIT):
    return pltpu.CompilerParams(vmem_limit_bytes=limit * 1024 * 1024)


def shards(queries, key_vectors, value_vectors, out_grad, near_offsets, far_offsets):
    length, width = queries.shape
    row_count = lax.axis_size("row")
    col_count = lax.axis_size("col")
    peers = SEG2 // length
    n, f = length // R2, length // R3
    groups = width // GW
    pairs = width // PW

    def like(rows):
        return jax.ShapeDtypeStruct((rows, width), BF)

    def swap(x, axis, mask):
        size = lax.axis_size(axis)
        return lax.ppermute(x, axis, [(i, i ^ mask) for i in range(size)])

    picked = pl.pallas_call(
        functools.partial(pick_kernel, peers),
        grid=(groups,),
        in_specs=[smem(), smem()] + [group_block(length)] * 4,
        out_specs=[group_block(2 * n)] * 2 + [group_block(FM)] + [group_block(2 * n)] * (peers - 1),
        out_shape=[like(2 * n)] * 2 + [like(FM)] + [like(2 * n)] * (peers - 1),
        compiler_params=params(PICK_LIMIT),
        name="pick",
    )(near_offsets, far_offsets, queries, key_vectors, value_vectors, out_grad)
    kv, qg, fr, msgs = picked[0], picked[1], picked[2], picked[3:]
    got = [swap(msgs[s - 1], "row", s) for s in range(1, peers)]

    ops = 2 * H * length * length * HD
    stats = jax.ShapeDtypeStruct((pairs * 8, length), F32)
    per = 2

    def pair_block(first):
        return pl.BlockSpec((length, per * PW), lambda p: (0, first + p))

    def stat_block(first):
        return pl.BlockSpec((per * 8, length), lambda p: (first + p, 0))

    att1, st1 = pl.pallas_call(
        functools.partial(forward_kernel, 256, 2),
        grid=(pairs // per,),
        in_specs=[pair_block(0)] * 4,
        out_specs=[pair_block(0), stat_block(0)],
        out_shape=[like(length), stats],
        compiler_params=params(),
        cost_estimate=pl.CostEstimate(flops=2 * ops * 4, bytes_accessed=6 * length * width * 2, transcendentals=0),
        name="forward",
    )(queries, key_vectors, value_vectors, out_grad)

    mine, st12, near_out = pl.pallas_call(
        functools.partial(merge_kernel, peers),
        grid=(1,),
        in_specs=[smem(), smem()]
        + [whole_block(2 * n, width)] * (peers + 1)
        + [whole_block(*stats.shape), whole_block(length, width), whole_block(FM, width)],
        out_specs=[whole_block(n + FM, width), whole_block(*stats.shape), whole_block(n, width)],
        out_shape=[like(n + FM), stats, like(n)],
        compiler_params=params(),
        name="merge",
    )(near_offsets, far_offsets, kv, qg, *got, st1, att1, fr)
    theirs = [swap(mine, "row", s) for s in range(1, peers)]

    grads = []
    pieces = pairs // per

    def backward(piece, grads):
        any_spec = pl.BlockSpec(memory_space=pl.ANY)
        aliased = len(grads)
        return pl.pallas_call(
            functools.partial(backward_kernel, 256, 1, aliased),
            grid=(1,),
            in_specs=[pair_block(piece)] * 4 + [stat_block(piece)] + [any_spec] * aliased,
            out_specs=[pair_block(piece)] * 3,
            out_shape=[like(length)] * 3,
            input_output_aliases={5 + i: i for i in range(aliased)},
            compiler_params=params(),
            cost_estimate=pl.CostEstimate(
                flops=5 * ops * 4 // pieces, bytes_accessed=8 * length * width * 2 // pieces, transcendentals=0
            ),
            name="backward",
        )(queries, key_vectors, value_vectors, out_grad, st12, *grads)

    grads = backward(0, grads)
    grads, theirs = lax.optimization_barrier((grads, theirs))
    at = 1
    far_all = jnp.concatenate([x[n:] for x in (mine, *theirs)], axis=0)
    masks = []
    for axis, size, least in (("row", row_count, peers), ("col", col_count, 1)):
        mask = size // 2
        while mask >= least:
            other = swap(far_all, axis, mask)
            if at < pieces:
                grads = backward(at, grads)
                grads, other = lax.optimization_barrier((grads, other))
                at += 1
            far_all = jnp.concatenate([far_all, other], axis=0)
            masks.append(mask if axis == "row" else mask * row_count)
            mask //= 2
    while at < pieces:
        grads = backward(at, grads)
        at += 1

    operands = (far_all, kv, qg, *got, mine, *theirs, key_vectors, value_vectors, att1, *grads, near_out)
    return pl.pallas_call(
        functools.partial(final_kernel, peers, tuple(masks)),
        in_specs=[smem(), smem()] + [pl.BlockSpec(memory_space=pl.ANY)] * len(operands),
        out_specs=[pl.BlockSpec(memory_space=pl.ANY)] * 4,
        out_shape=[like(length)] * 4,
        scratch_shapes=[pltpu.VMEM(x.shape, x.dtype) for x in operands]
        + [pltpu.VMEM((length, width), BF)] * 4
        + [pltpu.SemaphoreType.DMA((len(operands),)), pltpu.SemaphoreType.DMA((4, groups))],
        compiler_params=params(),
        name="final",
    )(near_offsets, far_offsets, *operands)


def solution(mesh):
    placed = (
        P(("col", "row"), None),
        P(("col", "row"), None),
        P(("col", "row"), None),
        P(("col", "row"), None),
        P(),
        P(),
    )
    return jax.shard_map(
        shards,
        mesh=mesh,
        in_specs=placed,
        out_specs=(
            P(("col", "row"), None),
            P(("col", "row"), None),
            P(("col", "row"), None),
            P(("col", "row"), None),
        ),
        check_vma=False,
    )
```

time: 68.7 us -> 49.5 us (0.72)
  Pallas kernels: 40.8 us -> 27.3 us
  local copies, waits for them, and re-layouts: 6.84 us -> 2.42 us
  waiting for transfers between devices: 7.23 us -> 5.87 us
    pallas_call x6, Pallas kernels: 38.5 us -> 23 us  [the longest x1 9.62 us: shards(): pl.pallas_call(functools.partial(final_kernel, peers, tuple(masks)), in_s...]
    unnamed x29 -> x27, local copies, waits for them, and re-layouts: 6.78 us -> 2.36 us
    pallas_call x1, Pallas kernels: 2.32 us -> 4.28 us  [shards(): pl.pallas_call(functools.partial(pick_kernel, peers), grid=(groups,), in_...]
    ppermute x9, waiting for transfers between devices: 7.23 us -> 5.87 us  [swap(): return lax.ppermute(x, axis, [(i, i ^ mask) for i in range(size)])]
  transfers between devices with their start and end apart: 9 -> 9, of which waited for: 2 -> 5; matrix products, arithmetic and copies ran while one was open for 0% -> 0% of each run, Pallas kernels for 35% -> 24%
where the time goes in v2:
time: 49.5 us; the launch traced here: 49.2 us
  Pallas kernels  27.3 us (55%)
  starting transfers between devices  12.6 us (25%)
  waiting for transfers between devices  5.87 us (12%)
  local copies, waits for them, and re-layouts  2.42 us (5%)
  between operations  1 us (2%)
    ppermute x9, starting transfers between devices, swap(): return lax.ppermute(x, axis, [(i, i ^ mask) for i in range(size)])  12.6 us
    pallas_call x1, Pallas kernels, shards(): pl.pallas_call(functools.partial(final_kernel, peers, tuple(masks)), in_s...  9.62 us
    pallas_call x3, Pallas kernels, backward(): pl.pallas_call(functools.partial(backward_kernel, 256, 1, aliased), grid=...  6.95 us
    ppermute x9, waiting for transfers between devices, swap(): return lax.ppermute(x, axis, [(i, i ^ mask) for i in range(size)])  5.87 us
    pallas_call x1, Pallas kernels, shards(): pl.pallas_call(functools.partial(forward_kernel, 256, 2), grid=(pairs //...  4.65 us
    pallas_call x1, Pallas kernels, shards(): pl.pallas_call(functools.partial(pick_kernel, peers), grid=(groups,), in_...  4.28 us
    unnamed x27, local copies, waits for them, and re-layouts  2.36 us
    pallas_call x1, Pallas kernels, shards(): pl.pallas_call(functools.partial(merge_kernel, peers), grid=(1,), in_spec...  1.82 us
  transfers between devices with their start and end apart: 9, of which 5 were waited for; matrix products, arithmetic and copies ran while one was open for 0% of the time, Pallas kernels for 24%

profile of v2, /device:TPU:0, one launch (start us, length us, event | category | flops | bytes accessed | tf_op | source)
XLA Modules:
  0.0 49.2 jit_solution(8608208631925238592)
XLA Ops:
  0.7 4.3 %pick.1 = (bf16[64,768]{1,0:T(8,128)(2,1)}, bf16[64,768]{1,0:T(8,128)(2,1)}, bf16[16,768]{1,0:T(8,128)(2,1)}, bf16[64,768]{1,0:T(8,128)(2,1)}, bf16[64,768]{1,0:T(8,128)(2,1)}, /*index=5*/bf16[64,768]{1,0:T(8,128)(2,1)}) custom-call(s32[12]{0:T(128)} %near_ref.5, s32[12]{0:T(128)} %far_ref.5, bf16[512,768]{1,0:T(8,128)(2,1)} %q_ref.9, ...), custom_call_target="tpu_custom_call" | custom-call | tf_op jit(solution)/shard_map/pick/pallas_call | solution.py:607
  4.9 3.0 %collective-permute-start = (bf16[64,768]{1,0:T(8,128)(2,1)}, bf16[64,768]{1,0:T(8,128)(2,1)S(1)}, u32[]{:S(2)}, u32[]{:S(2)}) collective-permute-start(bf16[64,768]{1,0:T(8,128)(2,1)} %get-tuple-element.40), channel_id=1, source_target_pairs={{0,8},{8,0},{16,24},{24,16},{1,9},{9,1},{17,25},{25,17},{2,10},{10... | collective-permute-start | bytes 294920 | tf_op jit(solution)/shard_map/ppermute | solution.py:605
  7.9 1.5 %collective-permute-start.1 = (bf16[64,768]{1,0:T(8,128)(2,1)}, bf16[64,768]{1,0:T(8,128)(2,1)S(1)}, u32[]{:S(2)}, u32[]{:S(2)}) collective-permute-start(bf16[64,768]{1,0:T(8,128)(2,1)} %get-tuple-element.41), channel_id=1, source_target_pairs={{0,16},{8,24},{16,0},{24,8},{1,17},{9,25},{17,1},{25,9},{2,18},{10... | collective-permute-start | bytes 294920 | tf_op jit(solution)/shard_map/ppermute | solution.py:605
  9.4 0.0 collective-permute-start.2
  9.5 1.1 %copy-done.2 = bf16[512,768]{1,0:T(8,128)(2,1)S(1)} copy-done((bf16[512,768]{1,0:T(8,128)(2,1)S(1)}, bf16[512,768]{1,0:T(8,128)(2,1)}, u32[]{:S(2)}) %copy-start.2) | copy-done | bytes 786456
  10.6 1.1 %copy-done.4 = bf16[512,768]{1,0:T(8,128)(2,1)S(1)} copy-done((bf16[512,768]{1,0:T(8,128)(2,1)S(1)}, bf16[512,768]{1,0:T(8,128)(2,1)}, u32[]{:S(2)}) %copy-start.4) | copy-done | bytes 786456
  11.8 0.0 copy-start.10
  11.8 4.6 %forward.1 = (bf16[512,768]{1,0:T(8,128)(2,1)S(1)}, f32[48,512]{1,0:T(8,128)S(1)}) custom-call(bf16[512,768]{1,0:T(8,128)(2,1)S(1)} %copy-done.2, bf16[512,768]{1,0:T(8,128)(2,1)S(1)} %copy-done, bf16[512,768]{1,0:T(8,128)(2,1)S(1)} %copy-done.1, bf16[512,768]{1,0:T(8,128)(2,1)S(1)} %copy-done.4), custom_call_target="tpu_custom_call" | custom-call | flops 3221225472 | bytes 4718592 | tf_op jit(solution)/shard_map/forward/pallas_call | solution.py:629
  16.5 1.8 %merge.1 = (bf16[48,768]{1,0:T(8,128)(2,1)S(1)}, f32[48,512]{1,0:T(8,128)S(1)}, bf16[32,768]{1,0:T(8,128)(2,1)S(1)}) custom-call(s32[12]{0:T(128)S(1)} %copy-done.9, s32[12]{0:T(128)S(1)} %copy-done.10, bf16[64,768]{1,0:T(8,128)(2,1)S(1)} %copy-done.6, bf16[64,768]{1,0:T(8,128)(2,1)S(1)} %copy-done.7, ...), custom_call_target="tpu_custom_call" | custom-call | tf_op jit(solution)/shard_map/merge/pallas_call | solution.py:640
  18.4 2.9 %collective-permute-start.5 = (bf16[48,768]{1,0:T(8,128)(2,1)S(1)}, bf16[48,768]{1,0:T(8,128)(2,1)S(1)}, u32[]{:S(2)}, u32[]{:S(2)}) collective-permute-start(bf16[48,768]{1,0:T(8,128)(2,1)S(1)} %get-tuple-element.46.refs_6_), channel_id=1, source_target_pairs={{0,24},{8,16},{16,8},{24,0},{1,25},{9,17},{17,9},{25,1},{2,26},{10... | collective-permute-start | bytes 221192 | tf_op jit(solution)/shard_map/ppermute | solution.py:605
  21.3 0.5 %collective-permute-start.4 = (bf16[48,768]{1,0:T(8,128)(2,1)S(1)}, bf16[48,768]{1,0:T(8,128)(2,1)S(1)}, u32[]{:S(2)}, u32[]{:S(2)}) collective-permute-start(bf16[48,768]{1,0:T(8,128)(2,1)S(1)} %get-tuple-element.46.refs_6_), channel_id=1, source_target_pairs={{0,16},{8,24},{16,0},{24,8},{1,17},{9,25},{17,1},{25,9},{2,18},{10... | collective-permute-start | bytes 221192 | tf_op jit(solution)/shard_map/ppermute | solution.py:605
  21.8 0.1 collective-permute-start.3
  21.9 2.3 %backward.3 = (bf16[512,768]{1,0:T(8,128)(2,1)S(1)}, bf16[512,768]{1,0:T(8,128)(2,1)S(1)}, bf16[512,768]{1,0:T(8,128)(2,1)S(1)}) custom-call(bf16[512,768]{1,0:T(8,128)(2,1)S(1)} %copy-done.3, bf16[512,768]{1,0:T(8,128)(2,1)S(1)} %copy-done, bf16[512,768]{1,0:T(8,128)(2,1)S(1)} %copy-done.1, bf16[512,768]{1,0:T(8,128)(2,1)S(1)} %copy-done.5, ...), custom_call_target="tpu_custom_call" | custom-call | flops 2684354560 | bytes 2097152 | tf_op jit(solution)/shard_map/backward/pallas_call | solution.py:659
  24.3 1.3 %collective-permute-done.4.refs_8_ = bf16[48,768]{1,0:T(8,128)(2,1)S(1)} collective-permute-done((bf16[48,768]{1,0:T(8,128)(2,1)S(1)}, bf16[48,768]{1,0:T(8,128)(2,1)S(1)}, u32[]{:S(2)}, u32[]{:S(2)}) %collective-permute-start.4) | collective-permute-done | bytes 73760 | tf_op jit(solution)/shard_map/ppermute | solution.py:605
  25.6 0.5 %collective-permute-done.3.refs_7_ = bf16[48,768]{1,0:T(8,128)(2,1)S(1)} collective-permute-done((bf16[48,768]{1,0:T(8,128)(2,1)S(1)}, bf16[48,768]{1,0:T(8,128)(2,1)S(1)}, u32[]{:S(2)}, u32[]{:S(2)}) %collective-permute-start.3) | collective-permute-done | bytes 73760 | tf_op jit(solution)/shard_map/ppermute | solution.py:605
  26.2 2.7 %collective-permute-start.6 = (bf16[64,768]{1,0:T(8,128)(2,1)S(1)}, bf16[64,768]{1,0:T(8,128)(2,1)S(1)}, u32[]{:S(2)}, u32[]{:S(2)}) collective-permute-start(bf16[64,768]{1,0:T(8,128)(2,1)S(1)} %pad_maximum_fusion), channel_id=1, source_target_pairs={{0,4},{1,5},{2,6},{3,7},{4,0},{5,1},{6,2},{7,3},{8,12},{9,13},{10,... | collective-permute-start | bytes 294920 | tf_op jit(solution)/shard_map/ppermute | solution.py:605
  28.9 2.3 %backward.4 = (bf16[512,768]{1,0:T(8,128)(2,1)S(1)}, bf16[512,768]{1,0:T(8,128)(2,1)S(1)}, bf16[512,768]{1,0:T(8,128)(2,1)S(1)}) custom-call(bf16[512,768]{1,0:T(8,128)(2,1)S(1)} %copy-done.3, bf16[512,768]{1,0:T(8,128)(2,1)S(1)} %copy-done, bf16[512,768]{1,0:T(8,128)(2,1)S(1)} %copy-done.1, ...), custom_call_target="tpu_custom_call", output_to_operand_aliasing={{0}: (5, {}), {1}: (6, {}), {2}: (7, {})} | custom-call | flops 2684354560 | bytes 2097152 | tf_op jit(solution)/shard_map/backward/pallas_call | solution.py:659
  31.2 0.6 %collective-permute-done.6 = bf16[64,768]{1,0:T(8,128)(2,1)S(1)} collective-permute-done((bf16[64,768]{1,0:T(8,128)(2,1)S(1)}, bf16[64,768]{1,0:T(8,128)(2,1)S(1)}, u32[]{:S(2)}, u32[]{:S(2)}) %collective-permute-start.6) | collective-permute-done | bytes 98336 | tf_op jit(solution)/shard_map/ppermute | solution.py:605
  31.9 1.8 %collective-permute-start.7 = (bf16[128,768]{1,0:T(8,128)(2,1)S(1)}, bf16[128,768]{1,0:T(8,128)(2,1)S(1)}, u32[]{:S(2)}, u32[]{:S(2)}) collective-permute-start(bf16[128,768]{1,0:T(8,128)(2,1)S(1)} %get-tuple-element.76), channel_id=1, source_target_pairs={{0,2},{1,3},{2,0},{3,1},{4,6},{5,7},{6,4},{7,5},{8,10},{9,11},{10,... | collective-permute-start | bytes 589832 | tf_op jit(solution)/shard_map/ppermute | solution.py:605
  33.6 2.3 %backward.5 = (bf16[512,768]{1,0:T(8,128)(2,1)S(1)}, bf16[512,768]{1,0:T(8,128)(2,1)S(1)}, bf16[512,768]{1,0:T(8,128)(2,1)S(1)}) custom-call(bf16[512,768]{1,0:T(8,128)(2,1)S(1)} %copy-done.3, bf16[512,768]{1,0:T(8,128)(2,1)S(1)} %copy-done, bf16[512,768]{1,0:T(8,128)(2,1)S(1)} %copy-done.1, ...), custom_call_target="tpu_custom_call", output_to_operand_aliasing={{0}: (5, {}), {1}: (6, {}), {2}: (7, {})} | custom-call | flops 2684354560 | bytes 2097152 | tf_op jit(solution)/shard_map/backward/pallas_call | solution.py:659
  36.0 1.6 %collective-permute-done.7 = bf16[128,768]{1,0:T(8,128)(2,1)S(1)} collective-permute-done((bf16[128,768]{1,0:T(8,128)(2,1)S(1)}, bf16[128,768]{1,0:T(8,128)(2,1)S(1)}, u32[]{:S(2)}, u32[]{:S(2)}) %collective-permute-start.7) | collective-permute-done | bytes 196640 | tf_op jit(solution)/shard_map/ppermute | solution.py:605
  37.6 0.1 collective-permute-start.8
  37.7 1.7 %collective-permute-done.8 = bf16[256,768]{1,0:T(8,128)(2,1)S(1)} collective-permute-done((bf16[256,768]{1,0:T(8,128)(2,1)S(1)}, bf16[256,768]{1,0:T(8,128)(2,1)S(1)}, u32[]{:S(2)}, u32[]{:S(2)}) %collective-permute-start.8) | collective-permute-done | bytes 393248 | tf_op jit(solution)/shard_map/ppermute | solution.py:605
  39.4 9.6 %final.1 = (bf16[512,768]{1,0:T(8,128)(2,1)}, bf16[512,768]{1,0:T(8,128)(2,1)}, bf16[512,768]{1,0:T(8,128)(2,1)}, bf16[512,768]{1,0:T(8,128)(2,1)}) custom-call(s32[12]{0:T(128)S(1)} %copy-done.9, s32[12]{0:T(128)S(1)} %copy-done.10, bf16[512,768]{1,0:T(8,128)(2,1)S(1)} %constant_dynamic-update-slice_fusion.11.refs_0_, bf16[64,768]{1,0:T(8,128)(2,1)S(1)} %copy-done.6, ...), custom_call_target="tpu_custom_call" | custom-call | tf_op jit(solution)/shard_map/final/pallas_call | solution.py:694
  (31 shorter events, 0.2 us)
Async XLA Ops:
  0.6 8.9 %copy-start.1 = (bf16[512,768]{1,0:T(8,128)(2,1)S(1)}, bf16[512,768]{1,0:T(8,128)(2,1)}, u32[]{:S(2)}) copy-start(bf16[512,768]{1,0:T(8,128)(2,1)} %refs_11_.1) | copy-start | bytes 2359300
  0.6 8.8 %copy-start = (bf16[512,768]{1,0:T(8,128)(2,1)S(1)}, bf16[512,768]{1,0:T(8,128)(2,1)}, u32[]{:S(2)}) copy-start(bf16[512,768]{1,0:T(8,128)(2,1)} %refs_10_.1) | copy-start | bytes 2359300
  4.9 11.5 %collective-permute-start = (bf16[64,768]{1,0:T(8,128)(2,1)}, bf16[64,768]{1,0:T(8,128)(2,1)S(1)}, u32[]{:S(2)}, u32[]{:S(2)}) collective-permute-start(bf16[64,768]{1,0:T(8,128)(2,1)} %get-tuple-element.40), channel_id=1, source_target_pairs={{0,8},{8,0},{16,24},{24,16},{1,9},{9,1},{17,25},{25,17},{2,10},{10... | collective-permute-start | bytes 294920 | tf_op jit(solution)/shard_map/ppermute | solution.py:605
  7.9 8.5 %collective-permute-start.1 = (bf16[64,768]{1,0:T(8,128)(2,1)}, bf16[64,768]{1,0:T(8,128)(2,1)S(1)}, u32[]{:S(2)}, u32[]{:S(2)}) collective-permute-start(bf16[64,768]{1,0:T(8,128)(2,1)} %get-tuple-element.41), channel_id=1, source_target_pairs={{0,16},{8,24},{16,0},{24,8},{1,17},{9,25},{17,1},{25,9},{2,18},{10... | collective-permute-start | bytes 294920 | tf_op jit(solution)/shard_map/ppermute | solution.py:605
  9.4 7.0 %collective-permute-start.2 = (bf16[64,768]{1,0:T(8,128)(2,1)}, bf16[64,768]{1,0:T(8,128)(2,1)S(1)}, u32[]{:S(2)}, u32[]{:S(2)}) collective-permute-start(bf16[64,768]{1,0:T(8,128)(2,1)} %get-tuple-element.42), channel_id=1, source_target_pairs={{0,24},{8,16},{16,8},{24,0},{1,25},{9,17},{17,9},{25,1},{2,26},{10... | collective-permute-start | bytes 294920 | tf_op jit(solution)/shard_map/ppermute | solution.py:605
  9.5 1.1 %copy-start.2 = (bf16[512,768]{1,0:T(8,128)(2,1)S(1)}, bf16[512,768]{1,0:T(8,128)(2,1)}, u32[]{:S(2)}) copy-start(bf16[512,768]{1,0:T(8,128)(2,1)} %q_ref.9) | copy-start | bytes 2359300
  10.6 1.1 %copy-start.4 = (bf16[512,768]{1,0:T(8,128)(2,1)S(1)}, bf16[512,768]{1,0:T(8,128)(2,1)}, u32[]{:S(2)}) copy-start(bf16[512,768]{1,0:T(8,128)(2,1)} %g_ref.9) | copy-start | bytes 2359300
  11.8 4.7 %copy-start.6 = (bf16[64,768]{1,0:T(8,128)(2,1)S(1)}, bf16[64,768]{1,0:T(8,128)(2,1)}, u32[]{:S(2)}) copy-start(bf16[64,768]{1,0:T(8,128)(2,1)} %get-tuple-element.38.kv_ref.refs_1_) | copy-start | bytes 294916
  11.8 4.7 %copy-start.7 = (bf16[64,768]{1,0:T(8,128)(2,1)S(1)}, bf16[64,768]{1,0:T(8,128)(2,1)}, u32[]{:S(2)}) copy-start(bf16[64,768]{1,0:T(8,128)(2,1)} %get-tuple-element.39.qg_ref.refs_2_) | copy-start | bytes 294916
  11.8 4.8 %copy-start.8 = (bf16[16,768]{1,0:T(8,128)(2,1)S(1)}, bf16[16,768]{1,0:T(8,128)(2,1)}, u32[]{:S(2)}) copy-start(bf16[16,768]{1,0:T(8,128)(2,1)} %get-tuple-element.45.rest_5_) | copy-start | bytes 73732
  11.8 4.8 %copy-start.9 = (s32[12]{0:T(128)S(1)}, s32[12]{0:T(128)}, u32[]{:S(2)}) copy-start(s32[12]{0:T(128)} %near_ref.5) | copy-start | bytes 148
  11.8 4.8 %copy-start.10 = (s32[12]{0:T(128)S(1)}, s32[12]{0:T(128)}, u32[]{:S(2)}) copy-start(s32[12]{0:T(128)} %far_ref.5) | copy-start | bytes 148
  11.8 10.1 %copy-start.5 = (bf16[512,768]{1,0:T(8,128)(2,1)S(1)}, bf16[512,768]{1,0:T(8,128)(2,1)}, u32[]{:S(2)}) copy-start(bf16[512,768]{1,0:T(8,128)(2,1)} %g_ref.9) | copy-start | bytes 2359300
  16.4 5.5 %copy-start.3 = (bf16[512,768]{1,0:T(8,128)(2,1)S(1)}, bf16[512,768]{1,0:T(8,128)(2,1)}, u32[]{:S(2)}) copy-start(bf16[512,768]{1,0:T(8,128)(2,1)} %q_ref.9) | copy-start | bytes 2359300
  18.4 5.9 %collective-permute-start.5 = (bf16[48,768]{1,0:T(8,128)(2,1)S(1)}, bf16[48,768]{1,0:T(8,128)(2,1)S(1)}, u32[]{:S(2)}, u32[]{:S(2)}) collective-permute-start(bf16[48,768]{1,0:T(8,128)(2,1)S(1)} %get-tuple-element.46.refs_6_), channel_id=1, source_target_pairs={{0,24},{8,16},{16,8},{24,0},{1,25},{9,17},{17,9},{25,1},{2,26},{10... | collective-permute-start | bytes 221192 | tf_op jit(solution)/shard_map/ppermute | solution.py:605
  21.3 4.4 %collective-permute-start.4 = (bf16[48,768]{1,0:T(8,128)(2,1)S(1)}, bf16[48,768]{1,0:T(8,128)(2,1)S(1)}, u32[]{:S(2)}, u32[]{:S(2)}) collective-permute-start(bf16[48,768]{1,0:T(8,128)(2,1)S(1)} %get-tuple-element.46.refs_6_), channel_id=1, source_target_pairs={{0,16},{8,24},{16,0},{24,8},{1,17},{9,25},{17,1},{25,9},{2,18},{10... | collective-permute-start | bytes 221192 | tf_op jit(solution)/shard_map/ppermute | solution.py:605
  21.8 4.4 %collective-permute-start.3 = (bf16[48,768]{1,0:T(8,128)(2,1)S(1)}, bf16[48,768]{1,0:T(8,128)(2,1)S(1)}, u32[]{:S(2)}, u32[]{:S(2)}) collective-permute-start(bf16[48,768]{1,0:T(8,128)(2,1)S(1)} %get-tuple-element.46.refs_6_), channel_id=1, source_target_pairs={{0,8},{8,0},{16,24},{24,16},{1,9},{9,1},{17,25},{25,17},{2,10},{10... | collective-permute-start | bytes 221192 | tf_op jit(solution)/shard_map/ppermute | solution.py:605
  26.2 5.6 %collective-permute-start.6 = (bf16[64,768]{1,0:T(8,128)(2,1)S(1)}, bf16[64,768]{1,0:T(8,128)(2,1)S(1)}, u32[]{:S(2)}, u32[]{:S(2)}) collective-permute-start(bf16[64,768]{1,0:T(8,128)(2,1)S(1)} %pad_maximum_fusion), channel_id=1, source_target_pairs={{0,4},{1,5},{2,6},{3,7},{4,0},{5,1},{6,2},{7,3},{8,12},{9,13},{10,... | collective-permute-start | bytes 294920 | tf_op jit(solution)/shard_map/ppermute | solution.py:605
  31.9 5.7 %collective-permute-start.7 = (bf16[128,768]{1,0:T(8,128)(2,1)S(1)}, bf16[128,768]{1,0:T(8,128)(2,1)S(1)}, u32[]{:S(2)}, u32[]{:S(2)}) collective-permute-start(bf16[128,768]{1,0:T(8,128)(2,1)S(1)} %get-tuple-element.76), channel_id=1, source_target_pairs={{0,2},{1,3},{2,0},{3,1},{4,6},{5,7},{6,4},{7,5},{8,10},{9,11},{10,... | collective-permute-start | bytes 589832 | tf_op jit(solution)/shard_map/ppermute | solution.py:605
  37.6 1.8 %collective-permute-start.8 = (bf16[256,768]{1,0:T(8,128)(2,1)S(1)}, bf16[256,768]{1,0:T(8,128)(2,1)S(1)}, u32[]{:S(2)}, u32[]{:S(2)}) collective-permute-start(bf16[256,768]{1,0:T(8,128)(2,1)S(1)} %get-tuple-element.72), channel_id=1, source_target_pairs={{0,1},{1,0},{2,3},{3,2},{4,5},{5,4},{6,7},{7,6},{8,9},{9,8},{10,11... | collective-permute-start | bytes 1179656 | tf_op jit(solution)/shard_map/ppermute | solution.py:605

commit v3 on v2

--- a/solution.py
+++ b/solution.py
@@ -23,7 +23,7 @@
 F32 = jnp.float32
 BF = jnp.bfloat16
 VMEM_LIMIT = 40
-PICK_LIMIT = 62
+PICK_LIMIT = 58
 
 
 def iota(shape, axis):
@@ -258,16 +258,28 @@
     return slice(group * GW, (group + 1) * GW)
 
 
-def fetch(sources, targets, sems):
-    copies = []
-    for i, (source, target) in enumerate(zip(sources, targets)):
-        copy = pltpu.make_async_copy(source, target, sems.at[i])
-        copy.start()
-        copies.append(copy)
-    return copies
-
-
-def merge_group(peers, group, near_ref, far_ref, kv_ref, qg_ref, got, st_ref, att_ref, fr_ref, out_ref, st_out, near_out):
+def pack_lanes(group):
+    l, m = iota((GW, 128), 0), iota((GW, 128), 1)
+    return onehot((l % HD < 6) & (m == (group * GH + l // HD) * 6 + l % HD))
+
+
+def unpack_lanes(group):
+    l, m = iota((128, GW), 1), iota((128, GW), 0)
+    return onehot((l % HD < 6) & (m == (group * GH + l // HD) * 6 + l % HD))
+
+
+def unpack_rows(peers, stride, n, f, fa_ref):
+    per = fa_ref.shape[1] // 128
+    rows = peers * stride * FM
+    r, c = iota((peers * n, rows), 0), iota((peers * n, rows), 1)
+    at_row = c == r // n * (stride * FM) + 5 * f + r % n // per
+    out = jnp.zeros((peers * n, 128), F32)
+    for at in range(per):
+        out += nn(onehot(at_row & (r % n % per == at)), fa_ref[:rows, at * 128 : (at + 1) * 128])
+    return out.astype(BF)
+
+
+def merge_group(peers, group, near_ref, far_ref, kv_ref, qg_ref, got, st_ref, att_ref, fr_ref, out_ref, st_out, near_out, blocks, packs):
     cols = group_columns(group)
     srows = slice(group * SR, (group + 1) * SR)
     length = att_ref.shape[0]
@@ -308,7 +320,7 @@
     dot12 = spread_sum(qg_ref[n:, cols].astype(F32) * out12, GW)
     yield
     aux12 = pack_aux(log12, dot12).astype(BF)
-    out_ref[:n, cols] = aux12
+    packs.append(nn(aux12, pack_lanes(group)))
     head, what = stat_row((SR, GW), 0)
     lane = iota((SR, GW), 1)
     compact = nt(onehot((lane // HD == head) & (lane % HD // 3 == what)), aux12)
@@ -324,13 +336,26 @@
     head, what = stat_row((3 * SR, GW), 0)
     lane, piece = iota((3 * SR, GW), 1), iota((3 * SR, GW), 0) // SR
     far_aux = nn(far_aux.astype(BF), onehot((lane // HD == head) & (lane % HD == what * 3 + piece)))
-    out_ref[n:, cols] = (fr_ref[:, cols].astype(F32) + far_aux).astype(BF)
+    blocks[group] = fr_ref[:, cols].astype(F32) + far_aux
 
 
 def merge_kernel(peers, near_ref, far_ref, kv_ref, qg_ref, *rest):
     got, rest = rest[: peers - 1], rest[peers - 1 :]
     groups = kv_ref.shape[1] // GW
-    lockstep(merge_group(peers, group, near_ref, far_ref, kv_ref, qg_ref, got, *rest) for group in range(groups))
+    out_ref = rest[3]
+    blocks, packs = {}, []
+    lockstep(
+        merge_group(peers, group, near_ref, far_ref, kv_ref, qg_ref, got, *rest, blocks, packs)
+        for group in range(groups)
+    )
+    packed = sum(packs[1:], packs[0]).astype(BF)
+    n, length = packed.shape[0], rest[1].shape[0]
+    per = out_ref.shape[1] // 128
+    r, c = iota((FM, n), 0) - 5 * (length // R3), iota((FM, n), 1)
+    for at in range(per):
+        block = blocks[at * 128 // GW][:, at * 128 % GW :][:, :128]
+        rows = nn(onehot((c // per == r) & (c % per == at)), packed)
+        out_ref[:, at * 128 : (at + 1) * 128] = (block + rows).astype(BF)
 
 
 def backward_kernel(strip, skew, aliased, q_ref, k_ref, v_ref, g_ref, st_ref, *rest):
@@ -380,17 +405,17 @@
     staged(units, (score, soften, mix), skew)
 
 
-def far_seq(index, f, peers, masks, own):
+def far_seq(index, f, digits, own):
     slot = index // f
-    seq = own ^ (slot % peers)
-    bits = slot // peers
-    for at, mask in enumerate(masks):
-        seq = seq ^ (((bits >> at) & 1) * mask)
+    seq = own
+    for radix, unit in digits:
+        seq = seq ^ (slot % radix * unit)
+        slot = slot // radix
     return seq * f + index % f
 
 
 def final_group(
-    peers, masks, group, near_ref, far_ref, got, auxs, fa_ref, k_ref, v_ref, base, near_out, outs, ready, done
+    peers, stride, digits, group, near_ref, far_ref, got, packed, fa_ref, k_ref, v_ref, base, near_out, outs, done
 ):
     kv_ref, qg_ref, got = got[0], got[1], got[2:]
     cols = group_columns(group)
@@ -403,7 +428,6 @@
     seq = lax.axis_index("col") * lax.axis_size("row") + row_here
     scale = jnp.asarray(SCALE, BF)
 
-    ready("far")
     r, c = iota((5 * F, blocks * FM), 0), iota((5 * F, blocks * FM), 1)
     i, at = r // F, r % F
     sel = onehot(c == at // f * FM + i * f + at % f)
@@ -416,20 +440,20 @@
     dp = nt(gx, fv)
     log12, dot12 = piece_column(ax, 0), piece_column(ax, 1)
     yield
-    ready("near")
     heads = [kv_ref, *got]
     keys = jnp.concatenate([x[:n, cols] for x in heads], axis=0)
     values = jnp.concatenate([x[n:, cols] for x in heads], axis=0)
     heads = [qg_ref, *got]
     queries = jnp.concatenate([x[:n, cols] for x in heads], axis=0) * scale
     grads = jnp.concatenate([x[n:, cols] for x in heads], axis=0)
+    naux = nn(packed(), unpack_lanes(group))
     near_s = nt(expand(queries[:n]), keys)
     near_dp = nt(expand(grads[:n]), values)
     near_s2 = nt(expand(keys[:n]), queries)
     near_dp2 = nt(expand(values[:n]), grads)
     yield
-    place_q = far_seq(iota((GH * F, 1), 0) % F, f, peers, masks, seq)
-    place_k = far_seq(iota((1, F), 1), f, peers, masks, seq)
+    place_q = far_seq(iota((GH * F, 1), 0) % F, f, digits, seq)
+    place_k = far_seq(iota((1, F), 1), f, digits, seq)
     s = jnp.where(place_k <= place_q, s, NEG)
     top = jnp.max(s, axis=1, keepdims=True)
     yield
@@ -458,7 +482,6 @@
     def own_rows(x):
         return jnp.concatenate([x[h * F : h * F + FM] for h in range(GH)], axis=0)
 
-    ready("local")
     qx, gx, log_own, dot_own = own_rows(qx), own_rows(gx), own_rows(log_all), own_rows(dot_all)
     k, v = k_ref[:, cols], v_ref[:, cols]
     s = nt(qx, k)
@@ -467,14 +490,13 @@
     rows = peers * n
     final_aux = collapse(
         pack_aux(jnp.broadcast_to(log_all, (GH * F, GW)), jnp.broadcast_to(dot_all, (GH * F, GW)))
-    )[:FM].astype(BF)
-    r, c = iota((rows, FM), 0), iota((rows, FM), 1)
-    subst = nn(onehot(c == r // n * f + r % n * R2 // R3), final_aux)
+    ).astype(BF)
+    r, c = iota((rows, F), 0), iota((rows, F), 1)
+    subst = nn(onehot(c == r // n * (stride * f) + r % n * R2 // R3), final_aux)
     yield
     noff, foff = lane_offsets(near_ref, group), lane_offsets(far_ref, group)
     also_far = (iota((rows, GW), 0) % (R3 // R2) == foff // R2) & (foff % R2 == noff)
-    naux = jnp.concatenate([a[:n, cols] for a in auxs], axis=0)
-    naux = jnp.where(also_far, subst, naux.astype(F32)).astype(BF)
+    naux = jnp.where(also_far, subst, naux).astype(BF)
     ax = expand(naux[:n])
     log_q, dot_q = piece_column(ax, 0), piece_column(ax, 1)
     r, c = iota((GH * n, GW), 0), iota((GH * n, GW), 1)
@@ -507,7 +529,6 @@
     near_dk = collapse(nn(ds2, queries))
     near_dv = collapse(nn(p2.astype(BF), grads))
     yield
-    ready("base")
     near, far = token_masks(near_ref, far_ref, group, length)
     place_n, place_f = near_place(n, length), far_place(length)
     att = jnp.where(near, nn(place_n, near_out[:, cols]), base[0][:, cols].astype(F32))
@@ -532,22 +553,18 @@
     done(0, cols)
 
 
-def final_kernel(peers, masks, near_ref, far_ref, *refs):
-    count = 1 + (peers + 1) + peers + 2 + 5
-    sources, results = refs[:count], refs[count : count + 4]
-    scratch = refs[count + 4 :]
-    held, outs, sems, out_sems = scratch[:count], scratch[count : count + 4], scratch[-2], scratch[-1]
-    copies = fetch(sources, held, sems)
-    ends = {"far": (0, 1), "near": (1, 2 + 2 * peers)}
-    ends["local"] = (ends["near"][1], ends["near"][1] + 2)
-    ends["base"] = (ends["local"][1], count)
-    waited = set()
-
-    def ready(what):
-        if what not in waited:
-            waited.add(what)
-            for copy in copies[slice(*ends[what])]:
-                copy.wait()
+def final_kernel(peers, stride, digits, near_ref, far_ref, *refs):
+    near_end = 2 + peers
+    count = near_end + 2 + 5
+    held, results = refs[:count], refs[count : count + 4]
+    outs, out_sems = refs[count + 4 : count + 8], refs[-1]
+    length = results[0].shape[0]
+    made = []
+
+    def packed():
+        if not made:
+            made.append(unpack_rows(peers, stride, length // R2, length // R3, held[0]))
+        return made[0]
 
     sent = []
 
@@ -558,13 +575,12 @@
         copy.start()
         sent.append(copy)
 
-    far, near, local = (held[slice(*ends[what])] for what in ("far", "near", "local"))
-    base = held[slice(*ends["base"])]
+    near, local, base = held[1:near_end], held[near_end : near_end + 2], held[near_end + 2 :]
     groups = results[0].shape[1] // GW
     lockstep(
         final_group(
-            peers, masks, group, near_ref, far_ref, near[: peers + 1], near[peers + 1 :], far[0], *local,
-            base[:4], base[4], outs, ready, done,
+            peers, stride, digits, group, near_ref, far_ref, near, packed, held[0], *local,
+            base[:4], base[4], outs, done,
         )
         for group in range(groups)
     )
@@ -643,12 +659,11 @@
         in_specs=[smem(), smem()]
         + [whole_block(2 * n, width)] * (peers + 1)
         + [whole_block(*stats.shape), whole_block(length, width), whole_block(FM, width)],
-        out_specs=[whole_block(n + FM, width), whole_block(*stats.shape), whole_block(n, width)],
-        out_shape=[like(n + FM), stats, like(n)],
+        out_specs=[whole_block(FM, width), whole_block(*stats.shape), whole_block(n, width)],
+        out_shape=[like(FM), stats, like(n)],
         compiler_params=params(),
         name="merge",
     )(near_offsets, far_offsets, kv, qg, *got, st1, att1, fr)
-    theirs = [swap(mine, "row", s) for s in range(1, peers)]
 
     grads = []
     pieces = pairs // per
@@ -670,35 +685,36 @@
             name="backward",
         )(queries, key_vectors, value_vectors, out_grad, st12, *grads)
 
-    grads = backward(0, grads)
-    grads, theirs = lax.optimization_barrier((grads, theirs))
-    at = 1
-    far_all = jnp.concatenate([x[n:] for x in (mine, *theirs)], axis=0)
-    masks = []
-    for axis, size, least in (("row", row_count, peers), ("col", col_count, 1)):
+    def masks_of(size, least):
         mask = size // 2
         while mask >= least:
-            other = swap(far_all, axis, mask)
-            if at < pieces:
-                grads = backward(at, grads)
-                grads, other = lax.optimization_barrier((grads, other))
-                at += 1
-            far_all = jnp.concatenate([far_all, other], axis=0)
-            masks.append(mask if axis == "row" else mask * row_count)
+            yield mask
             mask //= 2
-    while at < pieces:
+
+    steps = [("col", [m], 2, m * row_count) for m in masks_of(col_count, 2)]
+    steps += [("row", [m], 2, m) for m in masks_of(row_count, peers)]
+    stride = 2 ** len(steps)
+    steps.append(("row", list(range(1, peers)), peers, 1))
+    if col_count > 1:
+        steps.append(("col", [1], 2, row_count))
+    far_all = mine
+    for at, (axis, masks, _, _) in enumerate(steps):
+        others = [swap(far_all, axis, mask) for mask in masks]
+        if at < pieces:
+            grads = backward(at, grads)
+            grads, others = lax.optimization_barrier((grads, others))
+        far_all = jnp.concatenate([far_all, *others], axis=0)
+    for at in range(len(steps), pieces):
         grads = backward(at, grads)
-        at += 1
-
-    operands = (far_all, kv, qg, *got, mine, *theirs, key_vectors, value_vectors, att1, *grads, near_out)
+    digits = tuple((radix, unit) for _, _, radix, unit in steps)
+
+    operands = (far_all, kv, qg, *got, key_vectors, value_vectors, att1, *grads, near_out)
     return pl.pallas_call(
-        functools.partial(final_kernel, peers, tuple(masks)),
-        in_specs=[smem(), smem()] + [pl.BlockSpec(memory_space=pl.ANY)] * len(operands),
+        functools.partial(final_kernel, peers, stride, digits),
+        in_specs=[smem(), smem()] + [pl.BlockSpec(memory_space=pltpu.VMEM)] * len(operands),
         out_specs=[pl.BlockSpec(memory_space=pl.ANY)] * 4,
         out_shape=[like(length)] * 4,
-        scratch_shapes=[pltpu.VMEM(x.shape, x.dtype) for x in operands]
-        + [pltpu.VMEM((length, width), BF)] * 4
-        + [pltpu.SemaphoreType.DMA((len(operands),)), pltpu.SemaphoreType.DMA((4, groups))],
+        scratch_shapes=[pltpu.VMEM((length, width), BF)] * 4 + [pltpu.SemaphoreType.DMA((4, groups))],
         compiler_params=params(),
         name="final",
     )(near_offsets, far_offsets, *operands)

time: 49.5 us -> 44.1 us (0.89)
  waiting for transfers between devices: 5.87 us -> 4.16 us
  local copies, waits for them, and re-layouts: 2.42 us -> 0.78 us
  Pallas kernels: 27.3 us -> 25.7 us
    pallas_call x1, Pallas kernels: 9.62 us -> 7.91 us  [shards(): pl.pallas_call(functools.partial(final_kernel, peers, stride, digits), in...]
    ppermute x9, waiting for transfers between devices: 5.87 us -> 4.16 us  [swap(): return lax.ppermute(x, axis, [(i, i ^ mask) for i in range(size)])]
    unnamed x27 -> x23, local copies, waits for them, and re-layouts: 2.36 us -> 0.74 us
  transfers between devices with their start and end apart: 9 -> 9, of which waited for: 5 -> 5; matrix products, arithmetic and copies ran while one was open for 0% -> 0% of each run, Pallas kernels for 24% -> 26%
where the time goes in v3:
time: 44.1 us; the launch traced here: 43.9 us
  Pallas kernels  25.7 us (58%)
  starting transfers between devices  12.5 us (28%)
  waiting for transfers between devices  4.16 us (9%)
  between operations  0.82 us (2%)
  local copies, waits for them, and re-layouts  0.78 us (2%)
    ppermute x9, starting transfers between devices, swap(): return lax.ppermute(x, axis, [(i, i ^ mask) for i in range(size)])  12.5 us
    pallas_call x1, Pallas kernels, shards(): pl.pallas_call(functools.partial(final_kernel, peers, stride, digits), in...  7.91 us
    pallas_call x3, Pallas kernels, backward(): pl.pallas_call(functools.partial(backward_kernel, 256, 1, aliased), grid=...  6.89 us
    pallas_call x1, Pallas kernels, shards(): pl.pallas_call(functools.partial(forward_kernel, 256, 2), grid=(pairs //...  4.64 us
    pallas_call x1, Pallas kernels, shards(): pl.pallas_call(functools.partial(pick_kernel, peers), grid=(groups,), in_...  4.31 us
    ppermute x9, waiting for transfers between devices, swap(): return lax.ppermute(x, axis, [(i, i ^ mask) for i in range(size)])  4.16 us
    pallas_call x1, Pallas kernels, shards(): pl.pallas_call(functools.partial(merge_kernel, peers), grid=(1,), in_spec...  1.9 us
  transfers between devices with their start and end apart: 9, of which 5 were waited for; matrix products, arithmetic and copies ran while one was open for 0% of the time, Pallas kernels for 26%

profile of v3, /device:TPU:0, one launch (start us, length us, event | category | flops | bytes accessed | tf_op | source)
XLA Modules:
  0.0 43.9 jit_solution(1281988806241740772)
XLA Ops:
  0.7 4.3 %pick.1 = (bf16[64,768]{1,0:T(8,128)(2,1)}, bf16[64,768]{1,0:T(8,128)(2,1)}, bf16[16,768]{1,0:T(8,128)(2,1)}, bf16[64,768]{1,0:T(8,128)(2,1)}, bf16[64,768]{1,0:T(8,128)(2,1)}, /*index=5*/bf16[64,768]{1,0:T(8,128)(2,1)}) custom-call(s32[12]{0:T(128)} %near_ref.5, s32[12]{0:T(128)} %far_ref.5, bf16[512,768]{1,0:T(8,128)(2,1)} %q_ref.9, ...), custom_call_target="tpu_custom_call" | custom-call | tf_op jit(solution)/shard_map/pick/pallas_call | solution.py:623
  5.0 3.0 %collective-permute-start = (bf16[64,768]{1,0:T(8,128)(2,1)}, bf16[64,768]{1,0:T(8,128)(2,1)S(1)}, u32[]{:S(2)}, u32[]{:S(2)}) collective-permute-start(bf16[64,768]{1,0:T(8,128)(2,1)} %get-tuple-element.40), channel_id=1, source_target_pairs={{0,8},{8,0},{16,24},{24,16},{1,9},{9,1},{17,25},{25,17},{2,10},{10... | collective-permute-start | bytes 294920 | tf_op jit(solution)/shard_map/ppermute | solution.py:621
  8.0 1.5 %collective-permute-start.1 = (bf16[64,768]{1,0:T(8,128)(2,1)}, bf16[64,768]{1,0:T(8,128)(2,1)S(1)}, u32[]{:S(2)}, u32[]{:S(2)}) collective-permute-start(bf16[64,768]{1,0:T(8,128)(2,1)} %get-tuple-element.41), channel_id=1, source_target_pairs={{0,16},{8,24},{16,0},{24,8},{1,17},{9,25},{17,1},{25,9},{2,18},{10... | collective-permute-start | bytes 294920 | tf_op jit(solution)/shard_map/ppermute | solution.py:621
  9.5 0.0 collective-permute-start.2
  9.6 4.6 %forward.1 = (bf16[512,768]{1,0:T(8,128)(2,1)S(1)}, f32[48,512]{1,0:T(8,128)S(1)}) custom-call(bf16[512,768]{1,0:T(8,128)(2,1)S(1)} %copy-done.2, bf16[512,768]{1,0:T(8,128)(2,1)S(1)} %copy-done, bf16[512,768]{1,0:T(8,128)(2,1)S(1)} %copy-done.1, bf16[512,768]{1,0:T(8,128)(2,1)S(1)} %copy-done.3), custom_call_target="tpu_custom_call" | custom-call | flops 3221225472 | bytes 4718592 | tf_op jit(solution)/shard_map/forward/pallas_call | solution.py:645
  14.2 0.0 collective-permute-done.rest_0_.refs_3_
  14.2 1.0 %collective-permute-done.2.rest_2_.refs_5_ = bf16[64,768]{1,0:T(8,128)(2,1)S(1)} collective-permute-done((bf16[64,768]{1,0:T(8,128)(2,1)}, bf16[64,768]{1,0:T(8,128)(2,1)S(1)}, u32[]{:S(2)}, u32[]{:S(2)}) %collective-permute-start.2) | collective-permute-done | bytes 98336 | tf_op jit(solution)/shard_map/ppermute | solution.py:621
  15.3 0.6 %copy-done.7 = s32[12]{0:T(128)S(1)} copy-done((s32[12]{0:T(128)S(1)}, s32[12]{0:T(128)}, u32[]{:S(2)}) %copy-start.7) | copy-done | bytes 72
  15.9 0.0 copy-done.8
  15.9 1.9 %merge.1 = (bf16[16,768]{1,0:T(8,128)(2,1)S(1)}, f32[48,512]{1,0:T(8,128)S(1)}, bf16[32,768]{1,0:T(8,128)(2,1)S(1)}) custom-call(s32[12]{0:T(128)S(1)} %copy-done.7, s32[12]{0:T(128)S(1)} %copy-done.8, bf16[64,768]{1,0:T(8,128)(2,1)S(1)} %copy-done.4, bf16[64,768]{1,0:T(8,128)(2,1)S(1)} %copy-done.5, ...), custom_call_target="tpu_custom_call" | custom-call | tf_op jit(solution)/shard_map/merge/pallas_call | solution.py:656
  17.8 2.7 %collective-permute-start.3 = (bf16[16,768]{1,0:T(8,128)(2,1)S(1)}, bf16[16,768]{1,0:T(8,128)(2,1)S(1)}, u32[]{:S(2)}, u32[]{:S(2)}) collective-permute-start(bf16[16,768]{1,0:T(8,128)(2,1)S(1)} %get-tuple-element.46), channel_id=1, source_target_pairs={{0,4},{1,5},{2,6},{3,7},{4,0},{5,1},{6,2},{7,3},{8,12},{9,13},{10,... | collective-permute-start | bytes 73736 | tf_op jit(solution)/shard_map/ppermute | solution.py:621
  20.5 2.3 %backward.3 = (bf16[512,768]{1,0:T(8,128)(2,1)S(1)}, bf16[512,768]{1,0:T(8,128)(2,1)S(1)}, bf16[512,768]{1,0:T(8,128)(2,1)S(1)}) custom-call(bf16[512,768]{1,0:T(8,128)(2,1)S(1)} %copy-done.2, bf16[512,768]{1,0:T(8,128)(2,1)S(1)} %copy-done, bf16[512,768]{1,0:T(8,128)(2,1)S(1)} %copy-done.1, bf16[512,768]{1,0:T(8,128)(2,1)S(1)} %copy-done.3, ...), custom_call_target="tpu_custom_call" | custom-call | flops 2684354560 | bytes 2097152 | tf_op jit(solution)/shard_map/backward/pallas_call | solution.py:674
  22.8 1.6 %collective-permute-start.4 = (bf16[32,768]{1,0:T(8,128)(2,1)S(1)}, bf16[32,768]{1,0:T(8,128)(2,1)S(1)}, u32[]{:S(2)}, u32[]{:S(2)}) collective-permute-start(bf16[32,768]{1,0:T(8,128)(2,1)S(1)} %pad_maximum_fusion), channel_id=1, source_target_pairs={{0,2},{1,3},{2,0},{3,1},{4,6},{5,7},{6,4},{7,5},{8,10},{9,11},{10,... | collective-permute-start | bytes 147464 | tf_op jit(solution)/shard_map/ppermute | solution.py:621
  24.5 2.3 %backward.4 = (bf16[512,768]{1,0:T(8,128)(2,1)S(1)}, bf16[512,768]{1,0:T(8,128)(2,1)S(1)}, bf16[512,768]{1,0:T(8,128)(2,1)S(1)}) custom-call(bf16[512,768]{1,0:T(8,128)(2,1)S(1)} %copy-done.2, bf16[512,768]{1,0:T(8,128)(2,1)S(1)} %copy-done, bf16[512,768]{1,0:T(8,128)(2,1)S(1)} %copy-done.1, ...), custom_call_target="tpu_custom_call", output_to_operand_aliasing={{0}: (5, {}), {1}: (6, {}), {2}: (7, {})} | custom-call | flops 2684354560 | bytes 2097152 | tf_op jit(solution)/shard_map/backward/pallas_call | solution.py:674
  26.8 0.2 collective-permute-done.4
  27.0 2.0 %collective-permute-start.7 = (bf16[64,768]{1,0:T(8,128)(2,1)S(1)}, bf16[64,768]{1,0:T(8,128)(2,1)S(1)}, u32[]{:S(2)}, u32[]{:S(2)}) collective-permute-start(bf16[64,768]{1,0:T(8,128)(2,1)S(1)} %get-tuple-element.80), channel_id=1, source_target_pairs={{0,24},{8,16},{16,8},{24,0},{1,25},{9,17},{17,9},{25,1},{2,26},{10... | collective-permute-start | bytes 294920 | tf_op jit(solution)/shard_map/ppermute | solution.py:621
  29.0 0.5 %collective-permute-start.6 = (bf16[64,768]{1,0:T(8,128)(2,1)S(1)}, bf16[64,768]{1,0:T(8,128)(2,1)S(1)}, u32[]{:S(2)}, u32[]{:S(2)}) collective-permute-start(bf16[64,768]{1,0:T(8,128)(2,1)S(1)} %get-tuple-element.80), channel_id=1, source_target_pairs={{0,16},{8,24},{16,0},{24,8},{1,17},{9,25},{17,1},{25,9},{2,18},{10... | collective-permute-start | bytes 294920 | tf_op jit(solution)/shard_map/ppermute | solution.py:621
  29.5 1.1 %collective-permute-start.5 = (bf16[64,768]{1,0:T(8,128)(2,1)S(1)}, bf16[64,768]{1,0:T(8,128)(2,1)S(1)}, u32[]{:S(2)}, u32[]{:S(2)}) collective-permute-start(bf16[64,768]{1,0:T(8,128)(2,1)S(1)} %get-tuple-element.80), channel_id=1, source_target_pairs={{0,8},{8,0},{16,24},{24,16},{1,9},{9,1},{17,25},{25,17},{2,10},{10... | collective-permute-start | bytes 294920 | tf_op jit(solution)/shard_map/ppermute | solution.py:621
  30.5 2.3 %backward.5 = (bf16[512,768]{1,0:T(8,128)(2,1)S(1)}, bf16[512,768]{1,0:T(8,128)(2,1)S(1)}, bf16[512,768]{1,0:T(8,128)(2,1)S(1)}) custom-call(bf16[512,768]{1,0:T(8,128)(2,1)S(1)} %copy-done.2, bf16[512,768]{1,0:T(8,128)(2,1)S(1)} %copy-done, bf16[512,768]{1,0:T(8,128)(2,1)S(1)} %copy-done.1, ...), custom_call_target="tpu_custom_call", output_to_operand_aliasing={{0}: (5, {}), {1}: (6, {}), {2}: (7, {})} | custom-call | flops 2684354560 | bytes 2097152 | tf_op jit(solution)/shard_map/backward/pallas_call | solution.py:674
  32.9 1.0 %collective-permute-done.6 = bf16[64,768]{1,0:T(8,128)(2,1)S(1)} collective-permute-done((bf16[64,768]{1,0:T(8,128)(2,1)S(1)}, bf16[64,768]{1,0:T(8,128)(2,1)S(1)}, u32[]{:S(2)}, u32[]{:S(2)}) %collective-permute-start.6) | collective-permute-done | bytes 98336 | tf_op jit(solution)/shard_map/ppermute | solution.py:621
  33.9 0.2 collective-permute-done.5
  34.2 0.1 collective-permute-start.8
  34.2 1.7 %collective-permute-done.8 = bf16[256,768]{1,0:T(8,128)(2,1)S(1)} collective-permute-done((bf16[256,768]{1,0:T(8,128)(2,1)S(1)}, bf16[256,768]{1,0:T(8,128)(2,1)S(1)}, u32[]{:S(2)}, u32[]{:S(2)}) %collective-permute-start.8) | collective-permute-done | bytes 393248 | tf_op jit(solution)/shard_map/ppermute | solution.py:621
  36.0 7.9 %final.1 = (bf16[512,768]{1,0:T(8,128)(2,1)}, bf16[512,768]{1,0:T(8,128)(2,1)}, bf16[512,768]{1,0:T(8,128)(2,1)}, bf16[512,768]{1,0:T(8,128)(2,1)}) custom-call(s32[12]{0:T(128)S(1)} %copy-done.7, s32[12]{0:T(128)S(1)} %copy-done.8, bf16[512,768]{1,0:T(8,128)(2,1)S(1)} %constant_dynamic-update-slice_fusion.9.refs_0_, bf16[64,768]{1,0:T(8,128)(2,1)S(1)} %copy-done.4, ...), custom_call_target="tpu_custom_call" | custom-call | tf_op jit(solution)/shard_map/final/pallas_call | solution.py:712
  (27 shorter events, 0.1 us)
Async XLA Ops:
  0.6 8.9 %copy-start.1 = (bf16[512,768]{1,0:T(8,128)(2,1)S(1)}, bf16[512,768]{1,0:T(8,128)(2,1)}, u32[]{:S(2)}) copy-start(bf16[512,768]{1,0:T(8,128)(2,1)} %refs_7_.1) | copy-start | bytes 2359300
  0.6 8.9 %copy-start = (bf16[512,768]{1,0:T(8,128)(2,1)S(1)}, bf16[512,768]{1,0:T(8,128)(2,1)}, u32[]{:S(2)}) copy-start(bf16[512,768]{1,0:T(8,128)(2,1)} %refs_6_.1) | copy-start | bytes 2359300
  0.7 8.9 %copy-start.3 = (bf16[512,768]{1,0:T(8,128)(2,1)S(1)}, bf16[512,768]{1,0:T(8,128)(2,1)}, u32[]{:S(2)}) copy-start(bf16[512,768]{1,0:T(8,128)(2,1)} %g_ref.9) | copy-start | bytes 2359300
  0.7 8.9 %copy-start.2 = (bf16[512,768]{1,0:T(8,128)(2,1)S(1)}, bf16[512,768]{1,0:T(8,128)(2,1)}, u32[]{:S(2)}) copy-start(bf16[512,768]{1,0:T(8,128)(2,1)} %q_ref.9) | copy-start | bytes 2359300
  5.0 9.2 %collective-permute-start = (bf16[64,768]{1,0:T(8,128)(2,1)}, bf16[64,768]{1,0:T(8,128)(2,1)S(1)}, u32[]{:S(2)}, u32[]{:S(2)}) collective-permute-start(bf16[64,768]{1,0:T(8,128)(2,1)} %get-tuple-element.40), channel_id=1, source_target_pairs={{0,8},{8,0},{16,24},{24,16},{1,9},{9,1},{17,25},{25,17},{2,10},{10... | collective-permute-start | bytes 294920 | tf_op jit(solution)/shard_map/ppermute | solution.py:621
  8.0 6.2 %collective-permute-start.1 = (bf16[64,768]{1,0:T(8,128)(2,1)}, bf16[64,768]{1,0:T(8,128)(2,1)S(1)}, u32[]{:S(2)}, u32[]{:S(2)}) collective-permute-start(bf16[64,768]{1,0:T(8,128)(2,1)} %get-tuple-element.41), channel_id=1, source_target_pairs={{0,16},{8,24},{16,0},{24,8},{1,17},{9,25},{17,1},{25,9},{2,18},{10... | collective-permute-start | bytes 294920 | tf_op jit(solution)/shard_map/ppermute | solution.py:621
  9.5 5.7 %copy-start.4 = (bf16[64,768]{1,0:T(8,128)(2,1)S(1)}, bf16[64,768]{1,0:T(8,128)(2,1)}, u32[]{:S(2)}) copy-start(bf16[64,768]{1,0:T(8,128)(2,1)} %get-tuple-element.38.kv_ref.refs_1_) | copy-start | bytes 294916
  9.5 5.7 %copy-start.5 = (bf16[64,768]{1,0:T(8,128)(2,1)S(1)}, bf16[64,768]{1,0:T(8,128)(2,1)}, u32[]{:S(2)}) copy-start(bf16[64,768]{1,0:T(8,128)(2,1)} %get-tuple-element.39.qg_ref.refs_2_) | copy-start | bytes 294916
  9.5 5.7 %collective-permute-start.2 = (bf16[64,768]{1,0:T(8,128)(2,1)}, bf16[64,768]{1,0:T(8,128)(2,1)S(1)}, u32[]{:S(2)}, u32[]{:S(2)}) collective-permute-start(bf16[64,768]{1,0:T(8,128)(2,1)} %get-tuple-element.42), channel_id=1, source_target_pairs={{0,24},{8,16},{16,8},{24,0},{1,25},{9,17},{17,9},{25,1},{2,26},{10... | collective-permute-start | bytes 294920 | tf_op jit(solution)/shard_map/ppermute | solution.py:621
  9.6 5.7 %copy-start.6 = (bf16[16,768]{1,0:T(8,128)(2,1)S(1)}, bf16[16,768]{1,0:T(8,128)(2,1)}, u32[]{:S(2)}) copy-start(bf16[16,768]{1,0:T(8,128)(2,1)} %get-tuple-element.45.rest_5_) | copy-start | bytes 73732
  15.2 0.7 %copy-start.7 = (s32[12]{0:T(128)S(1)}, s32[12]{0:T(128)}, u32[]{:S(2)}) copy-start(s32[12]{0:T(128)} %near_ref.5) | copy-start | bytes 148
  15.2 0.7 %copy-start.8 = (s32[12]{0:T(128)S(1)}, s32[12]{0:T(128)}, u32[]{:S(2)}) copy-start(s32[12]{0:T(128)} %far_ref.5) | copy-start | bytes 148
  17.8 5.0 %collective-permute-start.3 = (bf16[16,768]{1,0:T(8,128)(2,1)S(1)}, bf16[16,768]{1,0:T(8,128)(2,1)S(1)}, u32[]{:S(2)}, u32[]{:S(2)}) collective-permute-start(bf16[16,768]{1,0:T(8,128)(2,1)S(1)} %get-tuple-element.46), channel_id=1, source_target_pairs={{0,4},{1,5},{2,6},{3,7},{4,0},{5,1},{6,2},{7,3},{8,12},{9,13},{10,... | collective-permute-start | bytes 73736 | tf_op jit(solution)/shard_map/ppermute | solution.py:621
  22.8 4.2 %collective-permute-start.4 = (bf16[32,768]{1,0:T(8,128)(2,1)S(1)}, bf16[32,768]{1,0:T(8,128)(2,1)S(1)}, u32[]{:S(2)}, u32[]{:S(2)}) collective-permute-start(bf16[32,768]{1,0:T(8,128)(2,1)S(1)} %pad_maximum_fusion), channel_id=1, source_target_pairs={{0,2},{1,3},{2,0},{3,1},{4,6},{5,7},{6,4},{7,5},{8,10},{9,11},{10,... | collective-permute-start | bytes 147464 | tf_op jit(solution)/shard_map/ppermute | solution.py:621
  27.0 5.9 %collective-permute-start.7 = (bf16[64,768]{1,0:T(8,128)(2,1)S(1)}, bf16[64,768]{1,0:T(8,128)(2,1)S(1)}, u32[]{:S(2)}, u32[]{:S(2)}) collective-permute-start(bf16[64,768]{1,0:T(8,128)(2,1)S(1)} %get-tuple-element.80), channel_id=1, source_target_pairs={{0,24},{8,16},{16,8},{24,0},{1,25},{9,17},{17,9},{25,1},{2,26},{10... | collective-permute-start | bytes 294920 | tf_op jit(solution)/shard_map/ppermute | solution.py:621
  29.0 4.9 %collective-permute-start.6 = (bf16[64,768]{1,0:T(8,128)(2,1)S(1)}, bf16[64,768]{1,0:T(8,128)(2,1)S(1)}, u32[]{:S(2)}, u32[]{:S(2)}) collective-permute-start(bf16[64,768]{1,0:T(8,128)(2,1)S(1)} %get-tuple-element.80), channel_id=1, source_target_pairs={{0,16},{8,24},{16,0},{24,8},{1,17},{9,25},{17,1},{25,9},{2,18},{10... | collective-permute-start | bytes 294920 | tf_op jit(solution)/shard_map/ppermute | solution.py:621
  29.5 4.6 %collective-permute-start.5 = (bf16[64,768]{1,0:T(8,128)(2,1)S(1)}, bf16[64,768]{1,0:T(8,128)(2,1)S(1)}, u32[]{:S(2)}, u32[]{:S(2)}) collective-permute-start(bf16[64,768]{1,0:T(8,128)(2,1)S(1)} %get-tuple-element.80), channel_id=1, source_target_pairs={{0,8},{8,0},{16,24},{24,16},{1,9},{9,1},{17,25},{25,17},{2,10},{10... | collective-permute-start | bytes 294920 | tf_op jit(solution)/shard_map/ppermute | solution.py:621
  34.2 1.8 %collective-permute-start.8 = (bf16[256,768]{1,0:T(8,128)(2,1)S(1)}, bf16[256,768]{1,0:T(8,128)(2,1)S(1)}, u32[]{:S(2)}, u32[]{:S(2)}) collective-permute-start(bf16[256,768]{1,0:T(8,128)(2,1)S(1)} %get-tuple-element.72), channel_id=1, source_target_pairs={{0,1},{1,0},{2,3},{3,2},{4,5},{5,4},{6,7},{7,6},{8,9},{9,8},{10,11... | collective-permute-start | bytes 1179656 | tf_op jit(solution)/shard_map/ppermute | solution.py:621

commit v4 on v3

--- a/solution.py
+++ b/solution.py
@@ -119,23 +119,49 @@
     return near, far
 
 
+class HeadOffsets:
+    def __init__(self, block, row, group):
+        self.lanes = block[row : row + 1].astype(jnp.int32)
+        self.first = group * GH
+
+    def __getitem__(self, head):
+        at = (head - self.first) * HD
+        return self.lanes[:, at : at + 1]
+
+
+def read_offsets(fr_ref, f, group):
+    block = fr_ref[:, group_columns(group)].astype(F32)
+    return HeadOffsets(block, 5 * f, group), HeadOffsets(block, 5 * f + 1, group)
+
+
+def head_rows(n, stride, length, ref, group):
+    r = iota((GH * n, 1), 0)
+    token = r % n * stride
+    for h in range(GH):
+        token = jnp.where(r // n == h, token + ref[group * GH + h], token)
+    return onehot(iota((GH * n, length), 1) == token)
+
+
 def pick_kernel(peers, near_ref, far_ref, q_ref, k_ref, v_ref, g_ref, kv_ref, qg_ref, fr_ref, *msg_refs):
     group = pl.program_id(0)
     length = q_ref.shape[0]
     n, f = length // R2, length // R3
-    near, far = token_masks(near_ref, far_ref, group, length)
-    near, far = onehot(near), onehot(far)
-    sel = near_select(n, length)
-    q, k, v, g = q_ref[...], k_ref[...], v_ref[...], g_ref[...]
-    picked = [nn(sel, x * near).astype(BF) for x in (k, v, q, g)]
-    kv = jnp.concatenate(picked[:2], axis=0)
-    qg = jnp.concatenate(picked[2:], axis=0)
+    sel = jnp.concatenate(
+        [head_rows(n, R2, length, near_ref, group), head_rows(8, R3, length, far_ref, group)], axis=0
+    )
+    picked, far = [], []
+    for ref in (q_ref, k_ref, v_ref, g_ref):
+        rows = nn(sel, ref[...])
+        picked.append(collapse(rows[: GH * n]).astype(BF))
+        far.append(collapse(rows[GH * n :])[:f])
+    offsets = [lane_offsets(ref, group).astype(F32) for ref in (near_ref, far_ref)]
+    far += [jnp.zeros((f, GW), F32), *offsets, jnp.zeros((FM - 5 * f - 2, GW), F32)]
+    fr_ref[...] = jnp.concatenate(far, axis=0).astype(BF)
+    q, k, v, g = picked
+    kv = jnp.concatenate([k, v], axis=0)
+    qg = jnp.concatenate([q, g], axis=0)
     kv_ref[...] = kv
     qg_ref[...] = qg
-    fr = jnp.zeros((FM, GW), F32)
-    for at, x in enumerate((q, k, v, g)):
-        fr += nn(far_select(FM, length, at * f), x * far)
-    fr_ref[...] = fr.astype(BF)
     own = lax.axis_index("row") % peers
     for slot in range(1, peers):
         later = (own ^ slot) > own
@@ -279,11 +305,12 @@
     return out.astype(BF)
 
 
-def merge_group(peers, group, near_ref, far_ref, kv_ref, qg_ref, got, st_ref, att_ref, fr_ref, out_ref, st_out, near_out, blocks, packs):
+def merge_group(peers, group, kv_ref, qg_ref, got, st_ref, att_ref, fr_ref, out_ref, st_out, near_out, blocks, packs):
     cols = group_columns(group)
     srows = slice(group * SR, (group + 1) * SR)
     length = att_ref.shape[0]
     n, f = length // R2, length // R3
+    near_ref, far_ref = read_offsets(fr_ref, f, group)
     own = lax.axis_index("row") % peers
     heads = (kv_ref, *got)
     keys = jnp.concatenate([r[:n, cols] for r in heads], axis=0)
@@ -296,8 +323,7 @@
     far_st = t % R3 == stat_offsets(far_ref, group)
     sel = near_select(n, length)
     log1 = nt(sel, pieces3(jnp.where(near_st, st, 0.0)))
-    near = onehot(iota((length, GW), 0) % R2 == lane_offsets(near_ref, group))
-    out1 = nn(sel, att_ref[:, cols] * near)
+    out1 = collapse(nn(head_rows(n, R2, length, near_ref, group), att_ref[:, cols]))
     yield
     s = jnp.where(near_valid_queries(s.shape, n, own), s, NEG)
     top = jnp.max(s, axis=1, keepdims=True)
@@ -336,16 +362,17 @@
     head, what = stat_row((3 * SR, GW), 0)
     lane, piece = iota((3 * SR, GW), 1), iota((3 * SR, GW), 0) // SR
     far_aux = nn(far_aux.astype(BF), onehot((lane // HD == head) & (lane % HD == what * 3 + piece)))
-    blocks[group] = fr_ref[:, cols].astype(F32) + far_aux
-
-
-def merge_kernel(peers, near_ref, far_ref, kv_ref, qg_ref, *rest):
+    raw = fr_ref[:, cols].astype(F32)
+    blocks[group] = jnp.where(iota(raw.shape, 0) < 4 * f, raw, 0.0) + far_aux
+
+
+def merge_kernel(peers, kv_ref, qg_ref, *rest):
     got, rest = rest[: peers - 1], rest[peers - 1 :]
     groups = kv_ref.shape[1] // GW
     out_ref = rest[3]
     blocks, packs = {}, []
     lockstep(
-        merge_group(peers, group, near_ref, far_ref, kv_ref, qg_ref, got, *rest, blocks, packs)
+        merge_group(peers, group, kv_ref, qg_ref, got, *rest, blocks, packs)
         for group in range(groups)
     )
     packed = sum(packs[1:], packs[0]).astype(BF)
@@ -358,9 +385,9 @@
         out_ref[:, at * 128 : (at + 1) * 128] = (block + rows).astype(BF)
 
 
-def backward_kernel(strip, skew, aliased, q_ref, k_ref, v_ref, g_ref, st_ref, *rest):
+def backward_kernel(strip, skew, span, aliased, q_ref, k_ref, v_ref, g_ref, st_ref, *rest):
     dq_ref, dk_ref, dv_ref = rest[aliased:]
-    length, width = q_ref.shape
+    length = q_ref.shape[0]
     first, in_head = head_masks()
     diag = iota((strip, strip), 0) <= iota((strip, strip), 1)
     eye = eye_of(PW)
@@ -401,7 +428,7 @@
             both = jnp.concatenate([kept.pop(("dq", p, c, 0)), kept.pop(("dq", p, c, 1))], axis=0)
             dq_ref[rows, cols] = both.T.astype(BF)
 
-    units = [(p, c, h) for p in range(width // PW) for c in range(strips) for h in range(2)]
+    units = [(p, c, h) for p in span for c in range(strips) for h in range(2)]
     staged(units, (score, soften, mix), skew)
 
 
@@ -414,13 +441,44 @@
     return seq * f + index % f
 
 
+def row_offsets(n, ref, group):
+    r = iota((GH * n, 1), 0)
+    out = jnp.zeros((GH * n, 1), jnp.int32)
+    for h in range(GH):
+        out = jnp.where(r // n == h, ref[group * GH + h], out)
+    return out
+
+
+def place_columns(n, length, near_ref, far_ref, group):
+    parts = []
+    for count, stride, ref in ((n, R2, near_ref), (FM, R3, far_ref)):
+        c = iota((1, GH * count), 1)
+        token = c % count * stride
+        for h in range(GH):
+            token = jnp.where(c // count == h, token + ref[group * GH + h], token)
+        parts.append(token)
+    return onehot(iota((length, GH * (n + FM)), 0) == jnp.concatenate(parts, axis=1))
+
+
+def own_lanes(x):
+    n = x.shape[0] // GH
+    return jnp.where(iota(x.shape, 1) // HD == iota(x.shape, 0) // n, x, 0.0)
+
+
+def piece_columns(aux_expanded):
+    a, c = iota((GW, 256), 0), iota((GW, 256), 1)
+    both = nn(aux_expanded, onehot(a % HD // 3 == c // 128))
+    return both[:, :1], both[:, 128:129]
+
+
 def final_group(
-    peers, stride, digits, group, near_ref, far_ref, got, packed, fa_ref, k_ref, v_ref, base, near_out, outs, done
+    peers, stride, digits, group, fr_ref, got, packed, fa_ref, k_ref, v_ref, base, near_out, outs, done
 ):
     kv_ref, qg_ref, got = got[0], got[1], got[2:]
     cols = group_columns(group)
     length = k_ref.shape[0]
     n, f = length // R2, length // R3
+    near_ref, far_ref = read_offsets(fr_ref, f, group)
     blocks = fa_ref.shape[0] // FM
     F = blocks * f
     row_here = lax.axis_index("row")
@@ -438,7 +496,7 @@
     qx, gx, ax = expand(fq * scale), expand(fg), expand(faux)
     s = nt(qx, fk)
     dp = nt(gx, fv)
-    log12, dot12 = piece_column(ax, 0), piece_column(ax, 1)
+    log12, dot12 = piece_columns(ax)
     yield
     heads = [kv_ref, *got]
     keys = jnp.concatenate([x[:n, cols] for x in heads], axis=0)
@@ -451,7 +509,6 @@
     near_dp = nt(expand(grads[:n]), values)
     near_s2 = nt(expand(keys[:n]), queries)
     near_dp2 = nt(expand(values[:n]), grads)
-    yield
     place_q = far_seq(iota((GH * F, 1), 0) % F, f, digits, seq)
     place_k = far_seq(iota((1, F), 1), f, digits, seq)
     s = jnp.where(place_k <= place_q, s, NEG)
@@ -460,6 +517,19 @@
     w = jnp.exp(s - top)
     total = jnp.sum(w, axis=1, keepdims=True)
     dot3 = jnp.sum(w * dp, axis=1, keepdims=True)
+    k, v = k_ref[:, cols], v_ref[:, cols]
+
+    def own_rows(x):
+        return jnp.concatenate([x[h * F : h * F + FM] for h in range(GH)], axis=0)
+
+    qo, go = own_rows(qx), own_rows(gx)
+    local_s = nt(qo, k)
+    local_dp = nt(go, v)
+    roff, rnear = row_offsets(FM, far_ref, group), row_offsets(FM, near_ref, group)
+    token = iota((GH * FM, 1), 0) % FM * R3 + roff
+    att_far = nn(onehot(iota((GH * FM, length), 1) == token), base[0][:, cols])
+    near_far = nn(onehot(iota((GH * FM, n), 1) * R2 + rnear == token), near_out[:, cols])
+    att_far = jnp.where(roff % R2 == rnear, near_far, att_far)
     yield
     log3 = top + jnp.log(total)
     dot3 = dot3 / total
@@ -471,89 +541,70 @@
     p = jnp.exp(s - log_all)
     ds = p * (dp - dot_all)
     pb, dsb = p.astype(BF), ds.astype(BF)
-    yield
-    far_dv = tn(pb, gx)[:FM]
-    far_dk = tn(dsb, qx)[:FM]
-    far_dq = collapse(nn(dsb, fk))[:FM] * SCALE
-    far_out = collapse(nn(pb, fv))[:FM]
-    keep = collapse(jnp.broadcast_to(e12 / both, (GH * F, GW)))[:FM]
-    yield
-
-    def own_rows(x):
-        return jnp.concatenate([x[h * F : h * F + FM] for h in range(GH)], axis=0)
-
-    qx, gx, log_own, dot_own = own_rows(qx), own_rows(gx), own_rows(log_all), own_rows(dot_all)
-    k, v = k_ref[:, cols], v_ref[:, cols]
-    s = nt(qx, k)
-    dp = nt(gx, v)
-
-    rows = peers * n
+    log_own, dot_own, keep = own_rows(log_all), own_rows(dot_all), own_rows(e12 / both)
+    yield
     final_aux = collapse(
         pack_aux(jnp.broadcast_to(log_all, (GH * F, GW)), jnp.broadcast_to(dot_all, (GH * F, GW)))
     ).astype(BF)
+    rows = peers * n
     r, c = iota((rows, F), 0), iota((rows, F), 1)
     subst = nn(onehot(c == r // n * (stride * f) + r % n * R2 // R3), final_aux)
-    yield
+    far_out = own_lanes(nn(own_rows(pb), fv) + keep * att_far)
+    far_dq = nn(own_rows(dsb), fk)
+    far_dv = tn(pb, gx)[:FM]
+    far_dk = tn(dsb, qx)[:FM]
+    yield
+    r = iota((GH * FM, 1), 0)
+    reach = jnp.where(r % FM < f, token, -1)
+    ok = iota((GH * FM, length), 1) <= reach
+    p = jnp.where(ok, jnp.exp(local_s - log_own), 0.0)
+    ds = (p * (local_dp - dot_own)).astype(BF)
+    pb = p.astype(BF)
     noff, foff = lane_offsets(near_ref, group), lane_offsets(far_ref, group)
     also_far = (iota((rows, GW), 0) % (R3 // R2) == foff // R2) & (foff % R2 == noff)
     naux = jnp.where(also_far, subst, naux).astype(BF)
-    ax = expand(naux[:n])
-    log_q, dot_q = piece_column(ax, 0), piece_column(ax, 1)
-    r, c = iota((GH * n, GW), 0), iota((GH * n, GW), 1)
-    mine = c // HD == r // n
-    log_k = nt(onehot(mine & (c % HD // 3 == 0)), naux)
-    dot_k = nt(onehot(mine & (c % HD // 3 == 1)), naux)
-    yield
-    r = iota((GH * FM, 1), 0)
-    reach = jnp.zeros((GH * FM, 1), jnp.int32)
-    for h in range(GH):
-        reach = jnp.where(r // FM == h, far_ref[group * GH + h], reach)
-    reach = jnp.where(r % FM < f, reach + r % FM * R3, -1)
-    ok = iota((GH * FM, length), 1) <= reach
-    p = jnp.where(ok, jnp.exp(s - log_own), 0.0)
-    ds = (p * (dp - dot_own)).astype(BF)
-    pb = p.astype(BF)
-    yield
-    far_dq += collapse(nn(ds, k)) * SCALE
-    dk = tn(ds, qx)
-    dv = tn(pb, gx)
+    yield
+    log_q, dot_q = piece_columns(expand(naux[:n]))
+    r, c = iota((2 * GH * n, GW), 0), iota((2 * GH * n, GW), 1)
+    head, which = r % (GH * n) // n, r // (GH * n)
+    stats = nt(onehot((c // HD == head) & (c % HD // 3 == which)), naux)
+    log_k, dot_k = stats[: GH * n], stats[GH * n :]
+    far_dq = own_lanes(far_dq + nn(ds, k))
+    place = place_columns(n, length, near_ref, far_ref, group)
+    alone = jnp.where(also_far[:n], 0.0, near_out[:, cols].astype(F32)).astype(BF)
+    placed = nn(place, jnp.concatenate([expand(alone), far_out.astype(BF)], axis=0))
+    yield
+    near, far = token_masks(near_ref, far_ref, group, length)
+    outs[0][:, cols] = jnp.where(near | far, placed, base[0][:, cols].astype(F32)).astype(BF)
+    done(0, cols)
     yield
     ok = near_valid_queries(near_s.shape, n, own)
-    p = jnp.where(ok, jnp.exp(near_s - log_q), 0.0)
-    ds = (p * (near_dp - dot_q)).astype(BF)
+    np = jnp.where(ok, jnp.exp(near_s - log_q), 0.0)
+    nds = (np * (near_dp - dot_q)).astype(BF)
     ok = near_valid_keys(near_s2.shape, n, own)
-    p2 = jnp.where(ok, jnp.exp(near_s2 - log_k), 0.0)
-    ds2 = (p2 * (near_dp2 - dot_k)).astype(BF)
-    yield
-    near_dq = collapse(nn(ds, keys)) * SCALE
-    near_dk = collapse(nn(ds2, queries))
-    near_dv = collapse(nn(p2.astype(BF), grads))
-    yield
-    near, far = token_masks(near_ref, far_ref, group, length)
-    place_n, place_f = near_place(n, length), far_place(length)
-    att = jnp.where(near, nn(place_n, near_out[:, cols]), base[0][:, cols].astype(F32))
-    far_out += keep * nn(far_select(FM, length, 0), att.astype(BF) * onehot(far))
-    yield
-
-    def terms(near_part, far_part):
-        return jnp.where(near, nn(place_n, near_part.astype(BF)), 0.0) + jnp.where(
-            far, nn(place_f, far_part.astype(BF)), 0.0
-        )
-
-    outs[1][:, cols] = (base[1][:, cols].astype(F32) + terms(near_dq, far_dq)).astype(BF)
+    np2 = jnp.where(ok, jnp.exp(near_s2 - log_k), 0.0)
+    nds2 = (np2 * (near_dp2 - dot_k)).astype(BF)
+    dk = tn(ds, qo)
+    dv = tn(pb, go)
+    yield
+    near_dq = own_lanes(nn(nds, keys))
+    near_dk = own_lanes(nn(nds2, queries))
+    near_dv = own_lanes(nn(np2.astype(BF), grads))
+    yield
+    terms = nn(place, (jnp.concatenate([near_dq, far_dq], axis=0) * SCALE).astype(BF))
+    outs[1][:, cols] = (base[1][:, cols].astype(F32) + terms).astype(BF)
     done(1, cols)
     yield
-    outs[2][:, cols] = (base[2][:, cols].astype(F32) + dk + terms(near_dk, far_dk)).astype(BF)
+    terms = dk + nn(place, jnp.concatenate([near_dk.astype(BF), expand(far_dk.astype(BF))], axis=0))
+    outs[2][:, cols] = (base[2][:, cols].astype(F32) + terms).astype(BF)
     done(2, cols)
     yield
-    outs[3][:, cols] = (base[3][:, cols].astype(F32) + dv + terms(near_dv, far_dv)).astype(BF)
+    terms = dv + nn(place, jnp.concatenate([near_dv.astype(BF), expand(far_dv.astype(BF))], axis=0))
+    outs[3][:, cols] = (base[3][:, cols].astype(F32) + terms).astype(BF)
     done(3, cols)
-    yield
-    outs[0][:, cols] = jnp.where(far, nn(place_f, far_out.astype(BF)), att).astype(BF)
-    done(0, cols)
-
-
-def final_kernel(peers, stride, digits, near_ref, far_ref, *refs):
+
+
+def final_kernel(peers, stride, digits, fr_ref, *refs):
     near_end = 2 + peers
     count = near_end + 2 + 5
     held, results = refs[:count], refs[count : count + 4]
@@ -579,7 +630,7 @@
     groups = results[0].shape[1] // GW
     lockstep(
         final_group(
-            peers, stride, digits, group, near_ref, far_ref, near, packed, held[0], *local,
+            peers, stride, digits, group, fr_ref, near, packed, held[0], *local,
             base[:4], base[4], outs, done,
         )
         for group in range(groups)
@@ -636,6 +687,8 @@
     stats = jax.ShapeDtypeStruct((pairs * 8, length), F32)
     per = 2
 
+    vmem_spec = pl.BlockSpec(memory_space=pltpu.VMEM)
+
     def pair_block(first):
         return pl.BlockSpec((length, per * PW), lambda p: (0, first + p))
 
@@ -644,9 +697,8 @@
 
     att1, st1 = pl.pallas_call(
         functools.partial(forward_kernel, 256, 2),
-        grid=(pairs // per,),
-        in_specs=[pair_block(0)] * 4,
-        out_specs=[pair_block(0), stat_block(0)],
+        in_specs=[vmem_spec] * 4,
+        out_specs=[vmem_spec] * 2,
         out_shape=[like(length), stats],
         compiler_params=params(),
         cost_estimate=pl.CostEstimate(flops=2 * ops * 4, bytes_accessed=6 * length * width * 2, transcendentals=0),
@@ -655,15 +707,12 @@
 
     mine, st12, near_out = pl.pallas_call(
         functools.partial(merge_kernel, peers),
-        grid=(1,),
-        in_specs=[smem(), smem()]
-        + [whole_block(2 * n, width)] * (peers + 1)
-        + [whole_block(*stats.shape), whole_block(length, width), whole_block(FM, width)],
-        out_specs=[whole_block(FM, width), whole_block(*stats.shape), whole_block(n, width)],
+        in_specs=[vmem_spec] * (peers + 4),
+        out_specs=[vmem_spec] * 3,
         out_shape=[like(FM), stats, like(n)],
         compiler_params=params(),
         name="merge",
-    )(near_offsets, far_offsets, kv, qg, *got, st1, att1, fr)
+    )(kv, qg, *got, st1, att1, fr)
 
     grads = []
     pieces = pairs // per
@@ -672,10 +721,9 @@
         any_spec = pl.BlockSpec(memory_space=pl.ANY)
         aliased = len(grads)
         return pl.pallas_call(
-            functools.partial(backward_kernel, 256, 1, aliased),
-            grid=(1,),
-            in_specs=[pair_block(piece)] * 4 + [stat_block(piece)] + [any_spec] * aliased,
-            out_specs=[pair_block(piece)] * 3,
+            functools.partial(backward_kernel, 256, 1, range(piece * per, (piece + 1) * per), aliased),
+            in_specs=[vmem_spec] * 5 + [vmem_spec] * aliased,
+            out_specs=[vmem_spec] * 3,
             out_shape=[like(length)] * 3,
             input_output_aliases={5 + i: i for i in range(aliased)},
             compiler_params=params(),
@@ -685,39 +733,41 @@
             name="backward",
         )(queries, key_vectors, value_vectors, out_grad, st12, *grads)
 
-    def masks_of(size, least):
-        mask = size // 2
-        while mask >= least:
-            yield mask
-            mask //= 2
-
-    steps = [("col", [m], 2, m * row_count) for m in masks_of(col_count, 2)]
-    steps += [("row", [m], 2, m) for m in masks_of(row_count, peers)]
-    stride = 2 ** len(steps)
-    steps.append(("row", list(range(1, peers)), peers, 1))
+    def bits_of(size, least):
+        while size > least:
+            pick = 4 if size >= 4 * least else 2
+            size //= pick
+            yield pick, size
+
+    steps = [("col", radix, unit, unit * row_count) for radix, unit in bits_of(col_count, 2)]
+    steps += [("row", radix, unit, unit) for radix, unit in bits_of(row_count, peers)]
+    stride = 1
+    for _, radix, _, _ in steps:
+        stride *= radix
+    steps.append(("row", peers, 1, 1))
     if col_count > 1:
-        steps.append(("col", [1], 2, row_count))
+        steps.append(("col", 2, 1, row_count))
     far_all = mine
-    for at, (axis, masks, _, _) in enumerate(steps):
-        others = [swap(far_all, axis, mask) for mask in masks]
+    for at, (axis, radix, unit, _) in enumerate(steps):
+        others = [swap(far_all, axis, digit * unit) for digit in range(1, radix)]
         if at < pieces:
             grads = backward(at, grads)
             grads, others = lax.optimization_barrier((grads, others))
         far_all = jnp.concatenate([far_all, *others], axis=0)
     for at in range(len(steps), pieces):
         grads = backward(at, grads)
-    digits = tuple((radix, unit) for _, _, radix, unit in steps)
-
-    operands = (far_all, kv, qg, *got, key_vectors, value_vectors, att1, *grads, near_out)
+    digits = tuple((radix, unit) for _, radix, _, unit in steps)
+
+    operands = (fr, far_all, kv, qg, *got, key_vectors, value_vectors, att1, *grads, near_out)
     return pl.pallas_call(
         functools.partial(final_kernel, peers, stride, digits),
-        in_specs=[smem(), smem()] + [pl.BlockSpec(memory_space=pltpu.VMEM)] * len(operands),
+        in_specs=[vmem_spec] * len(operands),
         out_specs=[pl.BlockSpec(memory_space=pl.ANY)] * 4,
         out_shape=[like(length)] * 4,
         scratch_shapes=[pltpu.VMEM((length, width), BF)] * 4 + [pltpu.SemaphoreType.DMA((4, groups))],
         compiler_params=params(),
         name="final",
-    )(near_offsets, far_offsets, *operands)
+    )(*operands)
 
 
 def solution(mesh):

time: 44.1 us -> 40.6 us (0.921)
  Pallas kernels: 25.7 us -> 21.8 us
  waiting for transfers between devices: 4.16 us -> 4.89 us
  local copies, waits for them, and re-layouts: 0.78 us -> 0.13 us
    pallas_call x1, Pallas kernels: 7.91 us -> 5.91 us  [shards(): pl.pallas_call(functools.partial(final_kernel, peers, stride, digits), in...]
    pallas_call x5, Pallas kernels: 13.4 us -> 11.8 us  [the longest x3 6.5 us: backward(): pl.pallas_call(functools.partial(backward_kernel, 256, 1, range(piece * p...]
    ppermute x9 -> x10, waiting for transfers between devices: 4.16 us -> 4.89 us  [swap(): return lax.ppermute(x, axis, [(i, i ^ mask) for i in range(size)])]
    unnamed x23 -> x20, local copies, waits for them, and re-layouts: 0.74 us -> 0.09 us
    ppermute x9 -> x10, starting transfers between devices: 12.5 us -> 12.6 us  [swap(): return lax.ppermute(x, axis, [(i, i ^ mask) for i in range(size)])]
  transfers between devices with their start and end apart: 9 -> 10, of which waited for: 5 -> 5; matrix products, arithmetic and copies ran while one was open for 0% -> 0% of each run, Pallas kernels for 26% -> 25%
where the time goes in v4:
time: 40.6 us; the launch traced here: 40.4 us
  Pallas kernels  21.8 us (54%)
  starting transfers between devices  12.6 us (31%)
  waiting for transfers between devices  4.89 us (12%)
  between operations  0.97 us (2%)
    ppermute x10, starting transfers between devices, swap(): return lax.ppermute(x, axis, [(i, i ^ mask) for i in range(size)])  12.6 us
    pallas_call x3, Pallas kernels, backward(): pl.pallas_call(functools.partial(backward_kernel, 256, 1, range(piece * p...  6.5 us
    pallas_call x1, Pallas kernels, shards(): pl.pallas_call(functools.partial(final_kernel, peers, stride, digits), in...  5.91 us
    ppermute x10, waiting for transfers between devices, swap(): return lax.ppermute(x, axis, [(i, i ^ mask) for i in range(size)])  4.89 us
    pallas_call x1, Pallas kernels, shards(): pl.pallas_call(functools.partial(pick_kernel, peers), grid=(groups,), in_...  4.1 us
    pallas_call x1, Pallas kernels, shards(): pl.pallas_call(functools.partial(forward_kernel, 256, 2), in_specs=[vmem_...  3.58 us
    pallas_call x1, Pallas kernels, shards(): pl.pallas_call(functools.partial(merge_kernel, peers), in_specs=[vmem_spe...  1.71 us
  transfers between devices with their start and end apart: 10, of which 5 were waited for; matrix products, arithmetic and copies ran while one was open for 0% of the time, Pallas kernels for 25%

profile of v4, /device:TPU:0, one launch (start us, length us, event | category | flops | bytes accessed | tf_op | source)
XLA Modules:
  0.0 40.4 jit_solution(7148866192661540248)
XLA Ops:
  0.7 4.1 %pick.1 = (bf16[64,768]{1,0:T(8,128)(2,1)}, bf16[64,768]{1,0:T(8,128)(2,1)}, bf16[16,768]{1,0:T(8,128)(2,1)}, bf16[64,768]{1,0:T(8,128)(2,1)}, bf16[64,768]{1,0:T(8,128)(2,1)}, /*index=5*/bf16[64,768]{1,0:T(8,128)(2,1)}) custom-call(s32[12]{0:T(128)} %near_ref.1, s32[12]{0:T(128)} %far_ref.1, bf16[512,768]{1,0:T(8,128)(2,1)} %q_ref.9, ...), custom_call_target="tpu_custom_call" | custom-call | tf_op jit(solution)/shard_map/pick/pallas_call | solution.py:674
  4.8 3.0 %collective-permute-start = (bf16[64,768]{1,0:T(8,128)(2,1)}, bf16[64,768]{1,0:T(8,128)(2,1)S(1)}, u32[]{:S(2)}, u32[]{:S(2)}) collective-permute-start(bf16[64,768]{1,0:T(8,128)(2,1)} %get-tuple-element.43), channel_id=1, source_target_pairs={{0,8},{8,0},{16,24},{24,16},{1,9},{9,1},{17,25},{25,17},{2,10},{10... | collective-permute-start | bytes 294920 | tf_op jit(solution)/shard_map/ppermute | solution.py:672
  7.8 1.5 %collective-permute-start.1 = (bf16[64,768]{1,0:T(8,128)(2,1)}, bf16[64,768]{1,0:T(8,128)(2,1)S(1)}, u32[]{:S(2)}, u32[]{:S(2)}) collective-permute-start(bf16[64,768]{1,0:T(8,128)(2,1)} %get-tuple-element.44), channel_id=1, source_target_pairs={{0,16},{8,24},{16,0},{24,8},{1,17},{9,25},{17,1},{25,9},{2,18},{10... | collective-permute-start | bytes 294920 | tf_op jit(solution)/shard_map/ppermute | solution.py:672
  9.3 0.0 collective-permute-start.2
  9.3 3.6 %forward.1 = (bf16[512,768]{1,0:T(8,128)(2,1)S(1)}, f32[48,512]{1,0:T(8,128)S(1)}) custom-call(bf16[512,768]{1,0:T(8,128)(2,1)S(1)} %copy-done.2, bf16[512,768]{1,0:T(8,128)(2,1)S(1)} %copy-done, bf16[512,768]{1,0:T(8,128)(2,1)S(1)} %copy-done.1, bf16[512,768]{1,0:T(8,128)(2,1)S(1)} %copy-done.3), custom_call_target="tpu_custom_call" | custom-call | flops 3221225472 | bytes 4718592 | tf_op jit(solution)/shard_map/forward/pallas_call | solution.py:698
  12.9 0.0 collective-permute-done.rest_0_.refs_3_
  12.9 0.7 %collective-permute-done.1.rest_1_.refs_4_ = bf16[64,768]{1,0:T(8,128)(2,1)S(1)} collective-permute-done((bf16[64,768]{1,0:T(8,128)(2,1)}, bf16[64,768]{1,0:T(8,128)(2,1)S(1)}, u32[]{:S(2)}, u32[]{:S(2)}) %collective-permute-start.1) | collective-permute-done | bytes 98336 | tf_op jit(solution)/shard_map/ppermute | solution.py:672
  13.6 1.4 %collective-permute-done.2.rest_2_.refs_5_ = bf16[64,768]{1,0:T(8,128)(2,1)S(1)} collective-permute-done((bf16[64,768]{1,0:T(8,128)(2,1)}, bf16[64,768]{1,0:T(8,128)(2,1)S(1)}, u32[]{:S(2)}, u32[]{:S(2)}) %collective-permute-start.2) | collective-permute-done | bytes 98336 | tf_op jit(solution)/shard_map/ppermute | solution.py:672
  15.0 1.7 %merge.1 = (bf16[16,768]{1,0:T(8,128)(2,1)S(1)}, f32[48,512]{1,0:T(8,128)S(1)}, bf16[32,768]{1,0:T(8,128)(2,1)S(1)}) custom-call(bf16[64,768]{1,0:T(8,128)(2,1)S(1)} %copy-done.4, bf16[64,768]{1,0:T(8,128)(2,1)S(1)} %copy-done.5, bf16[64,768]{1,0:T(8,128)(2,1)S(1)} %collective-permute-done.rest_0_.refs_3_, ...), custom_call_target="tpu_custom_call" | custom-call | tf_op jit(solution)/shard_map/merge/pallas_call | solution.py:708
  16.7 3.7 %collective-permute-start.5 = (bf16[16,768]{1,0:T(8,128)(2,1)S(1)}, bf16[16,768]{1,0:T(8,128)(2,1)S(1)}, u32[]{:S(2)}, u32[]{:S(2)}) collective-permute-start(bf16[16,768]{1,0:T(8,128)(2,1)S(1)} %get-tuple-element.48), channel_id=1, source_target_pairs={{0,6},{1,7},{2,4},{3,5},{4,2},{5,3},{6,0},{7,1},{8,14},{9,15},{10,... | collective-permute-start | bytes 73736 | tf_op jit(solution)/shard_map/ppermute | solution.py:672
  20.4 0.0 collective-permute-start.4
  20.4 0.8 %collective-permute-start.3 = (bf16[16,768]{1,0:T(8,128)(2,1)S(1)}, bf16[16,768]{1,0:T(8,128)(2,1)S(1)}, u32[]{:S(2)}, u32[]{:S(2)}) collective-permute-start(bf16[16,768]{1,0:T(8,128)(2,1)S(1)} %get-tuple-element.48), channel_id=1, source_target_pairs={{0,2},{1,3},{2,0},{3,1},{4,6},{5,7},{6,4},{7,5},{8,10},{9,11},{10,... | collective-permute-start | bytes 73736 | tf_op jit(solution)/shard_map/ppermute | solution.py:672
  21.2 2.2 %backward.3 = (bf16[512,768]{1,0:T(8,128)(2,1)S(1)}, bf16[512,768]{1,0:T(8,128)(2,1)S(1)}, bf16[512,768]{1,0:T(8,128)(2,1)S(1)}) custom-call(bf16[512,768]{1,0:T(8,128)(2,1)S(1)} %copy-done.2, bf16[512,768]{1,0:T(8,128)(2,1)S(1)} %copy-done, bf16[512,768]{1,0:T(8,128)(2,1)S(1)} %copy-done.1, bf16[512,768]{1,0:T(8,128)(2,1)S(1)} %copy-done.3, ...), custom_call_target="tpu_custom_call" | custom-call | flops 2684354560 | bytes 2097152 | tf_op jit(solution)/shard_map/backward/pallas_call | solution.py:723
  23.4 0.0 collective-permute-done.5
  23.4 1.7 %collective-permute-done.4 = bf16[16,768]{1,0:T(8,128)(2,1)S(1)} collective-permute-done((bf16[16,768]{1,0:T(8,128)(2,1)S(1)}, bf16[16,768]{1,0:T(8,128)(2,1)S(1)}, u32[]{:S(2)}, u32[]{:S(2)}) %collective-permute-start.4) | collective-permute-done | bytes 24608 | tf_op jit(solution)/shard_map/ppermute | solution.py:672
  25.2 1.1 %collective-permute-start.8 = (bf16[64,768]{1,0:T(8,128)(2,1)S(1)}, bf16[64,768]{1,0:T(8,128)(2,1)S(1)}, u32[]{:S(2)}, u32[]{:S(2)}) collective-permute-start(bf16[64,768]{1,0:T(8,128)(2,1)S(1)} %get-tuple-element.84), channel_id=1, source_target_pairs={{0,24},{8,16},{16,8},{24,0},{1,25},{9,17},{17,9},{25,1},{2,26},{10... | collective-permute-start | bytes 294920 | tf_op jit(solution)/shard_map/ppermute | solution.py:672
  26.3 1.1 %collective-permute-start.7 = (bf16[64,768]{1,0:T(8,128)(2,1)S(1)}, bf16[64,768]{1,0:T(8,128)(2,1)S(1)}, u32[]{:S(2)}, u32[]{:S(2)}) collective-permute-start(bf16[64,768]{1,0:T(8,128)(2,1)S(1)} %get-tuple-element.84), channel_id=1, source_target_pairs={{0,16},{8,24},{16,0},{24,8},{1,17},{9,25},{17,1},{25,9},{2,18},{10... | collective-permute-start | bytes 294920 | tf_op jit(solution)/shard_map/ppermute | solution.py:672
  27.3 1.4 %collective-permute-start.6 = (bf16[64,768]{1,0:T(8,128)(2,1)S(1)}, bf16[64,768]{1,0:T(8,128)(2,1)S(1)}, u32[]{:S(2)}, u32[]{:S(2)}) collective-permute-start(bf16[64,768]{1,0:T(8,128)(2,1)S(1)} %get-tuple-element.84), channel_id=1, source_target_pairs={{0,8},{8,0},{16,24},{24,16},{1,9},{9,1},{17,25},{25,17},{2,10},{10... | collective-permute-start | bytes 294920 | tf_op jit(solution)/shard_map/ppermute | solution.py:672
  28.7 2.2 %backward.4 = (bf16[512,768]{1,0:T(8,128)(2,1)S(1)}, bf16[512,768]{1,0:T(8,128)(2,1)S(1)}, bf16[512,768]{1,0:T(8,128)(2,1)S(1)}) custom-call(bf16[512,768]{1,0:T(8,128)(2,1)S(1)} %copy-done.2, bf16[512,768]{1,0:T(8,128)(2,1)S(1)} %copy-done, bf16[512,768]{1,0:T(8,128)(2,1)S(1)} %copy-done.1, ...), custom_call_target="tpu_custom_call", output_to_operand_aliasing={{0}: (5, {}), {1}: (6, {}), {2}: (7, {})} | custom-call | flops 2684354560 | bytes 2097152 | tf_op jit(solution)/shard_map/backward/pallas_call | solution.py:723
  30.9 0.9 %collective-permute-done.7 = bf16[64,768]{1,0:T(8,128)(2,1)S(1)} collective-permute-done((bf16[64,768]{1,0:T(8,128)(2,1)S(1)}, bf16[64,768]{1,0:T(8,128)(2,1)S(1)}, u32[]{:S(2)}, u32[]{:S(2)}) %collective-permute-start.7) | collective-permute-done | bytes 98336 | tf_op jit(solution)/shard_map/ppermute | solution.py:672
  31.8 0.1 collective-permute-done.6
  32.0 0.1 collective-permute-start.9
  32.1 2.2 %backward.5 = (bf16[512,768]{1,0:T(8,128)(2,1)S(1)}, bf16[512,768]{1,0:T(8,128)(2,1)S(1)}, bf16[512,768]{1,0:T(8,128)(2,1)S(1)}) custom-call(bf16[512,768]{1,0:T(8,128)(2,1)S(1)} %copy-done.2, bf16[512,768]{1,0:T(8,128)(2,1)S(1)} %copy-done, bf16[512,768]{1,0:T(8,128)(2,1)S(1)} %copy-done.1, ...), custom_call_target="tpu_custom_call", output_to_operand_aliasing={{0}: (5, {}), {1}: (6, {}), {2}: (7, {})} | custom-call | flops 2684354560 | bytes 2097152 | tf_op jit(solution)/shard_map/backward/pallas_call | solution.py:723
  34.3 5.9 %final.1 = (bf16[512,768]{1,0:T(8,128)(2,1)}, bf16[512,768]{1,0:T(8,128)(2,1)}, bf16[512,768]{1,0:T(8,128)(2,1)}, bf16[512,768]{1,0:T(8,128)(2,1)}) custom-call(bf16[16,768]{1,0:T(8,128)(2,1)S(1)} %copy-done.6, bf16[512,768]{1,0:T(8,128)(2,1)S(1)} %constant_dynamic-update-slice_fusion.11.refs_0_, bf16[64,768]{1,0:T(8,128)(2,1)S(1)} %copy-done.4, ...), custom_call_target="tpu_custom_call" | custom-call | tf_op jit(solution)/shard_map/final/pallas_call | solution.py:762
  (25 shorter events, 0.1 us)
Async XLA Ops:
  0.6 8.7 %copy-start.1 = (bf16[512,768]{1,0:T(8,128)(2,1)S(1)}, bf16[512,768]{1,0:T(8,128)(2,1)}, u32[]{:S(2)}) copy-start(bf16[512,768]{1,0:T(8,128)(2,1)} %refs_7_.1) | copy-start | bytes 2359300
  0.6 8.7 %copy-start = (bf16[512,768]{1,0:T(8,128)(2,1)S(1)}, bf16[512,768]{1,0:T(8,128)(2,1)}, u32[]{:S(2)}) copy-start(bf16[512,768]{1,0:T(8,128)(2,1)} %refs_6_.1) | copy-start | bytes 2359300
  0.7 8.7 %copy-start.3 = (bf16[512,768]{1,0:T(8,128)(2,1)S(1)}, bf16[512,768]{1,0:T(8,128)(2,1)}, u32[]{:S(2)}) copy-start(bf16[512,768]{1,0:T(8,128)(2,1)} %g_ref.9) | copy-start | bytes 2359300
  0.7 8.7 %copy-start.2 = (bf16[512,768]{1,0:T(8,128)(2,1)S(1)}, bf16[512,768]{1,0:T(8,128)(2,1)}, u32[]{:S(2)}) copy-start(bf16[512,768]{1,0:T(8,128)(2,1)} %q_ref.9) | copy-start | bytes 2359300
  4.8 8.2 %collective-permute-start = (bf16[64,768]{1,0:T(8,128)(2,1)}, bf16[64,768]{1,0:T(8,128)(2,1)S(1)}, u32[]{:S(2)}, u32[]{:S(2)}) collective-permute-start(bf16[64,768]{1,0:T(8,128)(2,1)} %get-tuple-element.43), channel_id=1, source_target_pairs={{0,8},{8,0},{16,24},{24,16},{1,9},{9,1},{17,25},{25,17},{2,10},{10... | collective-permute-start | bytes 294920 | tf_op jit(solution)/shard_map/ppermute | solution.py:672
  7.8 5.9 %collective-permute-start.1 = (bf16[64,768]{1,0:T(8,128)(2,1)}, bf16[64,768]{1,0:T(8,128)(2,1)S(1)}, u32[]{:S(2)}, u32[]{:S(2)}) collective-permute-start(bf16[64,768]{1,0:T(8,128)(2,1)} %get-tuple-element.44), channel_id=1, source_target_pairs={{0,16},{8,24},{16,0},{24,8},{1,17},{9,25},{17,1},{25,9},{2,18},{10... | collective-permute-start | bytes 294920 | tf_op jit(solution)/shard_map/ppermute | solution.py:672
  9.3 5.7 %copy-start.4 = (bf16[64,768]{1,0:T(8,128)(2,1)S(1)}, bf16[64,768]{1,0:T(8,128)(2,1)}, u32[]{:S(2)}) copy-start(bf16[64,768]{1,0:T(8,128)(2,1)} %get-tuple-element.41.kv_ref.refs_1_) | copy-start | bytes 294916
  9.3 5.7 %copy-start.5 = (bf16[64,768]{1,0:T(8,128)(2,1)S(1)}, bf16[64,768]{1,0:T(8,128)(2,1)}, u32[]{:S(2)}) copy-start(bf16[64,768]{1,0:T(8,128)(2,1)} %get-tuple-element.42.qg_ref.refs_2_) | copy-start | bytes 294916
  9.3 5.7 %collective-permute-start.2 = (bf16[64,768]{1,0:T(8,128)(2,1)}, bf16[64,768]{1,0:T(8,128)(2,1)S(1)}, u32[]{:S(2)}, u32[]{:S(2)}) collective-permute-start(bf16[64,768]{1,0:T(8,128)(2,1)} %get-tuple-element.45), channel_id=1, source_target_pairs={{0,24},{8,16},{16,8},{24,0},{1,25},{9,17},{17,9},{25,1},{2,26},{10... | collective-permute-start | bytes 294920 | tf_op jit(solution)/shard_map/ppermute | solution.py:672
  9.3 5.7 %copy-start.6 = (bf16[16,768]{1,0:T(8,128)(2,1)S(1)}, bf16[16,768]{1,0:T(8,128)(2,1)}, u32[]{:S(2)}) copy-start(bf16[16,768]{1,0:T(8,128)(2,1)} %get-tuple-element.40.rest_5_.fr_ref) | copy-start | bytes 73732
  16.7 6.6 %collective-permute-start.5 = (bf16[16,768]{1,0:T(8,128)(2,1)S(1)}, bf16[16,768]{1,0:T(8,128)(2,1)S(1)}, u32[]{:S(2)}, u32[]{:S(2)}) collective-permute-start(bf16[16,768]{1,0:T(8,128)(2,1)S(1)} %get-tuple-element.48), channel_id=1, source_target_pairs={{0,6},{1,7},{2,4},{3,5},{4,2},{5,3},{6,0},{7,1},{8,14},{9,15},{10,... | collective-permute-start | bytes 73736 | tf_op jit(solution)/shard_map/ppermute | solution.py:672
  20.4 4.7 %collective-permute-start.4 = (bf16[16,768]{1,0:T(8,128)(2,1)S(1)}, bf16[16,768]{1,0:T(8,128)(2,1)S(1)}, u32[]{:S(2)}, u32[]{:S(2)}) collective-permute-start(bf16[16,768]{1,0:T(8,128)(2,1)S(1)} %get-tuple-element.48), channel_id=1, source_target_pairs={{0,4},{1,5},{2,6},{3,7},{4,0},{5,1},{6,2},{7,3},{8,12},{9,13},{10,... | collective-permute-start | bytes 73736 | tf_op jit(solution)/shard_map/ppermute | solution.py:672
  20.4 4.7 %collective-permute-start.3 = (bf16[16,768]{1,0:T(8,128)(2,1)S(1)}, bf16[16,768]{1,0:T(8,128)(2,1)S(1)}, u32[]{:S(2)}, u32[]{:S(2)}) collective-permute-start(bf16[16,768]{1,0:T(8,128)(2,1)S(1)} %get-tuple-element.48), channel_id=1, source_target_pairs={{0,2},{1,3},{2,0},{3,1},{4,6},{5,7},{6,4},{7,5},{8,10},{9,11},{10,... | collective-permute-start | bytes 73736 | tf_op jit(solution)/shard_map/ppermute | solution.py:672
  25.2 5.7 %collective-permute-start.8 = (bf16[64,768]{1,0:T(8,128)(2,1)S(1)}, bf16[64,768]{1,0:T(8,128)(2,1)S(1)}, u32[]{:S(2)}, u32[]{:S(2)}) collective-permute-start(bf16[64,768]{1,0:T(8,128)(2,1)S(1)} %get-tuple-element.84), channel_id=1, source_target_pairs={{0,24},{8,16},{16,8},{24,0},{1,25},{9,17},{17,9},{25,1},{2,26},{10... | collective-permute-start | bytes 294920 | tf_op jit(solution)/shard_map/ppermute | solution.py:672
  26.3 5.5 %collective-permute-start.7 = (bf16[64,768]{1,0:T(8,128)(2,1)S(1)}, bf16[64,768]{1,0:T(8,128)(2,1)S(1)}, u32[]{:S(2)}, u32[]{:S(2)}) collective-permute-start(bf16[64,768]{1,0:T(8,128)(2,1)S(1)} %get-tuple-element.84), channel_id=1, source_target_pairs={{0,16},{8,24},{16,0},{24,8},{1,17},{9,25},{17,1},{25,9},{2,18},{10... | collective-permute-start | bytes 294920 | tf_op jit(solution)/shard_map/ppermute | solution.py:672
  27.3 4.6 %collective-permute-start.6 = (bf16[64,768]{1,0:T(8,128)(2,1)S(1)}, bf16[64,768]{1,0:T(8,128)(2,1)S(1)}, u32[]{:S(2)}, u32[]{:S(2)}) collective-permute-start(bf16[64,768]{1,0:T(8,128)(2,1)S(1)} %get-tuple-element.84), channel_id=1, source_target_pairs={{0,8},{8,0},{16,24},{24,16},{1,9},{9,1},{17,25},{25,17},{2,10},{10... | collective-permute-start | bytes 294920 | tf_op jit(solution)/shard_map/ppermute | solution.py:672
  32.0 2.3 %collective-permute-start.9 = (bf16[256,768]{1,0:T(8,128)(2,1)S(1)}, bf16[256,768]{1,0:T(8,128)(2,1)S(1)}, u32[]{:S(2)}, u32[]{:S(2)}) collective-permute-start(bf16[256,768]{1,0:T(8,128)(2,1)S(1)} %get-tuple-element.76), channel_id=1, source_target_pairs={{0,1},{1,0},{2,3},{3,2},{4,5},{5,4},{6,7},{7,6},{8,9},{9,8},{10,11... | collective-permute-start | bytes 1179656 | tf_op jit(solution)/shard_map/ppermute | solution.py:672

commit v5 on v4

--- a/solution.py
+++ b/solution.py
@@ -26,6 +26,14 @@
 PICK_LIMIT = 58
 
 
+def div(x, by):
+    return x >> (by.bit_length() - 1) if by & (by - 1) == 0 else lax.div(x, jnp.int32(by))
+
+
+def mod(x, by):
+    return x & (by - 1) if by & (by - 1) == 0 else lax.rem(x, jnp.int32(by))
+
+
 def iota(shape, axis):
     return lax.broadcasted_iota(jnp.int32, shape, axis)
 
@@ -47,7 +55,7 @@
 
 
 def lane_offsets(ref, group):
-    head = iota((1, GW), 1) // HD
+    head = div(iota((1, GW), 1), HD)
     out = jnp.zeros((1, GW), jnp.int32)
     for h in range(GH):
         out = jnp.where(head == h, ref[group * GH + h], out)
@@ -55,13 +63,13 @@
 
 
 def expand(x):
-    head = iota((1, GW), 1) // HD
+    head = div(iota((1, GW), 1), HD)
     return jnp.concatenate([x * onehot(head == h) for h in range(GH)], axis=0)
 
 
 def collapse(x):
     n = x.shape[0] // GH
-    head = iota((1, GW), 1) // HD
+    head = div(iota((1, GW), 1), HD)
     out = x[:n]
     for h in range(1, GH):
         out = jnp.where(head == h, x[h * n : (h + 1) * n], out)
@@ -77,7 +85,7 @@
 
 
 def pack_aux(log_total, row_dot):
-    lane = iota((1, log_total.shape[1]), 1) % HD
+    lane = mod(iota((1, log_total.shape[1]), 1), HD)
     out = jnp.zeros(log_total.shape, F32)
     for at, piece in enumerate(split3(log_total) + split3(row_dot)):
         out = jnp.where(lane == at, piece, out)
@@ -85,37 +93,37 @@
 
 
 def spread_sum(x, width):
-    block = onehot(iota((width, width), 0) // HD == iota((width, width), 1) // HD)
+    block = onehot(div(iota((width, 1), 0), HD) == div(iota((1, width), 1), HD))
     hi = x.astype(BF)
     low = (x - hi.astype(F32)).astype(BF)
     return nn(hi, block) + nn(low, block)
 
 
 def piece_column(aux_expanded, which):
-    a = iota((GW, 128), 0)
+    a = iota((GW, 1), 0)
     return nn(aux_expanded, onehot(a % HD // 3 == which))[:, :1]
 
 
 def near_select(n, length):
-    return onehot(iota((n, length), 1) // R2 == iota((n, length), 0))
+    return onehot(div(iota((1, length), 1), R2) == iota((n, 1), 0))
 
 
 def near_place(n, length):
-    return onehot(iota((length, n), 0) // R2 == iota((length, n), 1))
+    return onehot(iota((length, 1), 0) // R2 == iota((1, n), 1))
 
 
 def far_select(rows, length, first):
-    return onehot(iota((rows, length), 1) // R3 == iota((rows, length), 0) - first)
+    return onehot(div(iota((1, length), 1), R3) == iota((rows, 1), 0) - first)
 
 
 def far_place(length):
-    return onehot(iota((length, FM), 0) // R3 == iota((length, FM), 1))
+    return onehot(iota((length, 1), 0) // R3 == iota((1, FM), 1))
 
 
 def token_masks(near_ref, far_ref, group, length):
-    t = iota((length, GW), 0)
-    near = t % R2 == lane_offsets(near_ref, group)
-    far = t % R3 == lane_offsets(far_ref, group)
+    t = iota((length, 1), 0)
+    near = mod(t, R2) == lane_offsets(near_ref, group)
+    far = mod(t, R3) == lane_offsets(far_ref, group)
     return near, far
 
 
@@ -136,10 +144,10 @@
 
 def head_rows(n, stride, length, ref, group):
     r = iota((GH * n, 1), 0)
-    token = r % n * stride
+    token = mod(r, n) * stride
     for h in range(GH):
-        token = jnp.where(r // n == h, token + ref[group * GH + h], token)
-    return onehot(iota((GH * n, length), 1) == token)
+        token = jnp.where(div(r, n) == h, token + ref[group * GH + h], token)
+    return onehot(iota((1, length), 1) == token)
 
 
 def pick_kernel(peers, near_ref, far_ref, q_ref, k_ref, v_ref, g_ref, kv_ref, qg_ref, fr_ref, *msg_refs):
@@ -198,7 +206,7 @@
 
 
 def eye_of(n):
-    return onehot(iota((n, n), 0) == iota((n, n), 1))
+    return onehot(iota((n, 1), 0) == iota((1, n), 1))
 
 
 def pair_columns(p):
@@ -208,7 +216,7 @@
 def forward_kernel(strip, skew, q_ref, k_ref, v_ref, g_ref, att_ref, st_ref):
     length, width = q_ref.shape
     _, in_head = head_masks()
-    diag = iota((strip, strip), 0) <= iota((strip, strip), 1)
+    diag = iota((strip, 1), 0) <= iota((1, strip), 1)
     eye = eye_of(PW)
     kept = {}
 
@@ -249,14 +257,14 @@
 
 
 def near_valid_queries(shape, n, own):
-    row, lane = iota(shape, 0) % n, iota(shape, 1)
-    slot, key = lane // n, lane % n
+    row, lane = mod(iota((shape[0], 1), 0), n), iota((1, shape[1]), 1)
+    slot, key = div(lane, n), mod(lane, n)
     return ((slot ^ own) < own) | ((slot == 0) & (key <= row))
 
 
 def near_valid_keys(shape, n, own):
-    row, lane = iota(shape, 0) % n, iota(shape, 1)
-    slot, query = lane // n, lane % n
+    row, lane = mod(iota((shape[0], 1), 0), n), iota((1, shape[1]), 1)
+    slot, query = div(lane, n), mod(lane, n)
     return ((slot ^ own) > own) | ((slot == 0) & (row <= query))
 
 
@@ -264,8 +272,8 @@
 
 
 def stat_row(shape, axis):
-    r = iota(shape, axis) % SR
-    return r // 8 * 2 + r % 2, r % 8 // 2
+    r = mod(iota((shape[0], 1), axis), SR)
+    return div(r, 8) * 2 + mod(r, 2), div(mod(r, 8), 2)
 
 
 def stat_offsets(ref, group):
@@ -285,23 +293,23 @@
 
 
 def pack_lanes(group):
-    l, m = iota((GW, 128), 0), iota((GW, 128), 1)
-    return onehot((l % HD < 6) & (m == (group * GH + l // HD) * 6 + l % HD))
+    l, m = iota((GW, 1), 0), iota((1, 128), 1)
+    return onehot((mod(l, HD) < 6) & (m == (group * GH + div(l, HD)) * 6 + mod(l, HD)))
 
 
 def unpack_lanes(group):
-    l, m = iota((128, GW), 1), iota((128, GW), 0)
-    return onehot((l % HD < 6) & (m == (group * GH + l // HD) * 6 + l % HD))
+    l, m = iota((1, GW), 1), iota((128, 1), 0)
+    return onehot((mod(l, HD) < 6) & (m == (group * GH + div(l, HD)) * 6 + mod(l, HD)))
 
 
 def unpack_rows(peers, stride, n, f, fa_ref):
     per = fa_ref.shape[1] // 128
     rows = peers * stride * FM
-    r, c = iota((peers * n, rows), 0), iota((peers * n, rows), 1)
-    at_row = c == r // n * (stride * FM) + 5 * f + r % n // per
+    r, c = iota((peers * n, 1), 0), iota((1, rows), 1)
+    at_row = c == div(r, n) * (stride * FM) + 5 * f + div(mod(r, n), per)
     out = jnp.zeros((peers * n, 128), F32)
     for at in range(per):
-        out += nn(onehot(at_row & (r % n % per == at)), fa_ref[:rows, at * 128 : (at + 1) * 128])
+        out += nn(onehot(at_row & (mod(mod(r, n), per) == at)), fa_ref[:rows, at * 128 : (at + 1) * 128])
     return out.astype(BF)
 
 
@@ -318,9 +326,9 @@
     s = nt(expand(qg_ref[:n, cols] * jnp.asarray(SCALE, BF)), keys)
     yield
     st = st_ref[srows, :]
-    t = iota((SR, length), 1)
-    near_st = t % R2 == stat_offsets(near_ref, group)
-    far_st = t % R3 == stat_offsets(far_ref, group)
+    t = iota((1, length), 1)
+    near_st = mod(t, R2) == stat_offsets(near_ref, group)
+    far_st = mod(t, R3) == stat_offsets(far_ref, group)
     sel = near_select(n, length)
     log1 = nt(sel, pieces3(jnp.where(near_st, st, 0.0)))
     out1 = collapse(nn(head_rows(n, R2, length, near_ref, group), att_ref[:, cols]))
@@ -332,8 +340,8 @@
     total = jnp.sum(w, axis=1, keepdims=True)
     out2 = nn(w.astype(BF), values)
     head, what = stat_row((3 * SR, GW), 0)
-    lane = iota((3 * SR, GW), 1)
-    log1 = nn(log1.astype(BF), onehot((lane // HD == head) & (what == 0)))
+    lane = iota((1, GW), 1)
+    log1 = nn(log1.astype(BF), onehot((div(lane, HD) == head) & (what == 0)))
     yield
     out2 = collapse(out2 / total)
     log2 = collapse(jnp.broadcast_to(top + jnp.log(total), (GH * n, GW)))
@@ -348,10 +356,10 @@
     aux12 = pack_aux(log12, dot12).astype(BF)
     packs.append(nn(aux12, pack_lanes(group)))
     head, what = stat_row((SR, GW), 0)
-    lane = iota((SR, GW), 1)
-    compact = nt(onehot((lane // HD == head) & (lane % HD // 3 == what)), aux12)
-    yield
-    place = onehot(iota((n, length), 1) // R2 == iota((n, length), 0))
+    lane = iota((1, GW), 1)
+    compact = nt(onehot((div(lane, HD) == head) & (div(mod(lane, HD), 3) == what)), aux12)
+    yield
+    place = onehot(div(iota((1, length), 1), R2) == iota((n, 1), 0))
     placed = nn(pieces3(compact), place)
     yield
     placed = placed[:SR] + placed[SR : 2 * SR] + placed[2 * SR :]
@@ -360,8 +368,8 @@
     far_aux = nt(far_select(FM, length, 4 * f), pieces3(jnp.where(far_st, st, 0.0)))
     yield
     head, what = stat_row((3 * SR, GW), 0)
-    lane, piece = iota((3 * SR, GW), 1), iota((3 * SR, GW), 0) // SR
-    far_aux = nn(far_aux.astype(BF), onehot((lane // HD == head) & (lane % HD == what * 3 + piece)))
+    lane, piece = iota((1, GW), 1), div(iota((3 * SR, 1), 0), SR)
+    far_aux = nn(far_aux.astype(BF), onehot((div(lane, HD) == head) & (mod(lane, HD) == what * 3 + piece)))
     raw = fr_ref[:, cols].astype(F32)
     blocks[group] = jnp.where(iota(raw.shape, 0) < 4 * f, raw, 0.0) + far_aux
 
@@ -378,10 +386,10 @@
     packed = sum(packs[1:], packs[0]).astype(BF)
     n, length = packed.shape[0], rest[1].shape[0]
     per = out_ref.shape[1] // 128
-    r, c = iota((FM, n), 0) - 5 * (length // R3), iota((FM, n), 1)
+    r, c = iota((FM, 1), 0) - 5 * (length // R3), iota((1, n), 1)
     for at in range(per):
         block = blocks[at * 128 // GW][:, at * 128 % GW :][:, :128]
-        rows = nn(onehot((c // per == r) & (c % per == at)), packed)
+        rows = nn(onehot((div(c, per) == r) & (mod(c, per) == at)), packed)
         out_ref[:, at * 128 : (at + 1) * 128] = (block + rows).astype(BF)
 
 
@@ -389,7 +397,7 @@
     dq_ref, dk_ref, dv_ref = rest[aliased:]
     length = q_ref.shape[0]
     first, in_head = head_masks()
-    diag = iota((strip, strip), 0) <= iota((strip, strip), 1)
+    diag = iota((strip, 1), 0) <= iota((1, strip), 1)
     eye = eye_of(PW)
     strips = length // strip
     kept = {}
@@ -433,19 +441,19 @@
 
 
 def far_seq(index, f, digits, own):
-    slot = index // f
+    slot = div(index, f)
     seq = own
     for radix, unit in digits:
-        seq = seq ^ (slot % radix * unit)
-        slot = slot // radix
-    return seq * f + index % f
+        seq = seq ^ (mod(slot, radix) * unit)
+        slot = div(slot, radix)
+    return seq * f + mod(index, f)
 
 
 def row_offsets(n, ref, group):
     r = iota((GH * n, 1), 0)
     out = jnp.zeros((GH * n, 1), jnp.int32)
     for h in range(GH):
-        out = jnp.where(r // n == h, ref[group * GH + h], out)
+        out = jnp.where(div(r, n) == h, ref[group * GH + h], out)
     return out
 
 
@@ -453,26 +461,93 @@
     parts = []
     for count, stride, ref in ((n, R2, near_ref), (FM, R3, far_ref)):
         c = iota((1, GH * count), 1)
-        token = c % count * stride
+        token = mod(c, count) * stride
         for h in range(GH):
-            token = jnp.where(c // count == h, token + ref[group * GH + h], token)
+            token = jnp.where(div(c, count) == h, token + ref[group * GH + h], token)
         parts.append(token)
-    return onehot(iota((length, GH * (n + FM)), 0) == jnp.concatenate(parts, axis=1))
+    return onehot(iota((length, 1), 0) == jnp.concatenate(parts, axis=1))
 
 
 def own_lanes(x):
     n = x.shape[0] // GH
-    return jnp.where(iota(x.shape, 1) // HD == iota(x.shape, 0) // n, x, 0.0)
+    return jnp.where(div(iota((1, x.shape[1]), 1), HD) == div(iota((x.shape[0], 1), 0), n), x, 0.0)
 
 
 def piece_columns(aux_expanded):
-    a, c = iota((GW, 256), 0), iota((GW, 256), 1)
-    both = nn(aux_expanded, onehot(a % HD // 3 == c // 128))
+    a, c = iota((GW, 1), 0), iota((1, 256), 1)
+    both = nn(aux_expanded, onehot(div(mod(a, HD), 3) == div(c, 128)))
     return both[:, :1], both[:, 128:129]
 
 
+def near_group(peers, group, fr_ref, packed, kv_ref, qg_ref, got, dq_ref, dk_ref, dv_ref):
+    cols = group_columns(group)
+    n = dq_ref.shape[0]
+    f = n * R2 // R3
+    near_ref, far_ref = read_offsets(fr_ref, f, group)
+    own = lax.axis_index("row") % peers
+    keys, values, queries, grads = near_operands(n, cols, kv_ref, qg_ref, got)
+    naux = nn(packed(), unpack_lanes(group))
+    s = nt(expand(queries[:n]), keys)
+    dp = nt(expand(grads[:n]), values)
+    yield
+    s2 = nt(expand(keys[:n]), queries)
+    dp2 = nt(expand(values[:n]), grads)
+    noff, foff = lane_offsets(near_ref, group), lane_offsets(far_ref, group)
+    also_far = (mod(iota((naux.shape[0], 1), 0), R3 // R2) == div(foff, R2)) & (mod(foff, R2) == noff)
+    none = jnp.where(mod(iota((1, GW), 1), HD) == 0, -NEG, 0.0)
+    naux = jnp.where(also_far, none, naux).astype(BF)
+    yield
+    log_q, dot_q = piece_columns(expand(naux[:n]))
+    log_k, dot_k = piece_rows(n, naux)
+    yield
+    ok = near_valid_queries(s.shape, n, own)
+    p = jnp.where(ok, jnp.exp(s - log_q), 0.0)
+    ds = (p * (dp - dot_q)).astype(BF)
+    yield
+    ok = near_valid_keys(s2.shape, n, own)
+    p = jnp.where(ok, jnp.exp(s2 - log_k), 0.0)
+    ds2 = (p * (dp2 - dot_k)).astype(BF)
+    yield
+    dq_ref[:, cols] = (collapse(nn(ds, keys)) * SCALE).astype(BF)
+    yield
+    dk_ref[:, cols] = collapse(nn(ds2, queries)).astype(BF)
+    dv_ref[:, cols] = collapse(nn(p.astype(BF), grads)).astype(BF)
+
+
+def near_kernel(peers, stride, fr_ref, fa_ref, kv_ref, qg_ref, *rest):
+    got, outs = rest[: peers - 1], rest[peers - 1 :]
+    n, width = outs[0].shape
+    made = []
+
+    def packed():
+        if not made:
+            made.append(unpack_rows(peers, stride, n, n * R2 // R3, fa_ref))
+        return made[0]
+
+    lockstep(
+        near_group(peers, group, fr_ref, packed, kv_ref, qg_ref, got, *outs) for group in range(width // GW)
+    )
+
+
+def near_operands(n, cols, kv_ref, qg_ref, got):
+    heads = [kv_ref, *got]
+    keys = jnp.concatenate([x[:n, cols] for x in heads], axis=0)
+    values = jnp.concatenate([x[n:, cols] for x in heads], axis=0)
+    heads = [qg_ref, *got]
+    queries = jnp.concatenate([x[:n, cols] for x in heads], axis=0) * jnp.asarray(SCALE, BF)
+    grads = jnp.concatenate([x[n:, cols] for x in heads], axis=0)
+    return keys, values, queries, grads
+
+
+def piece_rows(n, aux):
+    r, c = iota((2 * GH * n, 1), 0), iota((1, GW), 1)
+    head, which = div(mod(r, GH * n), n), div(r, GH * n)
+    both = nt(onehot((div(c, HD) == head) & (div(mod(c, HD), 3) == which)), aux)
+    return both[: GH * n], both[GH * n :]
+
+
 def final_group(
-    peers, stride, digits, group, fr_ref, got, packed, fa_ref, k_ref, v_ref, base, near_out, outs, done
+    peers, stride, digits, group, fr_ref, got, fa_ref, k_ref, v_ref, base, near_out, near_grads, outs, done
 ):
     kv_ref, qg_ref, got = got[0], got[1], got[2:]
     cols = group_columns(group)
@@ -486,9 +561,9 @@
     seq = lax.axis_index("col") * lax.axis_size("row") + row_here
     scale = jnp.asarray(SCALE, BF)
 
-    r, c = iota((5 * F, blocks * FM), 0), iota((5 * F, blocks * FM), 1)
-    i, at = r // F, r % F
-    sel = onehot(c == at // f * FM + i * f + at % f)
+    r, c = iota((5 * F, 1), 0), iota((1, blocks * FM), 1)
+    i, at = div(r, F), mod(r, F)
+    sel = onehot(c == div(at, f) * FM + i * f + mod(at, f))
     fa = nn(sel, fa_ref[:, cols])
     yield
     fa = fa.astype(BF)
@@ -498,18 +573,12 @@
     dp = nt(gx, fv)
     log12, dot12 = piece_columns(ax)
     yield
-    heads = [kv_ref, *got]
-    keys = jnp.concatenate([x[:n, cols] for x in heads], axis=0)
-    values = jnp.concatenate([x[n:, cols] for x in heads], axis=0)
-    heads = [qg_ref, *got]
-    queries = jnp.concatenate([x[:n, cols] for x in heads], axis=0) * scale
-    grads = jnp.concatenate([x[n:, cols] for x in heads], axis=0)
-    naux = nn(packed(), unpack_lanes(group))
-    near_s = nt(expand(queries[:n]), keys)
-    near_dp = nt(expand(grads[:n]), values)
-    near_s2 = nt(expand(keys[:n]), queries)
-    near_dp2 = nt(expand(values[:n]), grads)
-    place_q = far_seq(iota((GH * F, 1), 0) % F, f, digits, seq)
+    keys, values, _, _ = near_operands(n, cols, kv_ref, qg_ref, got)
+    kx, vx = expand(keys[:n]), expand(values[:n])
+    fq = fq * scale
+    part = peers * stride * f
+    key_s, key_dp = nt(kx, fq[:part]), nt(vx, fg[:part])
+    place_q = far_seq(mod(iota((GH * F, 1), 0), F), f, digits, seq)
     place_k = far_seq(iota((1, F), 1), f, digits, seq)
     s = jnp.where(place_k <= place_q, s, NEG)
     top = jnp.max(s, axis=1, keepdims=True)
@@ -523,13 +592,13 @@
         return jnp.concatenate([x[h * F : h * F + FM] for h in range(GH)], axis=0)
 
     qo, go = own_rows(qx), own_rows(gx)
-    local_s = nt(qo, k)
-    local_dp = nt(go, v)
+    local_s, local_dp = nt(qo, k), nt(go, v)
+    near_s, near_dp = nt(qo, keys), nt(go, values)
     roff, rnear = row_offsets(FM, far_ref, group), row_offsets(FM, near_ref, group)
-    token = iota((GH * FM, 1), 0) % FM * R3 + roff
-    att_far = nn(onehot(iota((GH * FM, length), 1) == token), base[0][:, cols])
-    near_far = nn(onehot(iota((GH * FM, n), 1) * R2 + rnear == token), near_out[:, cols])
-    att_far = jnp.where(roff % R2 == rnear, near_far, att_far)
+    token = mod(iota((GH * FM, 1), 0), FM) * R3 + roff
+    att_far = nn(onehot(iota((1, length), 1) == token), base[0][:, cols])
+    near_far = nn(onehot(iota((1, n), 1) * R2 + rnear == token), near_out[:, cols])
+    att_far = jnp.where(mod(roff, R2) == rnear, near_far, att_far)
     yield
     log3 = top + jnp.log(total)
     dot3 = dot3 / total
@@ -543,55 +612,56 @@
     pb, dsb = p.astype(BF), ds.astype(BF)
     log_own, dot_own, keep = own_rows(log_all), own_rows(dot_all), own_rows(e12 / both)
     yield
-    final_aux = collapse(
-        pack_aux(jnp.broadcast_to(log_all, (GH * F, GW)), jnp.broadcast_to(dot_all, (GH * F, GW)))
+    final_aux = pack_aux(
+        *(collapse(jnp.broadcast_to(x, (GH * F, GW)))[:part] for x in (log_all, dot_all))
     ).astype(BF)
-    rows = peers * n
-    r, c = iota((rows, F), 0), iota((rows, F), 1)
-    subst = nn(onehot(c == r // n * (stride * f) + r % n * R2 // R3), final_aux)
     far_out = own_lanes(nn(own_rows(pb), fv) + keep * att_far)
     far_dq = nn(own_rows(dsb), fk)
     far_dv = tn(pb, gx)[:FM]
     far_dk = tn(dsb, qx)[:FM]
     yield
     r = iota((GH * FM, 1), 0)
-    reach = jnp.where(r % FM < f, token, -1)
-    ok = iota((GH * FM, length), 1) <= reach
+    reach = jnp.where(mod(r, FM) < f, token, -1)
+    ok = iota((1, length), 1) <= reach
     p = jnp.where(ok, jnp.exp(local_s - log_own), 0.0)
     ds = (p * (local_dp - dot_own)).astype(BF)
     pb = p.astype(BF)
-    noff, foff = lane_offsets(near_ref, group), lane_offsets(far_ref, group)
-    also_far = (iota((rows, GW), 0) % (R3 // R2) == foff // R2) & (foff % R2 == noff)
-    naux = jnp.where(also_far, subst, naux).astype(BF)
-    yield
-    log_q, dot_q = piece_columns(expand(naux[:n]))
-    r, c = iota((2 * GH * n, GW), 0), iota((2 * GH * n, GW), 1)
-    head, which = r % (GH * n) // n, r // (GH * n)
-    stats = nt(onehot((c // HD == head) & (c % HD // 3 == which)), naux)
-    log_k, dot_k = stats[: GH * n], stats[GH * n :]
+    twice = mod(roff, R2) == rnear
+    c = iota((1, peers * n), 1)
+    slot = div(c, n)
+    ok = twice & (reach >= 0) & (((slot ^ own) < own) | ((slot == 0) & (mod(c, n) <= div(reach, R2))))
+    np = jnp.where(ok, jnp.exp(near_s - log_own), 0.0)
+    nds = (np * (near_dp - dot_own)).astype(BF)
+    yield
+    log_k, dot_k = piece_rows(n, final_aux)
+    far_dq += nn(nds, keys)
     far_dq = own_lanes(far_dq + nn(ds, k))
     place = place_columns(n, length, near_ref, far_ref, group)
-    alone = jnp.where(also_far[:n], 0.0, near_out[:, cols].astype(F32)).astype(BF)
+    noff, foff = lane_offsets(near_ref, group), lane_offsets(far_ref, group)
+    also_far = (mod(iota((n, 1), 0), R3 // R2) == div(foff, R2)) & (mod(foff, R2) == noff)
+    alone = jnp.where(also_far, 0.0, near_out[:, cols].astype(F32)).astype(BF)
     placed = nn(place, jnp.concatenate([expand(alone), far_out.astype(BF)], axis=0))
     yield
     near, far = token_masks(near_ref, far_ref, group, length)
     outs[0][:, cols] = jnp.where(near | far, placed, base[0][:, cols].astype(F32)).astype(BF)
     done(0, cols)
     yield
-    ok = near_valid_queries(near_s.shape, n, own)
-    np = jnp.where(ok, jnp.exp(near_s - log_q), 0.0)
-    nds = (np * (near_dp - dot_q)).astype(BF)
-    ok = near_valid_keys(near_s2.shape, n, own)
-    np2 = jnp.where(ok, jnp.exp(near_s2 - log_k), 0.0)
-    nds2 = (np2 * (near_dp2 - dot_k)).astype(BF)
+    koff, knear = row_offsets(n, far_ref, group), row_offsets(n, near_ref, group)
+    c = iota((1, part), 1)
+    slot = div(c, f)
+    other = div(slot, stride)
+    late = ((other ^ own) > own) | ((other == 0) & (mod(iota((GH * n, 1), 0), n) <= div(mod(c, f) * R3 + koff, R2)))
+    ok = (mod(koff, R2) == knear) & (mod(slot, stride) == 0) & late
+    np = jnp.where(ok, jnp.exp(key_s - log_k), 0.0)
+    nds = (np * (key_dp - dot_k)).astype(BF)
     dk = tn(ds, qo)
     dv = tn(pb, go)
     yield
-    near_dq = own_lanes(nn(nds, keys))
-    near_dk = own_lanes(nn(nds2, queries))
-    near_dv = own_lanes(nn(np2.astype(BF), grads))
-    yield
-    terms = nn(place, (jnp.concatenate([near_dq, far_dq], axis=0) * SCALE).astype(BF))
+    near_dq = expand(near_grads[0][:, cols]).astype(F32)
+    near_dk = own_lanes(nn(nds, fq[:part])) + expand(near_grads[1][:, cols]).astype(F32)
+    near_dv = own_lanes(nn(np.astype(BF), fg[:part])) + expand(near_grads[2][:, cols]).astype(F32)
+    yield
+    terms = nn(place, jnp.concatenate([near_dq, far_dq * SCALE], axis=0).astype(BF))
     outs[1][:, cols] = (base[1][:, cols].astype(F32) + terms).astype(BF)
     done(1, cols)
     yield
@@ -606,16 +676,9 @@
 
 def final_kernel(peers, stride, digits, fr_ref, *refs):
     near_end = 2 + peers
-    count = near_end + 2 + 5
+    count = near_end + 2 + 8
     held, results = refs[:count], refs[count : count + 4]
     outs, out_sems = refs[count + 4 : count + 8], refs[-1]
-    length = results[0].shape[0]
-    made = []
-
-    def packed():
-        if not made:
-            made.append(unpack_rows(peers, stride, length // R2, length // R3, held[0]))
-        return made[0]
 
     sent = []
 
@@ -630,8 +693,8 @@
     groups = results[0].shape[1] // GW
     lockstep(
         final_group(
-            peers, stride, digits, group, fr_ref, near, packed, held[0], *local,
-            base[:4], base[4], outs, done,
+            peers, stride, digits, group, fr_ref, near, held[0], *local,
+            base[:4], base[4], base[5:], outs, done,
         )
         for group in range(groups)
     )
@@ -733,6 +796,22 @@
             name="backward",
         )(queries, key_vectors, value_vectors, out_grad, st12, *grads)
 
+    def beside(at, count):
+        if at == count - 1:
+            return range(pieces - 1 if count > 1 else 0, pieces)
+        return range(pieces - 1) if at == 0 else ()
+
+    def near_pass(far_all):
+        return pl.pallas_call(
+            functools.partial(near_kernel, peers, stride),
+            in_specs=[vmem_spec] * (peers + 3),
+            out_specs=[vmem_spec] * 3,
+            out_shape=[like(n)] * 3,
+            compiler_params=params(),
+            cost_estimate=pl.CostEstimate(flops=ops, bytes_accessed=2 * length * width, transcendentals=0),
+            name="near",
+        )(fr, far_all, kv, qg, *got)
+
     def bits_of(size, least):
         while size > least:
             pick = 4 if size >= 4 * least else 2
@@ -750,15 +829,19 @@
     far_all = mine
     for at, (axis, radix, unit, _) in enumerate(steps):
         others = [swap(far_all, axis, digit * unit) for digit in range(1, radix)]
-        if at < pieces:
-            grads = backward(at, grads)
+        if at == len(steps) - 1 and col_count > 1:
+            near_grads = near_pass(far_all)
+            near_grads, others = lax.optimization_barrier((near_grads, others))
+        else:
+            for piece in beside(at, len(steps) - 1):
+                grads = backward(piece, grads)
             grads, others = lax.optimization_barrier((grads, others))
         far_all = jnp.concatenate([far_all, *others], axis=0)
-    for at in range(len(steps), pieces):
-        grads = backward(at, grads)
+    if col_count == 1:
+        near_grads = near_pass(far_all)
     digits = tuple((radix, unit) for _, radix, _, unit in steps)
 
-    operands = (fr, far_all, kv, qg, *got, key_vectors, value_vectors, att1, *grads, near_out)
+    operands = (fr, far_all, kv, qg, *got, key_vectors, value_vectors, att1, *grads, near_out, *near_grads)
     return pl.pallas_call(
         functools.partial(final_kernel, peers, stride, digits),
         in_specs=[vmem_spec] * len(operands),

time: 40.6 us -> 39.5 us (0.973)
  waiting for transfers between devices: 4.89 us -> 3.56 us
    ppermute x10, waiting for transfers between devices: 4.89 us -> 3.56 us  [swap(): return lax.ppermute(x, axis, [(i, i ^ mask) for i in range(size)])]
    pallas_call x0 -> x1, Pallas kernels: none -> 1.28 us  [near_pass(): pl.pallas_call(functools.partial(near_kernel, peers, stride), in_specs=[v...]
    pallas_call x1, Pallas kernels: 5.91 us -> 4.95 us  [shards(): pl.pallas_call(functools.partial(final_kernel, peers, stride, digits), in...]
  transfers between devices with their start and end apart: 10 -> 10, of which waited for: 5 -> 5; matrix products, arithmetic and copies ran while one was open for 0% -> 0% of each run, Pallas kernels for 25% -> 29%
where the time goes in v5:
time: 39.5 us; the launch traced here: 39.4 us
  Pallas kernels  22.1 us (56%)
  starting transfers between devices  12.6 us (32%)
  waiting for transfers between devices  3.56 us (9%)
  between operations  0.98 us (2%)
    ppermute x10, starting transfers between devices, swap(): return lax.ppermute(x, axis, [(i, i ^ mask) for i in range(size)])  12.6 us
    pallas_call x3, Pallas kernels, backward(): pl.pallas_call(functools.partial(backward_kernel, 256, 1, range(piece * p...  6.49 us
    pallas_call x1, Pallas kernels, shards(): pl.pallas_call(functools.partial(final_kernel, peers, stride, digits), in...  4.95 us
    pallas_call x1, Pallas kernels, shards(): pl.pallas_call(functools.partial(pick_kernel, peers), grid=(groups,), in_...  4.06 us
    pallas_call x1, Pallas kernels, shards(): pl.pallas_call(functools.partial(forward_kernel, 256, 2), in_specs=[vmem_...  3.58 us
    ppermute x10, waiting for transfers between devices, swap(): return lax.ppermute(x, axis, [(i, i ^ mask) for i in range(size)])  3.56 us
    pallas_call x1, Pallas kernels, shards(): pl.pallas_call(functools.partial(merge_kernel, peers), in_specs=[vmem_spe...  1.73 us
    pallas_call x1, Pallas kernels, near_pass(): pl.pallas_call(functools.partial(near_kernel, peers, stride), in_specs=[v...  1.28 us
  transfers between devices with their start and end apart: 10, of which 5 were waited for; matrix products, arithmetic and copies ran while one was open for 0% of the time, Pallas kernels for 29%

profile of v5, /device:TPU:0, one launch (start us, length us, event | category | flops | bytes accessed | tf_op | source)
XLA Modules:
  0.0 39.4 jit_solution(3547188383052144440)
XLA Ops:
  0.7 4.1 %pick.1 = (bf16[64,768]{1,0:T(8,128)(2,1)}, bf16[64,768]{1,0:T(8,128)(2,1)}, bf16[16,768]{1,0:T(8,128)(2,1)}, bf16[64,768]{1,0:T(8,128)(2,1)}, bf16[64,768]{1,0:T(8,128)(2,1)}, /*index=5*/bf16[64,768]{1,0:T(8,128)(2,1)}) custom-call(s32[12]{0:T(128)} %near_ref.1, s32[12]{0:T(128)} %far_ref.1, bf16[512,768]{1,0:T(8,128)(2,1)} %q_ref.9, ...), custom_call_target="tpu_custom_call" | custom-call | tf_op jit(solution)/shard_map/pick/pallas_call | solution.py:737
  4.7 3.0 %collective-permute-start = (bf16[64,768]{1,0:T(8,128)(2,1)}, bf16[64,768]{1,0:T(8,128)(2,1)S(1)}, u32[]{:S(2)}, u32[]{:S(2)}) collective-permute-start(bf16[64,768]{1,0:T(8,128)(2,1)} %get-tuple-element.46), channel_id=1, source_target_pairs={{0,8},{8,0},{16,24},{24,16},{1,9},{9,1},{17,25},{25,17},{2,10},{10... | collective-permute-start | bytes 294920 | tf_op jit(solution)/shard_map/ppermute | solution.py:735
  7.7 1.5 %collective-permute-start.1 = (bf16[64,768]{1,0:T(8,128)(2,1)}, bf16[64,768]{1,0:T(8,128)(2,1)S(1)}, u32[]{:S(2)}, u32[]{:S(2)}) collective-permute-start(bf16[64,768]{1,0:T(8,128)(2,1)} %get-tuple-element.47), channel_id=1, source_target_pairs={{0,16},{8,24},{16,0},{24,8},{1,17},{9,25},{17,1},{25,9},{2,18},{10... | collective-permute-start | bytes 294920 | tf_op jit(solution)/shard_map/ppermute | solution.py:735
  9.3 0.0 collective-permute-start.2
  9.3 3.6 %forward.1 = (bf16[512,768]{1,0:T(8,128)(2,1)S(1)}, f32[48,512]{1,0:T(8,128)S(1)}) custom-call(bf16[512,768]{1,0:T(8,128)(2,1)S(1)} %copy-done.2, bf16[512,768]{1,0:T(8,128)(2,1)S(1)} %copy-done, bf16[512,768]{1,0:T(8,128)(2,1)S(1)} %copy-done.1, bf16[512,768]{1,0:T(8,128)(2,1)S(1)} %copy-done.3), custom_call_target="tpu_custom_call" | custom-call | flops 3221225472 | bytes 4718592 | tf_op jit(solution)/shard_map/forward/pallas_call | solution.py:761
  12.9 0.7 %collective-permute-done.1.rest_1_.refs_4_ = bf16[64,768]{1,0:T(8,128)(2,1)S(1)} collective-permute-done((bf16[64,768]{1,0:T(8,128)(2,1)}, bf16[64,768]{1,0:T(8,128)(2,1)S(1)}, u32[]{:S(2)}, u32[]{:S(2)}) %collective-permute-start.1) | collective-permute-done | bytes 98336 | tf_op jit(solution)/shard_map/ppermute | solution.py:735
  13.6 1.4 %collective-permute-done.2.rest_2_.refs_5_ = bf16[64,768]{1,0:T(8,128)(2,1)S(1)} collective-permute-done((bf16[64,768]{1,0:T(8,128)(2,1)}, bf16[64,768]{1,0:T(8,128)(2,1)S(1)}, u32[]{:S(2)}, u32[]{:S(2)}) %collective-permute-start.2) | collective-permute-done | bytes 98336 | tf_op jit(solution)/shard_map/ppermute | solution.py:735
  15.0 1.7 %merge.1 = (bf16[16,768]{1,0:T(8,128)(2,1)S(1)}, f32[48,512]{1,0:T(8,128)S(1)}, bf16[32,768]{1,0:T(8,128)(2,1)S(1)}) custom-call(bf16[64,768]{1,0:T(8,128)(2,1)S(1)} %copy-done.4, bf16[64,768]{1,0:T(8,128)(2,1)S(1)} %copy-done.5, bf16[64,768]{1,0:T(8,128)(2,1)S(1)} %collective-permute-done.rest_0_.refs_3_, ...), custom_call_target="tpu_custom_call" | custom-call | tf_op jit(solution)/shard_map/merge/pallas_call | solution.py:771
  16.7 3.7 %collective-permute-start.5 = (bf16[16,768]{1,0:T(8,128)(2,1)S(1)}, bf16[16,768]{1,0:T(8,128)(2,1)S(1)}, u32[]{:S(2)}, u32[]{:S(2)}) collective-permute-start(bf16[16,768]{1,0:T(8,128)(2,1)S(1)} %get-tuple-element.51), channel_id=1, source_target_pairs={{0,6},{1,7},{2,4},{3,5},{4,2},{5,3},{6,0},{7,1},{8,14},{9,15},{10,... | collective-permute-start | bytes 73736 | tf_op jit(solution)/shard_map/ppermute | solution.py:735
  20.4 0.0 collective-permute-start.4
  20.4 0.8 %collective-permute-start.3 = (bf16[16,768]{1,0:T(8,128)(2,1)S(1)}, bf16[16,768]{1,0:T(8,128)(2,1)S(1)}, u32[]{:S(2)}, u32[]{:S(2)}) collective-permute-start(bf16[16,768]{1,0:T(8,128)(2,1)S(1)} %get-tuple-element.51), channel_id=1, source_target_pairs={{0,2},{1,3},{2,0},{3,1},{4,6},{5,7},{6,4},{7,5},{8,10},{9,11},{10,... | collective-permute-start | bytes 73736 | tf_op jit(solution)/shard_map/ppermute | solution.py:735
  21.2 2.2 %backward.3 = (bf16[512,768]{1,0:T(8,128)(2,1)S(1)}, bf16[512,768]{1,0:T(8,128)(2,1)S(1)}, bf16[512,768]{1,0:T(8,128)(2,1)S(1)}) custom-call(bf16[512,768]{1,0:T(8,128)(2,1)S(1)} %copy-done.2, bf16[512,768]{1,0:T(8,128)(2,1)S(1)} %copy-done, bf16[512,768]{1,0:T(8,128)(2,1)S(1)} %copy-done.1, bf16[512,768]{1,0:T(8,128)(2,1)S(1)} %copy-done.3, ...), custom_call_target="tpu_custom_call" | custom-call | flops 2684354560 | bytes 2097152 | tf_op jit(solution)/shard_map/backward/pallas_call | solution.py:786
  23.4 2.2 %backward.4 = (bf16[512,768]{1,0:T(8,128)(2,1)S(1)}, bf16[512,768]{1,0:T(8,128)(2,1)S(1)}, bf16[512,768]{1,0:T(8,128)(2,1)S(1)}) custom-call(bf16[512,768]{1,0:T(8,128)(2,1)S(1)} %copy-done.2, bf16[512,768]{1,0:T(8,128)(2,1)S(1)} %copy-done, bf16[512,768]{1,0:T(8,128)(2,1)S(1)} %copy-done.1, ...), custom_call_target="tpu_custom_call", output_to_operand_aliasing={{0}: (5, {}), {1}: (6, {}), {2}: (7, {})} | custom-call | flops 2684354560 | bytes 2097152 | tf_op jit(solution)/shard_map/backward/pallas_call | solution.py:786
  25.5 0.0 collective-permute-done.4
  25.6 1.0 %collective-permute-start.8 = (bf16[64,768]{1,0:T(8,128)(2,1)S(1)}, bf16[64,768]{1,0:T(8,128)(2,1)S(1)}, u32[]{:S(2)}, u32[]{:S(2)}) collective-permute-start(bf16[64,768]{1,0:T(8,128)(2,1)S(1)} %get-tuple-element.90), channel_id=1, source_target_pairs={{0,24},{8,16},{16,8},{24,0},{1,25},{9,17},{17,9},{25,1},{2,26},{10... | collective-permute-start | bytes 294920 | tf_op jit(solution)/shard_map/ppermute | solution.py:735
  26.6 1.1 %collective-permute-start.7 = (bf16[64,768]{1,0:T(8,128)(2,1)S(1)}, bf16[64,768]{1,0:T(8,128)(2,1)S(1)}, u32[]{:S(2)}, u32[]{:S(2)}) collective-permute-start(bf16[64,768]{1,0:T(8,128)(2,1)S(1)} %get-tuple-element.90), channel_id=1, source_target_pairs={{0,16},{8,24},{16,0},{24,8},{1,17},{9,25},{17,1},{25,9},{2,18},{10... | collective-permute-start | bytes 294920 | tf_op jit(solution)/shard_map/ppermute | solution.py:735
  27.8 1.4 %collective-permute-start.6 = (bf16[64,768]{1,0:T(8,128)(2,1)S(1)}, bf16[64,768]{1,0:T(8,128)(2,1)S(1)}, u32[]{:S(2)}, u32[]{:S(2)}) collective-permute-start(bf16[64,768]{1,0:T(8,128)(2,1)S(1)} %get-tuple-element.90), channel_id=1, source_target_pairs={{0,8},{8,0},{16,24},{24,16},{1,9},{9,1},{17,25},{25,17},{2,10},{10... | collective-permute-start | bytes 294920 | tf_op jit(solution)/shard_map/ppermute | solution.py:735
  29.2 2.2 %backward.5 = (bf16[512,768]{1,0:T(8,128)(2,1)S(1)}, bf16[512,768]{1,0:T(8,128)(2,1)S(1)}, bf16[512,768]{1,0:T(8,128)(2,1)S(1)}) custom-call(bf16[512,768]{1,0:T(8,128)(2,1)S(1)} %copy-done.2, bf16[512,768]{1,0:T(8,128)(2,1)S(1)} %copy-done, bf16[512,768]{1,0:T(8,128)(2,1)S(1)} %copy-done.1, ...), custom_call_target="tpu_custom_call", output_to_operand_aliasing={{0}: (5, {}), {1}: (6, {}), {2}: (7, {})} | custom-call | flops 2684354560 | bytes 2097152 | tf_op jit(solution)/shard_map/backward/pallas_call | solution.py:786
  31.4 0.9 %collective-permute-done.7 = bf16[64,768]{1,0:T(8,128)(2,1)S(1)} collective-permute-done((bf16[64,768]{1,0:T(8,128)(2,1)S(1)}, bf16[64,768]{1,0:T(8,128)(2,1)S(1)}, u32[]{:S(2)}, u32[]{:S(2)}) %collective-permute-start.7) | collective-permute-done | bytes 98336 | tf_op jit(solution)/shard_map/ppermute | solution.py:735
  32.2 0.1 collective-permute-done.6
  32.5 0.1 collective-permute-start.9
  32.5 1.3 %near.1 = (bf16[32,768]{1,0:T(8,128)(2,1)S(1)}, bf16[32,768]{1,0:T(8,128)(2,1)S(1)}, bf16[32,768]{1,0:T(8,128)(2,1)S(1)}) custom-call(bf16[16,768]{1,0:T(8,128)(2,1)S(1)} %copy-done.6, bf16[256,768]{1,0:T(8,128)(2,1)S(1)} %get-tuple-element.82.fa_ref, bf16[64,768]{1,0:T(8,128)(2,1)S(1)} %copy-done.4, bf16[64,768]{1,0:T(8,128)(2,1)S(1)} %copy-done.5, ...), custom_call_target="tpu_custom_call" | custom-call | flops 402653184 | bytes 786432 | tf_op jit(solution)/shard_map/near/pallas_call | solution.py:805
  33.8 0.4 %collective-permute-done.9 = bf16[256,768]{1,0:T(8,128)(2,1)S(1)} collective-permute-done((bf16[256,768]{1,0:T(8,128)(2,1)S(1)}, bf16[256,768]{1,0:T(8,128)(2,1)S(1)}, u32[]{:S(2)}, u32[]{:S(2)}) %collective-permute-start.9) | collective-permute-done | bytes 393248 | tf_op jit(solution)/shard_map/ppermute | solution.py:735
  34.3 5.0 %final.1 = (bf16[512,768]{1,0:T(8,128)(2,1)}, bf16[512,768]{1,0:T(8,128)(2,1)}, bf16[512,768]{1,0:T(8,128)(2,1)}, bf16[512,768]{1,0:T(8,128)(2,1)}) custom-call(bf16[16,768]{1,0:T(8,128)(2,1)S(1)} %copy-done.6, bf16[512,768]{1,0:T(8,128)(2,1)S(1)} %constant_dynamic-update-slice_fusion.11.refs_0_, bf16[64,768]{1,0:T(8,128)(2,1)S(1)} %copy-done.4, ...), custom_call_target="tpu_custom_call" | custom-call | tf_op jit(solution)/shard_map/final/pallas_call | solution.py:845
  (26 shorter events, 0.1 us)
Async XLA Ops:
  0.6 8.6 %copy-start.1 = (bf16[512,768]{1,0:T(8,128)(2,1)S(1)}, bf16[512,768]{1,0:T(8,128)(2,1)}, u32[]{:S(2)}) copy-start(bf16[512,768]{1,0:T(8,128)(2,1)} %refs_7_.1) | copy-start | bytes 2359300
  0.6 8.6 %copy-start = (bf16[512,768]{1,0:T(8,128)(2,1)S(1)}, bf16[512,768]{1,0:T(8,128)(2,1)}, u32[]{:S(2)}) copy-start(bf16[512,768]{1,0:T(8,128)(2,1)} %refs_6_.1) | copy-start | bytes 2359300
  0.7 8.6 %copy-start.3 = (bf16[512,768]{1,0:T(8,128)(2,1)S(1)}, bf16[512,768]{1,0:T(8,128)(2,1)}, u32[]{:S(2)}) copy-start(bf16[512,768]{1,0:T(8,128)(2,1)} %g_ref.9) | copy-start | bytes 2359300
  0.7 8.6 %copy-start.2 = (bf16[512,768]{1,0:T(8,128)(2,1)S(1)}, bf16[512,768]{1,0:T(8,128)(2,1)}, u32[]{:S(2)}) copy-start(bf16[512,768]{1,0:T(8,128)(2,1)} %q_ref.9) | copy-start | bytes 2359300
  4.7 8.2 %collective-permute-start = (bf16[64,768]{1,0:T(8,128)(2,1)}, bf16[64,768]{1,0:T(8,128)(2,1)S(1)}, u32[]{:S(2)}, u32[]{:S(2)}) collective-permute-start(bf16[64,768]{1,0:T(8,128)(2,1)} %get-tuple-element.46), channel_id=1, source_target_pairs={{0,8},{8,0},{16,24},{24,16},{1,9},{9,1},{17,25},{25,17},{2,10},{10... | collective-permute-start | bytes 294920 | tf_op jit(solution)/shard_map/ppermute | solution.py:735
  7.7 5.9 %collective-permute-start.1 = (bf16[64,768]{1,0:T(8,128)(2,1)}, bf16[64,768]{1,0:T(8,128)(2,1)S(1)}, u32[]{:S(2)}, u32[]{:S(2)}) collective-permute-start(bf16[64,768]{1,0:T(8,128)(2,1)} %get-tuple-element.47), channel_id=1, source_target_pairs={{0,16},{8,24},{16,0},{24,8},{1,17},{9,25},{17,1},{25,9},{2,18},{10... | collective-permute-start | bytes 294920 | tf_op jit(solution)/shard_map/ppermute | solution.py:735
  9.2 5.7 %copy-start.4 = (bf16[64,768]{1,0:T(8,128)(2,1)S(1)}, bf16[64,768]{1,0:T(8,128)(2,1)}, u32[]{:S(2)}) copy-start(bf16[64,768]{1,0:T(8,128)(2,1)} %get-tuple-element.44.kv_ref.refs_1_) | copy-start | bytes 294916
  9.3 5.7 %copy-start.5 = (bf16[64,768]{1,0:T(8,128)(2,1)S(1)}, bf16[64,768]{1,0:T(8,128)(2,1)}, u32[]{:S(2)}) copy-start(bf16[64,768]{1,0:T(8,128)(2,1)} %get-tuple-element.45.qg_ref.refs_2_) | copy-start | bytes 294916
  9.3 5.7 %collective-permute-start.2 = (bf16[64,768]{1,0:T(8,128)(2,1)}, bf16[64,768]{1,0:T(8,128)(2,1)S(1)}, u32[]{:S(2)}, u32[]{:S(2)}) collective-permute-start(bf16[64,768]{1,0:T(8,128)(2,1)} %get-tuple-element.48), channel_id=1, source_target_pairs={{0,24},{8,16},{16,8},{24,0},{1,25},{9,17},{17,9},{25,1},{2,26},{10... | collective-permute-start | bytes 294920 | tf_op jit(solution)/shard_map/ppermute | solution.py:735
  9.3 5.7 %copy-start.6 = (bf16[16,768]{1,0:T(8,128)(2,1)S(1)}, bf16[16,768]{1,0:T(8,128)(2,1)}, u32[]{:S(2)}) copy-start(bf16[16,768]{1,0:T(8,128)(2,1)} %get-tuple-element.43.rest_5_.fr_ref) | copy-start | bytes 73732
  16.7 8.8 %collective-permute-start.5 = (bf16[16,768]{1,0:T(8,128)(2,1)S(1)}, bf16[16,768]{1,0:T(8,128)(2,1)S(1)}, u32[]{:S(2)}, u32[]{:S(2)}) collective-permute-start(bf16[16,768]{1,0:T(8,128)(2,1)S(1)} %get-tuple-element.51), channel_id=1, source_target_pairs={{0,6},{1,7},{2,4},{3,5},{4,2},{5,3},{6,0},{7,1},{8,14},{9,15},{10,... | collective-permute-start | bytes 73736 | tf_op jit(solution)/shard_map/ppermute | solution.py:735
  20.4 5.1 %collective-permute-start.4 = (bf16[16,768]{1,0:T(8,128)(2,1)S(1)}, bf16[16,768]{1,0:T(8,128)(2,1)S(1)}, u32[]{:S(2)}, u32[]{:S(2)}) collective-permute-start(bf16[16,768]{1,0:T(8,128)(2,1)S(1)} %get-tuple-element.51), channel_id=1, source_target_pairs={{0,4},{1,5},{2,6},{3,7},{4,0},{5,1},{6,2},{7,3},{8,12},{9,13},{10,... | collective-permute-start | bytes 73736 | tf_op jit(solution)/shard_map/ppermute | solution.py:735
  20.4 5.2 %collective-permute-start.3 = (bf16[16,768]{1,0:T(8,128)(2,1)S(1)}, bf16[16,768]{1,0:T(8,128)(2,1)S(1)}, u32[]{:S(2)}, u32[]{:S(2)}) collective-permute-start(bf16[16,768]{1,0:T(8,128)(2,1)S(1)} %get-tuple-element.51), channel_id=1, source_target_pairs={{0,2},{1,3},{2,0},{3,1},{4,6},{5,7},{6,4},{7,5},{8,10},{9,11},{10,... | collective-permute-start | bytes 73736 | tf_op jit(solution)/shard_map/ppermute | solution.py:735
  25.6 5.7 %collective-permute-start.8 = (bf16[64,768]{1,0:T(8,128)(2,1)S(1)}, bf16[64,768]{1,0:T(8,128)(2,1)S(1)}, u32[]{:S(2)}, u32[]{:S(2)}) collective-permute-start(bf16[64,768]{1,0:T(8,128)(2,1)S(1)} %get-tuple-element.90), channel_id=1, source_target_pairs={{0,24},{8,16},{16,8},{24,0},{1,25},{9,17},{17,9},{25,1},{2,26},{10... | collective-permute-start | bytes 294920 | tf_op jit(solution)/shard_map/ppermute | solution.py:735
  26.6 5.6 %collective-permute-start.7 = (bf16[64,768]{1,0:T(8,128)(2,1)S(1)}, bf16[64,768]{1,0:T(8,128)(2,1)S(1)}, u32[]{:S(2)}, u32[]{:S(2)}) collective-permute-start(bf16[64,768]{1,0:T(8,128)(2,1)S(1)} %get-tuple-element.90), channel_id=1, source_target_pairs={{0,16},{8,24},{16,0},{24,8},{1,17},{9,25},{17,1},{25,9},{2,18},{10... | collective-permute-start | bytes 294920 | tf_op jit(solution)/shard_map/ppermute | solution.py:735
  27.8 4.6 %collective-permute-start.6 = (bf16[64,768]{1,0:T(8,128)(2,1)S(1)}, bf16[64,768]{1,0:T(8,128)(2,1)S(1)}, u32[]{:S(2)}, u32[]{:S(2)}) collective-permute-start(bf16[64,768]{1,0:T(8,128)(2,1)S(1)} %get-tuple-element.90), channel_id=1, source_target_pairs={{0,8},{8,0},{16,24},{24,16},{1,9},{9,1},{17,25},{25,17},{2,10},{10... | collective-permute-start | bytes 294920 | tf_op jit(solution)/shard_map/ppermute | solution.py:735
  32.5 1.8 %collective-permute-start.9 = (bf16[256,768]{1,0:T(8,128)(2,1)S(1)}, bf16[256,768]{1,0:T(8,128)(2,1)S(1)}, u32[]{:S(2)}, u32[]{:S(2)}) collective-permute-start(bf16[256,768]{1,0:T(8,128)(2,1)S(1)} %get-tuple-element.82.fa_ref), channel_id=1, source_target_pairs={{0,1},{1,0},{2,3},{3,2},{4,5},{5,4},{6,7},{7,6},{8,9},{9,8},{10,11... | collective-permute-start | bytes 1179656 | tf_op jit(solution)/shard_map/ppermute | solution.py:735

commit v6 on v5

--- a/solution.py
+++ b/solution.py
@@ -99,25 +99,12 @@
     return nn(hi, block) + nn(low, block)
 
 
-def piece_column(aux_expanded, which):
-    a = iota((GW, 1), 0)
-    return nn(aux_expanded, onehot(a % HD // 3 == which))[:, :1]
-
-
 def near_select(n, length):
     return onehot(div(iota((1, length), 1), R2) == iota((n, 1), 0))
 
 
-def near_place(n, length):
-    return onehot(iota((length, 1), 0) // R2 == iota((1, n), 1))
-
-
 def far_select(rows, length, first):
     return onehot(div(iota((1, length), 1), R3) == iota((rows, 1), 0) - first)
-
-
-def far_place(length):
-    return onehot(iota((length, 1), 0) // R3 == iota((1, FM), 1))
 
 
 def token_masks(near_ref, far_ref, group, length):
@@ -313,7 +300,7 @@
     return out.astype(BF)
 
 
-def merge_group(peers, group, kv_ref, qg_ref, got, st_ref, att_ref, fr_ref, out_ref, st_out, near_out, blocks, packs):
+def merge_group(peers, group, kv_ref, qg_ref, got, st_ref, att_ref, fr_ref, out_ref, near_aux, near_out, blocks, packs):
     cols = group_columns(group)
     srows = slice(group * SR, (group + 1) * SR)
     length = att_ref.shape[0]
@@ -332,6 +319,7 @@
     sel = near_select(n, length)
     log1 = nt(sel, pieces3(jnp.where(near_st, st, 0.0)))
     out1 = collapse(nn(head_rows(n, R2, length, near_ref, group), att_ref[:, cols]))
+    far_aux = nt(far_select(FM, length, 4 * f), pieces3(jnp.where(far_st, st, 0.0)))
     yield
     s = jnp.where(near_valid_queries(s.shape, n, own), s, NEG)
     top = jnp.max(s, axis=1, keepdims=True)
@@ -341,7 +329,9 @@
     out2 = nn(w.astype(BF), values)
     head, what = stat_row((3 * SR, GW), 0)
     lane = iota((1, GW), 1)
+    piece = div(iota((3 * SR, 1), 0), SR)
     log1 = nn(log1.astype(BF), onehot((div(lane, HD) == head) & (what == 0)))
+    far_aux = nn(far_aux.astype(BF), onehot((div(lane, HD) == head) & (mod(lane, HD) == what * 3 + piece)))
     yield
     out2 = collapse(out2 / total)
     log2 = collapse(jnp.broadcast_to(top + jnp.log(total), (GH * n, GW)))
@@ -355,27 +345,21 @@
     yield
     aux12 = pack_aux(log12, dot12).astype(BF)
     packs.append(nn(aux12, pack_lanes(group)))
-    head, what = stat_row((SR, GW), 0)
-    lane = iota((1, GW), 1)
-    compact = nt(onehot((div(lane, HD) == head) & (div(mod(lane, HD), 3) == what)), aux12)
-    yield
-    place = onehot(div(iota((1, length), 1), R2) == iota((n, 1), 0))
-    placed = nn(pieces3(compact), place)
-    yield
-    placed = placed[:SR] + placed[SR : 2 * SR] + placed[2 * SR :]
-    st = jnp.where(near_st, placed, st)
-    st_out[srows, :] = jnp.where(far_st, -NEG, st)
-    far_aux = nt(far_select(FM, length, 4 * f), pieces3(jnp.where(far_st, st, 0.0)))
-    yield
-    head, what = stat_row((3 * SR, GW), 0)
-    lane, piece = iota((1, GW), 1), div(iota((3 * SR, 1), 0), SR)
-    far_aux = nn(far_aux.astype(BF), onehot((div(lane, HD) == head) & (mod(lane, HD) == what * 3 + piece)))
+    near_aux[:, cols] = aux12
+    r = iota((GH * FM, 1), 0)
+    j = mod(r, FM) - 4 * f
+    foff, noff = row_offsets(FM, far_ref, group), row_offsets(FM, near_ref, group)
+    row = jnp.where((j >= 0) & (j < f) & (mod(foff, R2) == noff), j * (R3 // R2) + div(foff, R2), -1)
+    from_near = collapse(nn(onehot(iota((1, n), 1) == row), aux12))
+    yield
+    twice = mod(lane_offsets(far_ref, group), R2) == lane_offsets(near_ref, group)
     raw = fr_ref[:, cols].astype(F32)
-    blocks[group] = jnp.where(iota(raw.shape, 0) < 4 * f, raw, 0.0) + far_aux
+    raw = jnp.where(iota((FM, 1), 0) < 4 * f, raw, 0.0)
+    blocks[group] = raw + jnp.where(twice, from_near, far_aux)
 
 
 def merge_kernel(peers, kv_ref, qg_ref, *rest):
-    got, rest = rest[: peers - 1], rest[peers - 1 :]
+    got, rest = unturned(rest[: peers - 1]), rest[peers - 1 :]
     groups = kv_ref.shape[1] // GW
     out_ref = rest[3]
     blocks, packs = {}, []
@@ -393,7 +377,22 @@
         out_ref[:, at * 128 : (at + 1) * 128] = (block + rows).astype(BF)
 
 
-def backward_kernel(strip, skew, span, aliased, q_ref, k_ref, v_ref, g_ref, st_ref, *rest):
+def pair_statistics(p, st_ref, aux_ref, fr_ref):
+    length = st_ref.shape[1]
+    n, f = length // R2, length // R3
+    near, far = read_offsets(fr_ref, f, p * 2 // GH)
+    r, lane, t = iota((8, 1), 0), iota((1, PW), 1), iota((1, length), 1)
+    noff, foff = (jnp.where(mod(r, 2) == 0, ref[2 * p], ref[2 * p + 1]) for ref in (near, far))
+    mine = (div(lane, HD) == mod(r, 2)) & (div(mod(lane, HD), 3) == div(r, 2)) & (r < 4)
+    merged = nt(onehot(mine), aux_ref[:, pair_columns(p)])
+    place = onehot(div(t, R2) == iota((n, 1), 0))
+    merged = nn(pieces3(merged), place)
+    merged = merged[:8] + merged[8:16] + merged[16:]
+    st = jnp.where(mod(t, R2) == noff, merged, st_ref[p * 8 : p * 8 + 8, :])
+    return jnp.where(mod(t, R3) == foff, -NEG, st)
+
+
+def backward_kernel(strip, skew, span, aliased, q_ref, k_ref, v_ref, g_ref, st_ref, aux_ref, fr_ref, *rest):
     dq_ref, dk_ref, dv_ref = rest[aliased:]
     length = q_ref.shape[0]
     first, in_head = head_masks()
@@ -407,16 +406,18 @@
         if c == 0 and h == 0:
             kept["k", p] = (nt(eye, k_ref[:, cols]) * SCALE).astype(BF)
             kept["q", p] = q_ref[:, cols] * jnp.asarray(SCALE, BF)
+            kept["st", p] = pair_statistics(p, st_ref, aux_ref, fr_ref)
         s = nt(k_ref[rows, cols] * in_head[h], kept["q", p][c * strip :])
         dp = nt(v_ref[rows, cols] * in_head[h], g_ref[c * strip :, cols])
         kept["s", p, c, h] = s, dp
 
     def soften(p, c, h):
         s, dp = kept.pop(("s", p, c, h))
-        prob = jnp.exp(s - st_ref[p * 8 + h : p * 8 + h + 1, c * strip :])
+        st = kept["st", p][:, c * strip :]
+        prob = jnp.exp(s - st[h : h + 1])
         head = jnp.where(diag, prob[:, :strip], 0.0)
         prob = jnp.concatenate([head, prob[:, strip:]], axis=1) if c + 1 < strips else head
-        ds = prob * (dp - st_ref[p * 8 + 2 + h : p * 8 + 3 + h, c * strip :])
+        ds = prob * (dp - st[2 + h : 3 + h])
         kept["p", p, c, h] = prob.astype(BF), ds.astype(BF)
 
     def mix(p, c, h):
@@ -515,7 +516,7 @@
 
 
 def near_kernel(peers, stride, fr_ref, fa_ref, kv_ref, qg_ref, *rest):
-    got, outs = rest[: peers - 1], rest[peers - 1 :]
+    got, outs = unturned(rest[: peers - 1]), rest[peers - 1 :]
     n, width = outs[0].shape
     made = []
 
@@ -549,7 +550,7 @@
 def final_group(
     peers, stride, digits, group, fr_ref, got, fa_ref, k_ref, v_ref, base, near_out, near_grads, outs, done
 ):
-    kv_ref, qg_ref, got = got[0], got[1], got[2:]
+    kv_ref, qg_ref, got = got[0], got[1], unturned(got[2:])
     cols = group_columns(group)
     length = k_ref.shape[0]
     n, f = length // R2, length // R3
@@ -702,6 +703,14 @@
         copy.wait()
 
 
+def turned(x):
+    return [x[-1], *x[:-1]]
+
+
+def unturned(x):
+    return [*x[1:], x[0]]
+
+
 def smem():
     return pl.BlockSpec(memory_space=pltpu.SMEM)
 
@@ -748,7 +757,7 @@
 
     ops = 2 * H * length * length * HD
     stats = jax.ShapeDtypeStruct((pairs * 8, length), F32)
-    per = 2
+    per = 3
 
     vmem_spec = pl.BlockSpec(memory_space=pltpu.VMEM)
 
@@ -768,14 +777,14 @@
         name="forward",
     )(queries, key_vectors, value_vectors, out_grad)
 
-    mine, st12, near_out = pl.pallas_call(
+    mine, near_aux, near_out = pl.pallas_call(
         functools.partial(merge_kernel, peers),
         in_specs=[vmem_spec] * (peers + 4),
         out_specs=[vmem_spec] * 3,
-        out_shape=[like(FM), stats, like(n)],
+        out_shape=[like(FM), like(n), like(n)],
         compiler_params=params(),
         name="merge",
-    )(kv, qg, *got, st1, att1, fr)
+    )(kv, qg, *turned(got), st1, att1, fr)
 
     grads = []
     pieces = pairs // per
@@ -785,16 +794,16 @@
         aliased = len(grads)
         return pl.pallas_call(
             functools.partial(backward_kernel, 256, 1, range(piece * per, (piece + 1) * per), aliased),
-            in_specs=[vmem_spec] * 5 + [vmem_spec] * aliased,
+            in_specs=[vmem_spec] * (7 + aliased),
             out_specs=[vmem_spec] * 3,
             out_shape=[like(length)] * 3,
-            input_output_aliases={5 + i: i for i in range(aliased)},
+            input_output_aliases={7 + i: i for i in range(aliased)},
             compiler_params=params(),
             cost_estimate=pl.CostEstimate(
                 flops=5 * ops * 4 // pieces, bytes_accessed=8 * length * width * 2 // pieces, transcendentals=0
             ),
             name="backward",
-        )(queries, key_vectors, value_vectors, out_grad, st12, *grads)
+        )(queries, key_vectors, value_vectors, out_grad, st1, near_aux, fr, *grads)
 
     def beside(at, count):
         if at == count - 1:
@@ -810,7 +819,7 @@
             compiler_params=params(),
             cost_estimate=pl.CostEstimate(flops=ops, bytes_accessed=2 * length * width, transcendentals=0),
             name="near",
-        )(fr, far_all, kv, qg, *got)
+        )(fr, far_all, kv, qg, *turned(got))
 
     def bits_of(size, least):
         while size > least:
@@ -841,7 +850,7 @@
         near_grads = near_pass(far_all)
     digits = tuple((radix, unit) for _, radix, _, unit in steps)
 
-    operands = (fr, far_all, kv, qg, *got, key_vectors, value_vectors, att1, *grads, near_out, *near_grads)
+    operands = (fr, far_all, kv, qg, *turned(got), key_vectors, value_vectors, att1, *grads, near_out, *near_grads)
     return pl.pallas_call(
         functools.partial(final_kernel, peers, stride, digits),
         in_specs=[vmem_spec] * len(operands),

time: 39.5 us -> 39.3 us (level)
  waiting for transfers between devices: 3.56 us -> 2.82 us
    ppermute x10, waiting for transfers between devices: 3.56 us -> 2.82 us  [swap(): return lax.ppermute(x, axis, [(i, i ^ mask) for i in range(size)])]
    pallas_call x3 -> x2, Pallas kernels: 6.49 us -> 7.09 us  [backward(): pl.pallas_call(functools.partial(backward_kernel, 256, 1, range(piece * p...]
  transfers between devices with their start and end apart: 10 -> 10, of which waited for: 5 -> 5; matrix products, arithmetic and copies ran while one was open for 0% -> 0% of each run, Pallas kernels for 29% -> 30%
where the time goes in v6:
time: 39.3 us; the launch traced here: 39.1 us
  Pallas kernels  22.4 us (57%)
  starting transfers between devices  12.9 us (33%)
  waiting for transfers between devices  2.82 us (7%)
  between operations  0.97 us (2%)
    ppermute x10, starting transfers between devices, swap(): return lax.ppermute(x, axis, [(i, i ^ mask) for i in range(size)])  12.9 us
    pallas_call x2, Pallas kernels, backward(): pl.pallas_call(functools.partial(backward_kernel, 256, 1, range(piece * p...  7.09 us
    pallas_call x1, Pallas kernels, shards(): pl.pallas_call(functools.partial(final_kernel, peers, stride, digits), in...  4.95 us
    pallas_call x1, Pallas kernels, shards(): pl.pallas_call(functools.partial(pick_kernel, peers), grid=(groups,), in_...  4.06 us
    pallas_call x1, Pallas kernels, shards(): pl.pallas_call(functools.partial(forward_kernel, 256, 2), in_specs=[vmem_...  3.58 us
    ppermute x10, waiting for transfers between devices, swap(): return lax.ppermute(x, axis, [(i, i ^ mask) for i in range(size)])  2.82 us
    pallas_call x1, Pallas kernels, shards(): pl.pallas_call(functools.partial(merge_kernel, peers), in_specs=[vmem_spe...  1.59 us
    pallas_call x1, Pallas kernels, near_pass(): pl.pallas_call(functools.partial(near_kernel, peers, stride), in_specs=[v...  1.1 us
  transfers between devices with their start and end apart: 10, of which 5 were waited for; matrix products, arithmetic and copies ran while one was open for 0% of the time, Pallas kernels for 30%

profile of v6, /device:TPU:0, one launch (start us, length us, event | category | flops | bytes accessed | tf_op | source)
XLA Modules:
  0.0 39.1 jit_solution(10130954789976149947)
XLA Ops:
  0.7 4.1 %pick.1 = (bf16[64,768]{1,0:T(8,128)(2,1)}, bf16[64,768]{1,0:T(8,128)(2,1)}, bf16[16,768]{1,0:T(8,128)(2,1)}, bf16[64,768]{1,0:T(8,128)(2,1)}, bf16[64,768]{1,0:T(8,128)(2,1)}, /*index=5*/bf16[64,768]{1,0:T(8,128)(2,1)}) custom-call(s32[12]{0:T(128)} %near_ref.1, s32[12]{0:T(128)} %far_ref.1, bf16[512,768]{1,0:T(8,128)(2,1)} %q_ref.7, ...), custom_call_target="tpu_custom_call" | custom-call | tf_op jit(solution)/shard_map/pick/pallas_call | solution.py:746
  4.7 4.0 %collective-permute-start = (bf16[64,768]{1,0:T(8,128)(2,1)}, bf16[64,768]{1,0:T(8,128)(2,1)S(1)}, u32[]{:S(2)}, u32[]{:S(2)}) collective-permute-start(bf16[64,768]{1,0:T(8,128)(2,1)} %get-tuple-element.43), channel_id=1, source_target_pairs={{0,24},{8,16},{16,8},{24,0},{1,25},{9,17},{17,9},{25,1},{2,26},{10... | collective-permute-start | bytes 294920 | tf_op jit(solution)/shard_map/ppermute | solution.py:744
  8.7 0.5 %collective-permute-start.1 = (bf16[64,768]{1,0:T(8,128)(2,1)}, bf16[64,768]{1,0:T(8,128)(2,1)S(1)}, u32[]{:S(2)}, u32[]{:S(2)}) collective-permute-start(bf16[64,768]{1,0:T(8,128)(2,1)} %get-tuple-element.44), channel_id=1, source_target_pairs={{0,8},{8,0},{16,24},{24,16},{1,9},{9,1},{17,25},{25,17},{2,10},{10... | collective-permute-start | bytes 294920 | tf_op jit(solution)/shard_map/ppermute | solution.py:744
  9.2 0.1 collective-permute-start.2
  9.4 3.6 %forward.1 = (bf16[512,768]{1,0:T(8,128)(2,1)S(1)}, f32[48,512]{1,0:T(8,128)S(1)}) custom-call(bf16[512,768]{1,0:T(8,128)(2,1)S(1)} %copy-done.2, bf16[512,768]{1,0:T(8,128)(2,1)S(1)} %copy-done, bf16[512,768]{1,0:T(8,128)(2,1)S(1)} %copy-done.1, bf16[512,768]{1,0:T(8,128)(2,1)S(1)} %copy-done.3), custom_call_target="tpu_custom_call" | custom-call | flops 3221225472 | bytes 4718592 | tf_op jit(solution)/shard_map/forward/pallas_call | solution.py:770
  12.9 0.0 collective-permute-done.rest_0_.refs_3_
  12.9 1.2 %collective-permute-done.1.rest_1_.refs_4_ = bf16[64,768]{1,0:T(8,128)(2,1)S(1)} collective-permute-done((bf16[64,768]{1,0:T(8,128)(2,1)}, bf16[64,768]{1,0:T(8,128)(2,1)S(1)}, u32[]{:S(2)}, u32[]{:S(2)}) %collective-permute-start.1) | collective-permute-done | bytes 98336 | tf_op jit(solution)/shard_map/ppermute | solution.py:744
  14.1 0.0 collective-permute-done.2.rest_2_.refs_5_
  14.1 1.6 %merge.1 = (bf16[16,768]{1,0:T(8,128)(2,1)S(1)}, bf16[32,768]{1,0:T(8,128)(2,1)S(1)}, bf16[32,768]{1,0:T(8,128)(2,1)S(1)}) custom-call(bf16[64,768]{1,0:T(8,128)(2,1)S(1)} %copy-done.4, bf16[64,768]{1,0:T(8,128)(2,1)S(1)} %copy-done.5, bf16[64,768]{1,0:T(8,128)(2,1)S(1)} %collective-permute-done.rest_0_.refs_3_, ...), custom_call_target="tpu_custom_call" | custom-call | tf_op jit(solution)/shard_map/merge/pallas_call | solution.py:780
  15.7 3.8 %collective-permute-start.5 = (bf16[16,768]{1,0:T(8,128)(2,1)S(1)}, bf16[16,768]{1,0:T(8,128)(2,1)S(1)}, u32[]{:S(2)}, u32[]{:S(2)}) collective-permute-start(bf16[16,768]{1,0:T(8,128)(2,1)S(1)} %get-tuple-element.48), channel_id=1, source_target_pairs={{0,6},{1,7},{2,4},{3,5},{4,2},{5,3},{6,0},{7,1},{8,14},{9,15},{10,... | collective-permute-start | bytes 73736 | tf_op jit(solution)/shard_map/ppermute | solution.py:744
  19.5 0.7 %collective-permute-start.3 = (bf16[16,768]{1,0:T(8,128)(2,1)S(1)}, bf16[16,768]{1,0:T(8,128)(2,1)S(1)}, u32[]{:S(2)}, u32[]{:S(2)}) collective-permute-start(bf16[16,768]{1,0:T(8,128)(2,1)S(1)} %get-tuple-element.48), channel_id=1, source_target_pairs={{0,2},{1,3},{2,0},{3,1},{4,6},{5,7},{6,4},{7,5},{8,10},{9,11},{10,... | collective-permute-start | bytes 73736 | tf_op jit(solution)/shard_map/ppermute | solution.py:744
  20.2 3.5 %backward.2 = (bf16[512,768]{1,0:T(8,128)(2,1)S(1)}, bf16[512,768]{1,0:T(8,128)(2,1)S(1)}, bf16[512,768]{1,0:T(8,128)(2,1)S(1)}) custom-call(bf16[512,768]{1,0:T(8,128)(2,1)S(1)} %copy-done.2, bf16[512,768]{1,0:T(8,128)(2,1)S(1)} %copy-done, bf16[512,768]{1,0:T(8,128)(2,1)S(1)} %copy-done.1, bf16[512,768]{1,0:T(8,128)(2,1)S(1)} %copy-done.3, ...), custom_call_target="tpu_custom_call" | custom-call | flops 4026531840 | bytes 3145728 | tf_op jit(solution)/shard_map/backward/pallas_call | solution.py:795
  23.8 0.0 collective-permute-done.5
  23.8 0.5 %collective-permute-done.4 = bf16[16,768]{1,0:T(8,128)(2,1)S(1)} collective-permute-done((bf16[16,768]{1,0:T(8,128)(2,1)S(1)}, bf16[16,768]{1,0:T(8,128)(2,1)S(1)}, u32[]{:S(2)}, u32[]{:S(2)}) %collective-permute-start.4) | collective-permute-done | bytes 24608 | tf_op jit(solution)/shard_map/ppermute | solution.py:744
  24.3 2.3 %collective-permute-start.8 = (bf16[64,768]{1,0:T(8,128)(2,1)S(1)}, bf16[64,768]{1,0:T(8,128)(2,1)S(1)}, u32[]{:S(2)}, u32[]{:S(2)}) collective-permute-start(bf16[64,768]{1,0:T(8,128)(2,1)S(1)} %get-tuple-element.84), channel_id=1, source_target_pairs={{0,24},{8,16},{16,8},{24,0},{1,25},{9,17},{17,9},{25,1},{2,26},{10... | collective-permute-start | bytes 294920 | tf_op jit(solution)/shard_map/ppermute | solution.py:744
  26.5 0.8 %collective-permute-start.7 = (bf16[64,768]{1,0:T(8,128)(2,1)S(1)}, bf16[64,768]{1,0:T(8,128)(2,1)S(1)}, u32[]{:S(2)}, u32[]{:S(2)}) collective-permute-start(bf16[64,768]{1,0:T(8,128)(2,1)S(1)} %get-tuple-element.84), channel_id=1, source_target_pairs={{0,16},{8,24},{16,0},{24,8},{1,17},{9,25},{17,1},{25,9},{2,18},{10... | collective-permute-start | bytes 294920 | tf_op jit(solution)/shard_map/ppermute | solution.py:744
  27.3 0.5 %collective-permute-start.6 = (bf16[64,768]{1,0:T(8,128)(2,1)S(1)}, bf16[64,768]{1,0:T(8,128)(2,1)S(1)}, u32[]{:S(2)}, u32[]{:S(2)}) collective-permute-start(bf16[64,768]{1,0:T(8,128)(2,1)S(1)} %get-tuple-element.84), channel_id=1, source_target_pairs={{0,8},{8,0},{16,24},{24,16},{1,9},{9,1},{17,25},{25,17},{2,10},{10... | collective-permute-start | bytes 294920 | tf_op jit(solution)/shard_map/ppermute | solution.py:744
  27.8 3.5 %backward.3 = (bf16[512,768]{1,0:T(8,128)(2,1)S(1)}, bf16[512,768]{1,0:T(8,128)(2,1)S(1)}, bf16[512,768]{1,0:T(8,128)(2,1)S(1)}) custom-call(bf16[512,768]{1,0:T(8,128)(2,1)S(1)} %copy-done.2, bf16[512,768]{1,0:T(8,128)(2,1)S(1)} %copy-done, bf16[512,768]{1,0:T(8,128)(2,1)S(1)} %copy-done.1, ...), custom_call_target="tpu_custom_call", output_to_operand_aliasing={{0}: (7, {}), {1}: (8, {}), {2}: (9, {})} | custom-call | flops 4026531840 | bytes 3145728 | tf_op jit(solution)/shard_map/backward/pallas_call | solution.py:795
  31.4 0.1 collective-permute-done.7
  31.5 0.4 %collective-permute-done.6 = bf16[64,768]{1,0:T(8,128)(2,1)S(1)} collective-permute-done((bf16[64,768]{1,0:T(8,128)(2,1)S(1)}, bf16[64,768]{1,0:T(8,128)(2,1)S(1)}, u32[]{:S(2)}, u32[]{:S(2)}) %collective-permute-start.6) | collective-permute-done | bytes 98336 | tf_op jit(solution)/shard_map/ppermute | solution.py:744
  32.0 0.3 collective-permute-start.9
  32.3 1.1 %near.1 = (bf16[32,768]{1,0:T(8,128)(2,1)S(1)}, bf16[32,768]{1,0:T(8,128)(2,1)S(1)}, bf16[32,768]{1,0:T(8,128)(2,1)S(1)}) custom-call(bf16[16,768]{1,0:T(8,128)(2,1)S(1)} %copy-done.6, bf16[256,768]{1,0:T(8,128)(2,1)S(1)} %get-tuple-element.76.fa_ref, bf16[64,768]{1,0:T(8,128)(2,1)S(1)} %copy-done.4, bf16[64,768]{1,0:T(8,128)(2,1)S(1)} %copy-done.5, ...), custom_call_target="tpu_custom_call" | custom-call | flops 402653184 | bytes 786432 | tf_op jit(solution)/shard_map/near/pallas_call | solution.py:814
  33.4 0.6 %collective-permute-done.9 = bf16[256,768]{1,0:T(8,128)(2,1)S(1)} collective-permute-done((bf16[256,768]{1,0:T(8,128)(2,1)S(1)}, bf16[256,768]{1,0:T(8,128)(2,1)S(1)}, u32[]{:S(2)}, u32[]{:S(2)}) %collective-permute-start.9) | collective-permute-done | bytes 393248 | tf_op jit(solution)/shard_map/ppermute | solution.py:744
  34.0 5.0 %final.1 = (bf16[512,768]{1,0:T(8,128)(2,1)}, bf16[512,768]{1,0:T(8,128)(2,1)}, bf16[512,768]{1,0:T(8,128)(2,1)}, bf16[512,768]{1,0:T(8,128)(2,1)}) custom-call(bf16[16,768]{1,0:T(8,128)(2,1)S(1)} %copy-done.6, bf16[512,768]{1,0:T(8,128)(2,1)S(1)} %constant_dynamic-update-slice_fusion.11.refs_0_, bf16[64,768]{1,0:T(8,128)(2,1)S(1)} %copy-done.4, ...), custom_call_target="tpu_custom_call" | custom-call | tf_op jit(solution)/shard_map/final/pallas_call | solution.py:854
  (25 shorter events, 0.1 us)
Async XLA Ops:
  0.6 8.7 %copy-start.1 = (bf16[512,768]{1,0:T(8,128)(2,1)S(1)}, bf16[512,768]{1,0:T(8,128)(2,1)}, u32[]{:S(2)}) copy-start(bf16[512,768]{1,0:T(8,128)(2,1)} %refs_7_.1) | copy-start | bytes 2359300
  0.6 8.7 %copy-start = (bf16[512,768]{1,0:T(8,128)(2,1)S(1)}, bf16[512,768]{1,0:T(8,128)(2,1)}, u32[]{:S(2)}) copy-start(bf16[512,768]{1,0:T(8,128)(2,1)} %refs_6_.1) | copy-start | bytes 2359300
  0.7 8.7 %copy-start.3 = (bf16[512,768]{1,0:T(8,128)(2,1)S(1)}, bf16[512,768]{1,0:T(8,128)(2,1)}, u32[]{:S(2)}) copy-start(bf16[512,768]{1,0:T(8,128)(2,1)} %g_ref.7) | copy-start | bytes 2359300
  0.7 8.7 %copy-start.2 = (bf16[512,768]{1,0:T(8,128)(2,1)S(1)}, bf16[512,768]{1,0:T(8,128)(2,1)}, u32[]{:S(2)}) copy-start(bf16[512,768]{1,0:T(8,128)(2,1)} %q_ref.7) | copy-start | bytes 2359300
  4.7 8.2 %collective-permute-start = (bf16[64,768]{1,0:T(8,128)(2,1)}, bf16[64,768]{1,0:T(8,128)(2,1)S(1)}, u32[]{:S(2)}, u32[]{:S(2)}) collective-permute-start(bf16[64,768]{1,0:T(8,128)(2,1)} %get-tuple-element.43), channel_id=1, source_target_pairs={{0,24},{8,16},{16,8},{24,0},{1,25},{9,17},{17,9},{25,1},{2,26},{10... | collective-permute-start | bytes 294920 | tf_op jit(solution)/shard_map/ppermute | solution.py:744
  8.7 5.4 %collective-permute-start.1 = (bf16[64,768]{1,0:T(8,128)(2,1)}, bf16[64,768]{1,0:T(8,128)(2,1)S(1)}, u32[]{:S(2)}, u32[]{:S(2)}) collective-permute-start(bf16[64,768]{1,0:T(8,128)(2,1)} %get-tuple-element.44), channel_id=1, source_target_pairs={{0,8},{8,0},{16,24},{24,16},{1,9},{9,1},{17,25},{25,17},{2,10},{10... | collective-permute-start | bytes 294920 | tf_op jit(solution)/shard_map/ppermute | solution.py:744
  9.2 4.9 %copy-start.4 = (bf16[64,768]{1,0:T(8,128)(2,1)S(1)}, bf16[64,768]{1,0:T(8,128)(2,1)}, u32[]{:S(2)}) copy-start(bf16[64,768]{1,0:T(8,128)(2,1)} %get-tuple-element.41.kv_ref.refs_1_) | copy-start | bytes 294916
  9.2 4.9 %copy-start.5 = (bf16[64,768]{1,0:T(8,128)(2,1)S(1)}, bf16[64,768]{1,0:T(8,128)(2,1)}, u32[]{:S(2)}) copy-start(bf16[64,768]{1,0:T(8,128)(2,1)} %get-tuple-element.42.qg_ref.refs_2_) | copy-start | bytes 294916
  9.2 4.9 %collective-permute-start.2 = (bf16[64,768]{1,0:T(8,128)(2,1)}, bf16[64,768]{1,0:T(8,128)(2,1)S(1)}, u32[]{:S(2)}, u32[]{:S(2)}) collective-permute-start(bf16[64,768]{1,0:T(8,128)(2,1)} %get-tuple-element.45), channel_id=1, source_target_pairs={{0,16},{8,24},{16,0},{24,8},{1,17},{9,25},{17,1},{25,9},{2,18},{10... | collective-permute-start | bytes 294920 | tf_op jit(solution)/shard_map/ppermute | solution.py:744
  9.3 4.8 %copy-start.6 = (bf16[16,768]{1,0:T(8,128)(2,1)S(1)}, bf16[16,768]{1,0:T(8,128)(2,1)}, u32[]{:S(2)}) copy-start(bf16[16,768]{1,0:T(8,128)(2,1)} %get-tuple-element.40.rest_5_.fr_ref) | copy-start | bytes 73732
  15.7 8.0 %collective-permute-start.5 = (bf16[16,768]{1,0:T(8,128)(2,1)S(1)}, bf16[16,768]{1,0:T(8,128)(2,1)S(1)}, u32[]{:S(2)}, u32[]{:S(2)}) collective-permute-start(bf16[16,768]{1,0:T(8,128)(2,1)S(1)} %get-tuple-element.48), channel_id=1, source_target_pairs={{0,6},{1,7},{2,4},{3,5},{4,2},{5,3},{6,0},{7,1},{8,14},{9,15},{10,... | collective-permute-start | bytes 73736 | tf_op jit(solution)/shard_map/ppermute | solution.py:744
  19.5 4.7 %collective-permute-start.4 = (bf16[16,768]{1,0:T(8,128)(2,1)S(1)}, bf16[16,768]{1,0:T(8,128)(2,1)S(1)}, u32[]{:S(2)}, u32[]{:S(2)}) collective-permute-start(bf16[16,768]{1,0:T(8,128)(2,1)S(1)} %get-tuple-element.48), channel_id=1, source_target_pairs={{0,4},{1,5},{2,6},{3,7},{4,0},{5,1},{6,2},{7,3},{8,12},{9,13},{10,... | collective-permute-start | bytes 73736 | tf_op jit(solution)/shard_map/ppermute | solution.py:744
  19.5 4.7 %collective-permute-start.3 = (bf16[16,768]{1,0:T(8,128)(2,1)S(1)}, bf16[16,768]{1,0:T(8,128)(2,1)S(1)}, u32[]{:S(2)}, u32[]{:S(2)}) collective-permute-start(bf16[16,768]{1,0:T(8,128)(2,1)S(1)} %get-tuple-element.48), channel_id=1, source_target_pairs={{0,2},{1,3},{2,0},{3,1},{4,6},{5,7},{6,4},{7,5},{8,10},{9,11},{10,... | collective-permute-start | bytes 73736 | tf_op jit(solution)/shard_map/ppermute | solution.py:744
  24.3 7.1 %collective-permute-start.8 = (bf16[64,768]{1,0:T(8,128)(2,1)S(1)}, bf16[64,768]{1,0:T(8,128)(2,1)S(1)}, u32[]{:S(2)}, u32[]{:S(2)}) collective-permute-start(bf16[64,768]{1,0:T(8,128)(2,1)S(1)} %get-tuple-element.84), channel_id=1, source_target_pairs={{0,24},{8,16},{16,8},{24,0},{1,25},{9,17},{17,9},{25,1},{2,26},{10... | collective-permute-start | bytes 294920 | tf_op jit(solution)/shard_map/ppermute | solution.py:744
  26.5 5.0 %collective-permute-start.7 = (bf16[64,768]{1,0:T(8,128)(2,1)S(1)}, bf16[64,768]{1,0:T(8,128)(2,1)S(1)}, u32[]{:S(2)}, u32[]{:S(2)}) collective-permute-start(bf16[64,768]{1,0:T(8,128)(2,1)S(1)} %get-tuple-element.84), channel_id=1, source_target_pairs={{0,16},{8,24},{16,0},{24,8},{1,17},{9,25},{17,1},{25,9},{2,18},{10... | collective-permute-start | bytes 294920 | tf_op jit(solution)/shard_map/ppermute | solution.py:744
  27.3 4.6 %collective-permute-start.6 = (bf16[64,768]{1,0:T(8,128)(2,1)S(1)}, bf16[64,768]{1,0:T(8,128)(2,1)S(1)}, u32[]{:S(2)}, u32[]{:S(2)}) collective-permute-start(bf16[64,768]{1,0:T(8,128)(2,1)S(1)} %get-tuple-element.84), channel_id=1, source_target_pairs={{0,8},{8,0},{16,24},{24,16},{1,9},{9,1},{17,25},{25,17},{2,10},{10... | collective-permute-start | bytes 294920 | tf_op jit(solution)/shard_map/ppermute | solution.py:744
  32.0 2.0 %collective-permute-start.9 = (bf16[256,768]{1,0:T(8,128)(2,1)S(1)}, bf16[256,768]{1,0:T(8,128)(2,1)S(1)}, u32[]{:S(2)}, u32[]{:S(2)}) collective-permute-start(bf16[256,768]{1,0:T(8,128)(2,1)S(1)} %get-tuple-element.76.fa_ref), channel_id=1, source_target_pairs={{0,1},{1,0},{2,3},{3,2},{4,5},{5,4},{6,7},{7,6},{8,9},{9,8},{10,11... | collective-permute-start | bytes 1179656 | tf_op jit(solution)/shard_map/ppermute | solution.py:744

commit v7 on v6

--- a/solution.py
+++ b/solution.py
@@ -406,7 +406,6 @@
         if c == 0 and h == 0:
             kept["k", p] = (nt(eye, k_ref[:, cols]) * SCALE).astype(BF)
             kept["q", p] = q_ref[:, cols] * jnp.asarray(SCALE, BF)
-            kept["st", p] = pair_statistics(p, st_ref, aux_ref, fr_ref)
         s = nt(k_ref[rows, cols] * in_head[h], kept["q", p][c * strip :])
         dp = nt(v_ref[rows, cols] * in_head[h], g_ref[c * strip :, cols])
         kept["s", p, c, h] = s, dp
@@ -437,6 +436,8 @@
             both = jnp.concatenate([kept.pop(("dq", p, c, 0)), kept.pop(("dq", p, c, 1))], axis=0)
             dq_ref[rows, cols] = both.T.astype(BF)
 
+    for p in span:
+        kept["st", p] = pair_statistics(p, st_ref, aux_ref, fr_ref)
     units = [(p, c, h) for p in span for c in range(strips) for h in range(2)]
     staged(units, (score, soften, mix), skew)
 
@@ -480,7 +481,7 @@
     return both[:, :1], both[:, 128:129]
 
 
-def near_group(peers, group, fr_ref, packed, kv_ref, qg_ref, got, dq_ref, dk_ref, dv_ref):
+def near_group(peers, group, fr_ref, packed, kv_ref, qg_ref, got, dq_ref, dk_ref, dv_ref, keep_ref):
     cols = group_columns(group)
     n = dq_ref.shape[0]
     f = n * R2 // R3
@@ -513,6 +514,9 @@
     yield
     dk_ref[:, cols] = collapse(nn(ds2, queries)).astype(BF)
     dv_ref[:, cols] = collapse(nn(p.astype(BF), grads)).astype(BF)
+    yield
+    near, far = token_masks(near_ref, far_ref, group, n * R2)
+    keep_ref[:, cols] = onehot(jnp.logical_not(near | far))
 
 
 def near_kernel(peers, stride, fr_ref, fa_ref, kv_ref, qg_ref, *rest):
@@ -548,7 +552,7 @@
 
 
 def final_group(
-    peers, stride, digits, group, fr_ref, got, fa_ref, k_ref, v_ref, base, near_out, near_grads, outs, done
+    peers, stride, digits, group, fr_ref, got, fa_ref, k_ref, v_ref, base, near_out, near_grads, sel, outs, done
 ):
     kv_ref, qg_ref, got = got[0], got[1], unturned(got[2:])
     cols = group_columns(group)
@@ -562,9 +566,6 @@
     seq = lax.axis_index("col") * lax.axis_size("row") + row_here
     scale = jnp.asarray(SCALE, BF)
 
-    r, c = iota((5 * F, 1), 0), iota((1, blocks * FM), 1)
-    i, at = div(r, F), mod(r, F)
-    sel = onehot(c == div(at, f) * FM + i * f + mod(at, f))
     fa = nn(sel, fa_ref[:, cols])
     yield
     fa = fa.astype(BF)
@@ -643,8 +644,7 @@
     alone = jnp.where(also_far, 0.0, near_out[:, cols].astype(F32)).astype(BF)
     placed = nn(place, jnp.concatenate([expand(alone), far_out.astype(BF)], axis=0))
     yield
-    near, far = token_masks(near_ref, far_ref, group, length)
-    outs[0][:, cols] = jnp.where(near | far, placed, base[0][:, cols].astype(F32)).astype(BF)
+    outs[0][:, cols] = ((base[0][:, cols] * near_grads[3][:, cols]).astype(F32) + placed).astype(BF)
     done(0, cols)
     yield
     koff, knear = row_offsets(n, far_ref, group), row_offsets(n, near_ref, group)
@@ -677,7 +677,7 @@
 
 def final_kernel(peers, stride, digits, fr_ref, *refs):
     near_end = 2 + peers
-    count = near_end + 2 + 8
+    count = near_end + 2 + 9
     held, results = refs[:count], refs[count : count + 4]
     outs, out_sems = refs[count + 4 : count + 8], refs[-1]
 
@@ -692,10 +692,16 @@
 
     near, local, base = held[1:near_end], held[near_end : near_end + 2], held[near_end + 2 :]
     groups = results[0].shape[1] // GW
+    length = results[0].shape[0]
+    f, rows = length // R3, held[0].shape[0]
+    F = rows // FM * f
+    r, c = iota((5 * F, 1), 0), iota((1, rows), 1)
+    i, at = div(r, F), mod(r, F)
+    sel = onehot(c == div(at, f) * FM + i * f + mod(at, f))
     lockstep(
         final_group(
             peers, stride, digits, group, fr_ref, near, held[0], *local,
-            base[:4], base[4], base[5:], outs, done,
+            base[:4], base[4], base[5:], sel, outs, done,
         )
         for group in range(groups)
     )
@@ -814,8 +820,8 @@
         return pl.pallas_call(
             functools.partial(near_kernel, peers, stride),
             in_specs=[vmem_spec] * (peers + 3),
-            out_specs=[vmem_spec] * 3,
-            out_shape=[like(n)] * 3,
+            out_specs=[vmem_spec] * 4,
+            out_shape=[like(n)] * 3 + [like(length)],
             compiler_params=params(),
             cost_estimate=pl.CostEstimate(flops=ops, bytes_accessed=2 * length * width, transcendentals=0),
             name="near",

time: 39.3 us -> 39 us (level)
  waiting for transfers between devices: 2.82 us -> 2.27 us
  Pallas kernels: 22.4 us -> 22.8 us
    pallas_call x1, Pallas kernels: 1.1 us -> 1.65 us  [near_pass(): pl.pallas_call(functools.partial(near_kernel, peers, stride), in_specs=[v...]
    ppermute x10, waiting for transfers between devices: 2.82 us -> 2.27 us  [swap(): return lax.ppermute(x, axis, [(i, i ^ mask) for i in range(size)])]
  transfers between devices with their start and end apart: 10 -> 10, of which waited for: 5 -> 4; matrix products, arithmetic and copies ran while one was open for 0% -> 0% of each run, Pallas kernels for 30% -> 32%
where the time goes in v7:
time: 39 us; the launch traced here: 38.9 us
  Pallas kernels  22.8 us (58%)
  starting transfers between devices  12.7 us (33%)
  waiting for transfers between devices  2.27 us (6%)
  between operations  0.97 us (2%)
    ppermute x10, starting transfers between devices, swap(): return lax.ppermute(x, axis, [(i, i ^ mask) for i in range(size)])  12.7 us
    pallas_call x2, Pallas kernels, backward(): pl.pallas_call(functools.partial(backward_kernel, 256, 1, range(piece * p...  7.09 us
    pallas_call x1, Pallas kernels, shards(): pl.pallas_call(functools.partial(final_kernel, peers, stride, digits), in...  4.88 us
    pallas_call x1, Pallas kernels, shards(): pl.pallas_call(functools.partial(pick_kernel, peers), grid=(groups,), in_...  4.06 us
    pallas_call x1, Pallas kernels, shards(): pl.pallas_call(functools.partial(forward_kernel, 256, 2), in_specs=[vmem_...  3.58 us
    ppermute x10, waiting for transfers between devices, swap(): return lax.ppermute(x, axis, [(i, i ^ mask) for i in range(size)])  2.27 us
    pallas_call x1, Pallas kernels, near_pass(): pl.pallas_call(functools.partial(near_kernel, peers, stride), in_specs=[v...  1.65 us
    pallas_call x1, Pallas kernels, shards(): pl.pallas_call(functools.partial(merge_kernel, peers), in_specs=[vmem_spe...  1.59 us
  transfers between devices with their start and end apart: 10, of which 4 were waited for; matrix products, arithmetic and copies ran while one was open for 0% of the time, Pallas kernels for 32%

profile of v7, /device:TPU:0, one launch (start us, length us, event | category | flops | bytes accessed | tf_op | source)
XLA Modules:
  0.0 38.9 jit_solution(735809913075621344)
XLA Ops:
  0.7 4.1 %pick.1 = (bf16[64,768]{1,0:T(8,128)(2,1)}, bf16[64,768]{1,0:T(8,128)(2,1)}, bf16[16,768]{1,0:T(8,128)(2,1)}, bf16[64,768]{1,0:T(8,128)(2,1)}, bf16[64,768]{1,0:T(8,128)(2,1)}, /*index=5*/bf16[64,768]{1,0:T(8,128)(2,1)}) custom-call(s32[12]{0:T(128)} %near_ref.1, s32[12]{0:T(128)} %far_ref.1, bf16[512,768]{1,0:T(8,128)(2,1)} %q_ref.7, ...), custom_call_target="tpu_custom_call" | custom-call | tf_op jit(solution)/shard_map/pick/pallas_call | solution.py:752
  4.7 4.0 %collective-permute-start = (bf16[64,768]{1,0:T(8,128)(2,1)}, bf16[64,768]{1,0:T(8,128)(2,1)S(1)}, u32[]{:S(2)}, u32[]{:S(2)}) collective-permute-start(bf16[64,768]{1,0:T(8,128)(2,1)} %get-tuple-element.45), channel_id=1, source_target_pairs={{0,24},{8,16},{16,8},{24,0},{1,25},{9,17},{17,9},{25,1},{2,26},{10... | collective-permute-start | bytes 294920 | tf_op jit(solution)/shard_map/ppermute | solution.py:750
  8.7 0.5 %collective-permute-start.1 = (bf16[64,768]{1,0:T(8,128)(2,1)}, bf16[64,768]{1,0:T(8,128)(2,1)S(1)}, u32[]{:S(2)}, u32[]{:S(2)}) collective-permute-start(bf16[64,768]{1,0:T(8,128)(2,1)} %get-tuple-element.46), channel_id=1, source_target_pairs={{0,8},{8,0},{16,24},{24,16},{1,9},{9,1},{17,25},{25,17},{2,10},{10... | collective-permute-start | bytes 294920 | tf_op jit(solution)/shard_map/ppermute | solution.py:750
  9.2 0.1 collective-permute-start.2
  9.4 3.6 %forward.1 = (bf16[512,768]{1,0:T(8,128)(2,1)S(1)}, f32[48,512]{1,0:T(8,128)S(1)}) custom-call(bf16[512,768]{1,0:T(8,128)(2,1)S(1)} %copy-done.2, bf16[512,768]{1,0:T(8,128)(2,1)S(1)} %copy-done, bf16[512,768]{1,0:T(8,128)(2,1)S(1)} %copy-done.1, bf16[512,768]{1,0:T(8,128)(2,1)S(1)} %copy-done.3), custom_call_target="tpu_custom_call" | custom-call | flops 3221225472 | bytes 4718592 | tf_op jit(solution)/shard_map/forward/pallas_call | solution.py:776
  12.9 0.0 collective-permute-done.rest_0_.refs_3_
  12.9 1.2 %collective-permute-done.1.rest_1_.refs_4_ = bf16[64,768]{1,0:T(8,128)(2,1)S(1)} collective-permute-done((bf16[64,768]{1,0:T(8,128)(2,1)}, bf16[64,768]{1,0:T(8,128)(2,1)S(1)}, u32[]{:S(2)}, u32[]{:S(2)}) %collective-permute-start.1) | collective-permute-done | bytes 98336 | tf_op jit(solution)/shard_map/ppermute | solution.py:750
  14.1 0.0 collective-permute-done.2.rest_2_.refs_5_
  14.1 1.6 %merge.1 = (bf16[16,768]{1,0:T(8,128)(2,1)S(1)}, bf16[32,768]{1,0:T(8,128)(2,1)S(1)}, bf16[32,768]{1,0:T(8,128)(2,1)S(1)}) custom-call(bf16[64,768]{1,0:T(8,128)(2,1)S(1)} %copy-done.4, bf16[64,768]{1,0:T(8,128)(2,1)S(1)} %copy-done.5, bf16[64,768]{1,0:T(8,128)(2,1)S(1)} %collective-permute-done.rest_0_.refs_3_, ...), custom_call_target="tpu_custom_call" | custom-call | tf_op jit(solution)/shard_map/merge/pallas_call | solution.py:786
  15.7 3.8 %collective-permute-start.5 = (bf16[16,768]{1,0:T(8,128)(2,1)S(1)}, bf16[16,768]{1,0:T(8,128)(2,1)S(1)}, u32[]{:S(2)}, u32[]{:S(2)}) collective-permute-start(bf16[16,768]{1,0:T(8,128)(2,1)S(1)} %get-tuple-element.50), channel_id=1, source_target_pairs={{0,6},{1,7},{2,4},{3,5},{4,2},{5,3},{6,0},{7,1},{8,14},{9,15},{10,... | collective-permute-start | bytes 73736 | tf_op jit(solution)/shard_map/ppermute | solution.py:750
  19.5 0.0 collective-permute-start.4
  19.5 0.7 %collective-permute-start.3 = (bf16[16,768]{1,0:T(8,128)(2,1)S(1)}, bf16[16,768]{1,0:T(8,128)(2,1)S(1)}, u32[]{:S(2)}, u32[]{:S(2)}) collective-permute-start(bf16[16,768]{1,0:T(8,128)(2,1)S(1)} %get-tuple-element.50), channel_id=1, source_target_pairs={{0,2},{1,3},{2,0},{3,1},{4,6},{5,7},{6,4},{7,5},{8,10},{9,11},{10,... | collective-permute-start | bytes 73736 | tf_op jit(solution)/shard_map/ppermute | solution.py:750
  20.2 3.5 %backward.2 = (bf16[512,768]{1,0:T(8,128)(2,1)S(1)}, bf16[512,768]{1,0:T(8,128)(2,1)S(1)}, bf16[512,768]{1,0:T(8,128)(2,1)S(1)}) custom-call(bf16[512,768]{1,0:T(8,128)(2,1)S(1)} %copy-done.2, bf16[512,768]{1,0:T(8,128)(2,1)S(1)} %copy-done, bf16[512,768]{1,0:T(8,128)(2,1)S(1)} %copy-done.1, bf16[512,768]{1,0:T(8,128)(2,1)S(1)} %copy-done.3, ...), custom_call_target="tpu_custom_call" | custom-call | flops 4026531840 | bytes 3145728 | tf_op jit(solution)/shard_map/backward/pallas_call | solution.py:801
  23.8 0.5 %collective-permute-done.4 = bf16[16,768]{1,0:T(8,128)(2,1)S(1)} collective-permute-done((bf16[16,768]{1,0:T(8,128)(2,1)S(1)}, bf16[16,768]{1,0:T(8,128)(2,1)S(1)}, u32[]{:S(2)}, u32[]{:S(2)}) %collective-permute-start.4) | collective-permute-done | bytes 24608 | tf_op jit(solution)/shard_map/ppermute | solution.py:750
  24.3 2.3 %collective-permute-start.8 = (bf16[64,768]{1,0:T(8,128)(2,1)S(1)}, bf16[64,768]{1,0:T(8,128)(2,1)S(1)}, u32[]{:S(2)}, u32[]{:S(2)}) collective-permute-start(bf16[64,768]{1,0:T(8,128)(2,1)S(1)} %get-tuple-element.88), channel_id=1, source_target_pairs={{0,24},{8,16},{16,8},{24,0},{1,25},{9,17},{17,9},{25,1},{2,26},{10... | collective-permute-start | bytes 294920 | tf_op jit(solution)/shard_map/ppermute | solution.py:750
  26.5 0.8 %collective-permute-start.7 = (bf16[64,768]{1,0:T(8,128)(2,1)S(1)}, bf16[64,768]{1,0:T(8,128)(2,1)S(1)}, u32[]{:S(2)}, u32[]{:S(2)}) collective-permute-start(bf16[64,768]{1,0:T(8,128)(2,1)S(1)} %get-tuple-element.88), channel_id=1, source_target_pairs={{0,16},{8,24},{16,0},{24,8},{1,17},{9,25},{17,1},{25,9},{2,18},{10... | collective-permute-start | bytes 294920 | tf_op jit(solution)/shard_map/ppermute | solution.py:750
  27.3 0.5 %collective-permute-start.6 = (bf16[64,768]{1,0:T(8,128)(2,1)S(1)}, bf16[64,768]{1,0:T(8,128)(2,1)S(1)}, u32[]{:S(2)}, u32[]{:S(2)}) collective-permute-start(bf16[64,768]{1,0:T(8,128)(2,1)S(1)} %get-tuple-element.88), channel_id=1, source_target_pairs={{0,8},{8,0},{16,24},{24,16},{1,9},{9,1},{17,25},{25,17},{2,10},{10... | collective-permute-start | bytes 294920 | tf_op jit(solution)/shard_map/ppermute | solution.py:750
  27.8 3.5 %backward.3 = (bf16[512,768]{1,0:T(8,128)(2,1)S(1)}, bf16[512,768]{1,0:T(8,128)(2,1)S(1)}, bf16[512,768]{1,0:T(8,128)(2,1)S(1)}) custom-call(bf16[512,768]{1,0:T(8,128)(2,1)S(1)} %copy-done.2, bf16[512,768]{1,0:T(8,128)(2,1)S(1)} %copy-done, bf16[512,768]{1,0:T(8,128)(2,1)S(1)} %copy-done.1, ...), custom_call_target="tpu_custom_call", output_to_operand_aliasing={{0}: (7, {}), {1}: (8, {}), {2}: (9, {})} | custom-call | flops 4026531840 | bytes 3145728 | tf_op jit(solution)/shard_map/backward/pallas_call | solution.py:801
  31.4 0.1 collective-permute-done.7
  31.5 0.4 %collective-permute-done.6 = bf16[64,768]{1,0:T(8,128)(2,1)S(1)} collective-permute-done((bf16[64,768]{1,0:T(8,128)(2,1)S(1)}, bf16[64,768]{1,0:T(8,128)(2,1)S(1)}, u32[]{:S(2)}, u32[]{:S(2)}) %collective-permute-start.6) | collective-permute-done | bytes 98336 | tf_op jit(solution)/shard_map/ppermute | solution.py:750
  32.0 0.1 collective-permute-start.9
  32.1 1.7 %near.1 = (bf16[32,768]{1,0:T(8,128)(2,1)S(1)}, bf16[32,768]{1,0:T(8,128)(2,1)S(1)}, bf16[32,768]{1,0:T(8,128)(2,1)S(1)}, bf16[512,768]{1,0:T(8,128)(2,1)S(1)}) custom-call(bf16[16,768]{1,0:T(8,128)(2,1)S(1)} %copy-done.6, bf16[256,768]{1,0:T(8,128)(2,1)S(1)} %get-tuple-element.80.fa_ref, bf16[64,768]{1,0:T(8,128)(2,1)S(1)} %copy-done.4, ...), custom_call_target="tpu_custom_call" | custom-call | flops 402653184 | bytes 786432 | tf_op jit(solution)/shard_map/near/pallas_call | solution.py:820
  33.8 0.0 collective-permute-done.9
  33.8 4.9 %final.1 = (bf16[512,768]{1,0:T(8,128)(2,1)}, bf16[512,768]{1,0:T(8,128)(2,1)}, bf16[512,768]{1,0:T(8,128)(2,1)}, bf16[512,768]{1,0:T(8,128)(2,1)}) custom-call(bf16[16,768]{1,0:T(8,128)(2,1)S(1)} %copy-done.6, bf16[512,768]{1,0:T(8,128)(2,1)S(1)} %constant_dynamic-update-slice_fusion.11.refs_0_, bf16[64,768]{1,0:T(8,128)(2,1)S(1)} %copy-done.4, ...), custom_call_target="tpu_custom_call" | custom-call | tf_op jit(solution)/shard_map/final/pallas_call | solution.py:860
  (25 shorter events, 0.1 us)
Async XLA Ops:
  0.6 8.7 %copy-start.1 = (bf16[512,768]{1,0:T(8,128)(2,1)S(1)}, bf16[512,768]{1,0:T(8,128)(2,1)}, u32[]{:S(2)}) copy-start(bf16[512,768]{1,0:T(8,128)(2,1)} %refs_7_.1) | copy-start | bytes 2359300
  0.6 8.7 %copy-start = (bf16[512,768]{1,0:T(8,128)(2,1)S(1)}, bf16[512,768]{1,0:T(8,128)(2,1)}, u32[]{:S(2)}) copy-start(bf16[512,768]{1,0:T(8,128)(2,1)} %refs_6_.1) | copy-start | bytes 2359300
  0.7 8.7 %copy-start.3 = (bf16[512,768]{1,0:T(8,128)(2,1)S(1)}, bf16[512,768]{1,0:T(8,128)(2,1)}, u32[]{:S(2)}) copy-start(bf16[512,768]{1,0:T(8,128)(2,1)} %g_ref.7) | copy-start | bytes 2359300
  0.7 8.7 %copy-start.2 = (bf16[512,768]{1,0:T(8,128)(2,1)S(1)}, bf16[512,768]{1,0:T(8,128)(2,1)}, u32[]{:S(2)}) copy-start(bf16[512,768]{1,0:T(8,128)(2,1)} %q_ref.7) | copy-start | bytes 2359300
  4.7 8.2 %collective-permute-start = (bf16[64,768]{1,0:T(8,128)(2,1)}, bf16[64,768]{1,0:T(8,128)(2,1)S(1)}, u32[]{:S(2)}, u32[]{:S(2)}) collective-permute-start(bf16[64,768]{1,0:T(8,128)(2,1)} %get-tuple-element.45), channel_id=1, source_target_pairs={{0,24},{8,16},{16,8},{24,0},{1,25},{9,17},{17,9},{25,1},{2,26},{10... | collective-permute-start | bytes 294920 | tf_op jit(solution)/shard_map/ppermute | solution.py:750
  8.7 5.4 %collective-permute-start.1 = (bf16[64,768]{1,0:T(8,128)(2,1)}, bf16[64,768]{1,0:T(8,128)(2,1)S(1)}, u32[]{:S(2)}, u32[]{:S(2)}) collective-permute-start(bf16[64,768]{1,0:T(8,128)(2,1)} %get-tuple-element.46), channel_id=1, source_target_pairs={{0,8},{8,0},{16,24},{24,16},{1,9},{9,1},{17,25},{25,17},{2,10},{10... | collective-permute-start | bytes 294920 | tf_op jit(solution)/shard_map/ppermute | solution.py:750
  9.2 4.9 %copy-start.4 = (bf16[64,768]{1,0:T(8,128)(2,1)S(1)}, bf16[64,768]{1,0:T(8,128)(2,1)}, u32[]{:S(2)}) copy-start(bf16[64,768]{1,0:T(8,128)(2,1)} %get-tuple-element.43.kv_ref.refs_1_) | copy-start | bytes 294916
  9.2 4.9 %copy-start.5 = (bf16[64,768]{1,0:T(8,128)(2,1)S(1)}, bf16[64,768]{1,0:T(8,128)(2,1)}, u32[]{:S(2)}) copy-start(bf16[64,768]{1,0:T(8,128)(2,1)} %get-tuple-element.44.qg_ref.refs_2_) | copy-start | bytes 294916
  9.2 4.9 %collective-permute-start.2 = (bf16[64,768]{1,0:T(8,128)(2,1)}, bf16[64,768]{1,0:T(8,128)(2,1)S(1)}, u32[]{:S(2)}, u32[]{:S(2)}) collective-permute-start(bf16[64,768]{1,0:T(8,128)(2,1)} %get-tuple-element.47), channel_id=1, source_target_pairs={{0,16},{8,24},{16,0},{24,8},{1,17},{9,25},{17,1},{25,9},{2,18},{10... | collective-permute-start | bytes 294920 | tf_op jit(solution)/shard_map/ppermute | solution.py:750
  9.3 4.8 %copy-start.6 = (bf16[16,768]{1,0:T(8,128)(2,1)S(1)}, bf16[16,768]{1,0:T(8,128)(2,1)}, u32[]{:S(2)}) copy-start(bf16[16,768]{1,0:T(8,128)(2,1)} %get-tuple-element.42.rest_5_.fr_ref) | copy-start | bytes 73732
  15.7 8.0 %collective-permute-start.5 = (bf16[16,768]{1,0:T(8,128)(2,1)S(1)}, bf16[16,768]{1,0:T(8,128)(2,1)S(1)}, u32[]{:S(2)}, u32[]{:S(2)}) collective-permute-start(bf16[16,768]{1,0:T(8,128)(2,1)S(1)} %get-tuple-element.50), channel_id=1, source_target_pairs={{0,6},{1,7},{2,4},{3,5},{4,2},{5,3},{6,0},{7,1},{8,14},{9,15},{10,... | collective-permute-start | bytes 73736 | tf_op jit(solution)/shard_map/ppermute | solution.py:750
  19.5 4.7 %collective-permute-start.4 = (bf16[16,768]{1,0:T(8,128)(2,1)S(1)}, bf16[16,768]{1,0:T(8,128)(2,1)S(1)}, u32[]{:S(2)}, u32[]{:S(2)}) collective-permute-start(bf16[16,768]{1,0:T(8,128)(2,1)S(1)} %get-tuple-element.50), channel_id=1, source_target_pairs={{0,4},{1,5},{2,6},{3,7},{4,0},{5,1},{6,2},{7,3},{8,12},{9,13},{10,... | collective-permute-start | bytes 73736 | tf_op jit(solution)/shard_map/ppermute | solution.py:750
  19.5 4.7 %collective-permute-start.3 = (bf16[16,768]{1,0:T(8,128)(2,1)S(1)}, bf16[16,768]{1,0:T(8,128)(2,1)S(1)}, u32[]{:S(2)}, u32[]{:S(2)}) collective-permute-start(bf16[16,768]{1,0:T(8,128)(2,1)S(1)} %get-tuple-element.50), channel_id=1, source_target_pairs={{0,2},{1,3},{2,0},{3,1},{4,6},{5,7},{6,4},{7,5},{8,10},{9,11},{10,... | collective-permute-start | bytes 73736 | tf_op jit(solution)/shard_map/ppermute | solution.py:750
  24.3 7.1 %collective-permute-start.8 = (bf16[64,768]{1,0:T(8,128)(2,1)S(1)}, bf16[64,768]{1,0:T(8,128)(2,1)S(1)}, u32[]{:S(2)}, u32[]{:S(2)}) collective-permute-start(bf16[64,768]{1,0:T(8,128)(2,1)S(1)} %get-tuple-element.88), channel_id=1, source_target_pairs={{0,24},{8,16},{16,8},{24,0},{1,25},{9,17},{17,9},{25,1},{2,26},{10... | collective-permute-start | bytes 294920 | tf_op jit(solution)/shard_map/ppermute | solution.py:750
  26.5 5.0 %collective-permute-start.7 = (bf16[64,768]{1,0:T(8,128)(2,1)S(1)}, bf16[64,768]{1,0:T(8,128)(2,1)S(1)}, u32[]{:S(2)}, u32[]{:S(2)}) collective-permute-start(bf16[64,768]{1,0:T(8,128)(2,1)S(1)} %get-tuple-element.88), channel_id=1, source_target_pairs={{0,16},{8,24},{16,0},{24,8},{1,17},{9,25},{17,1},{25,9},{2,18},{10... | collective-permute-start | bytes 294920 | tf_op jit(solution)/shard_map/ppermute | solution.py:750
  27.3 4.6 %collective-permute-start.6 = (bf16[64,768]{1,0:T(8,128)(2,1)S(1)}, bf16[64,768]{1,0:T(8,128)(2,1)S(1)}, u32[]{:S(2)}, u32[]{:S(2)}) collective-permute-start(bf16[64,768]{1,0:T(8,128)(2,1)S(1)} %get-tuple-element.88), channel_id=1, source_target_pairs={{0,8},{8,0},{16,24},{24,16},{1,9},{9,1},{17,25},{25,17},{2,10},{10... | collective-permute-start | bytes 294920 | tf_op jit(solution)/shard_map/ppermute | solution.py:750
  32.0 1.8 %collective-permute-start.9 = (bf16[256,768]{1,0:T(8,128)(2,1)S(1)}, bf16[256,768]{1,0:T(8,128)(2,1)S(1)}, u32[]{:S(2)}, u32[]{:S(2)}) collective-permute-start(bf16[256,768]{1,0:T(8,128)(2,1)S(1)} %get-tuple-element.80.fa_ref), channel_id=1, source_target_pairs={{0,1},{1,0},{2,3},{3,2},{4,5},{5,4},{6,7},{7,6},{8,9},{9,8},{10,11... | collective-permute-start | bytes 1179656 | tf_op jit(solution)/shard_map/ppermute | solution.py:750
